TPU v7x, 256 devices: a whole 4x4x8 slice. The times are simulated.
256 devices in a mesh: member: 4 (over y_lo, core), tile: 64 (over z, x, y_hi).
Axes of the slice: x: 4, y: 4 (y_hi: 2, y_lo: 2; y = y_hi * 2 + y_lo), z: 8, core: 2. Of those that a mesh axis runs over, the one named last changes fastest.
Arguments:
- initial: float32 [4, 8, 1024, 1024], P('member', None, 'tile'), may hold values from -6 to 6
- target: float32 [8, 1024, 1024], P(None, 'tile'), may hold values from -6 to 6
- noise: bfloat16 [2, 4, 8, 1024, 1024], P(None, 'member', None, 'tile'), may hold values from -6 to 6
- w_qkv: bfloat16 [1024, 3072], replicated, may hold values from -0.1875 to 0.1875
- w_out: bfloat16 [1024, 1024], replicated, may hold values from -0.1875 to 0.1875
- gain: float32 [1024], replicated, may hold values from 0.5 to 1.5
- noise_scale: float32 [1024], replicated, may hold values from 0.3 to 1
- shifts: int32 [2, 2], replicated, may hold values from 1 to 7
Outputs:
- state_grad: float32 [4, 8, 1024, 1024], P('member', None, 'tile')
- gain_grad: float32 [1024], replicated
- scale_grad: float32 [1024], replicated
Inputs may be any that keep to these rules, and one draw needn't show every extreme that they name: `shifts`: each step's offsets of the window grid, in cells.
All inputs are finite; a program needn't handle non-finite values.
Results may differ from a plain program's by a relative error of at most 0.025.
Values may be sent and summed in bfloat16 or wider, within the bound.
No kernel may reach another device: no remote copies, remote signals or barrier semaphores. Data moves between devices by JAX's collectives and lax.ppermute only.
A program may use at most 128 MiB of HBM per device.

v0:
```python
import functools

import jax
import jax.numpy as jnp
from jax import lax
from jax.experimental import pallas as pl
from jax.experimental.pallas import tpu as pltpu
from jax.sharding import PartitionSpec as P

C = 1024
HEAD = 32
WIN = 8
LAT = 8
TOK = LAT * WIN
GROUP = 4
LANES = GROUP * HEAD
GROUPS = C // LANES
SPAN = GROUP * TOK
SCALE = HEAD ** (-0.5)
SMOOTH = 0.25
F32 = jnp.float32
BF16 = jnp.bfloat16
VMEM_LIMIT = 40 * 1024 * 1024


def dot(left, right):
    return lax.dot_general(left, right, (((1,), (0,)), ((), ())), preferred_element_type=F32)


def dot_nt(left, right):
    return lax.dot_general(left, right, (((1,), (1,)), ((), ())), preferred_element_type=F32)


def dot_tn(left, right):
    return lax.dot_general(left, right, (((0,), (0,)), ((), ())), preferred_element_type=F32)


def head_masks():
    lane = lax.broadcasted_iota(jnp.int32, (TOK, LANES), 1) // HEAD
    return [lane == head for head in range(GROUP)]


def by_head(value, masks):
    zero = jnp.zeros_like(value)
    return jnp.concatenate([jnp.where(mask, value, zero) for mask in masks], axis=0)


def fold_heads(stacked, masks):
    out = stacked[:TOK]
    for head in range(1, GROUP):
        out = jnp.where(masks[head], stacked[head * TOK : (head + 1) * TOK], out)
    return out


def lat_mask(lat_shift):
    key_lat = lax.broadcasted_iota(jnp.int32, (TOK, SPAN), 0) // WIN
    query_lat = (lax.broadcasted_iota(jnp.int32, (TOK, SPAN), 1) % TOK) // WIN
    return (key_lat < lat_shift) == (query_lat < lat_shift)


def lanes(start, size):
    return pl.ds(pl.multiple_of(start, 128), size)


def fill(ext, own_ref, west, east):
    for row in range(LAT):
        ext[row, 0:8, :] = west[row * WIN : (row + 1) * WIN]
        ext[row, 8:24, :] = own_ref[row].astype(F32)
        ext[row, 24:32, :] = east[row * WIN : (row + 1) * WIN]


def frame(ext, row, start, columns):
    return pltpu.roll(ext[row], lax.rem(32 - start, 32), 0)[:columns]


def norm_rows(x_ref, rows, gain, normed_ref, scaled_ref, spread_ref, saved_from):
    for at in range(0, rows, 32):
        x = x_ref[at : at + 32, :]
        centre = jnp.mean(x, axis=-1, keepdims=True)
        offset = x - centre
        spread = lax.rsqrt(jnp.mean(offset * offset, axis=-1, keepdims=True) + 1e-05)
        scaled = offset * spread
        normed_ref[at : at + 32, :] = (scaled * gain).astype(BF16)
        if at >= saved_from:
            scaled_ref[at - saved_from : at - saved_from + 32, :] = scaled
            spread_ref[at - saved_from : at - saved_from + 32, :] = jnp.broadcast_to(
                spread, (32, 128)
            )


def attend(windows, packed_ref, weights_ref, mixed_ref, lat_shift, saved_from):
    masks = head_masks()
    allowed = lat_mask(lat_shift)

    def group(at, _):
        for window in range(windows):
            rows = slice(window * TOK, (window + 1) * TOK)
            queries = packed_ref[rows, lanes(at * LANES, LANES)]
            keys = packed_ref[rows, lanes(C + at * LANES, LANES)]
            values = packed_ref[rows, lanes(2 * C + at * LANES, LANES)]
            scores = dot_nt(keys, by_head(queries, masks))
            scores = jnp.where(allowed, scores, -1e9 / SCALE)
            highest = jnp.max(scores, axis=0, keepdims=True)
            raised = jnp.exp((scores - highest) * SCALE)
            total = jnp.sum(raised, axis=0, keepdims=True)
            weights = (raised * (1.0 / total)).astype(BF16)
            if window >= saved_from:
                weights_ref[(window - saved_from) * GROUPS + at] = weights
            mixed = fold_heads(dot_tn(weights, values), masks)
            mixed_ref[rows, lanes(at * LANES, LANES)] = mixed.astype(BF16)
        return 0

    lax.fori_loop(0, GROUPS, group, 0)


def forward_kernel(
    shifts,
    initial,
    target,
    noise,
    east,
    west,
    gain,
    noise_scale,
    w_qkv_hbm,
    w_out_hbm,
    final_out,
    sent_out,
    target_out,
    noise_out,
    packed0_out,
    weights0_out,
    scaled0_out,
    spread0_out,
    packed1_out,
    weights1_out,
    scaled1_out,
    spread1_out,
    w_qkv,
    w_out,
    ext,
    state,
    normed,
    packed,
    mixed,
    sems,
):
    copies = []
    for part in range(6):
        at = pl.ds(part * 512, 512)
        copies.append(
            pltpu.make_async_copy(w_qkv_hbm.at[:, at], w_qkv.at[:, at], sems.at[part])
        )
    copies.append(pltpu.make_async_copy(w_out_hbm, w_out, sems.at[6]))
    for copy in copies:
        copy.start()
    lat0, lon0, lat1, lon1 = shifts[0, 0], shifts[0, 1], shifts[1, 0], shifts[1, 1]
    origin1 = jnp.where(lon1 <= lon0, lon1, lon1 - WIN)

    fill(ext, initial, west[0].astype(F32), east[0].astype(F32))
    for row in range(LAT):
        part = frame(ext, row, lon0, 24)
        for window in range(3):
            state[window * TOK + row * WIN : window * TOK + (row + 1) * WIN, :] = part[
                window * WIN : (window + 1) * WIN
            ]
    norm_rows(state, 3 * TOK, gain[...], normed, scaled0_out, spread0_out, TOK)
    for part in range(6):
        copies[part].wait()
        packed[:, part * 512 : (part + 1) * 512] = dot(
            normed[...], w_qkv[:, part * 512 : (part + 1) * 512]
        ).astype(BF16)
    packed0_out[...] = packed[TOK:, :]
    attend(3, packed, weights0_out, mixed, lat0, 1)
    copies[6].wait()
    for part in range(4):
        at = slice(part * 256, (part + 1) * 256)
        branch = dot(mixed[...], w_out[:, at])
        for row in range(LAT):
            for window in range(3):
                rows = slice(window * TOK + row * WIN, window * TOK + (row + 1) * WIN)
                ext[row, window * WIN : (window + 1) * WIN, at] = state[rows, at] + branch[rows]

    scale = noise_scale[...]
    for row in range(LAT):
        part = frame(ext, row, origin1 - lon0 + WIN, 16)
        for window in range(2):
            rows = slice(window * TOK + row * WIN, window * TOK + (row + 1) * WIN)
            state[rows, :] = part[window * WIN : (window + 1) * WIN]
    for step in range(2):
        fill(ext, noise.at[step], west[1 + step].astype(F32), east[1 + step].astype(F32))
        for row in range(LAT):
            part = frame(ext, row, origin1 + WIN, 16)
            for window in range(2):
                rows = slice(window * TOK + row * WIN, window * TOK + (row + 1) * WIN)
                here = part[window * WIN : (window + 1) * WIN]
                if step == 0:
                    state[rows, :] = state[rows, :] + scale * here
                else:
                    final_out[rows, :] = scale * here
                noise_out[step, rows, :] = here
    norm_rows(state, 2 * TOK, gain[...], normed, scaled1_out, spread1_out, 0)
    for part in range(6):
        packed1_out[:, part * 512 : (part + 1) * 512] = dot(
            normed[: 2 * TOK, :], w_qkv[:, part * 512 : (part + 1) * 512]
        ).astype(BF16)
    attend(2, packed1_out, weights1_out, mixed, lat1, 0)
    for part in range(4):
        at = slice(part * 256, (part + 1) * 256)
        branch = dot(mixed[: 2 * TOK, :], w_out[:, at])
        final = state[: 2 * TOK, at] + branch + final_out[:, at]
        final_out[:, at] = final
        sent_out[:, at] = final.astype(BF16)
    fill(ext, target, west[3].astype(F32), east[3].astype(F32))
    for row in range(LAT):
        part = frame(ext, row, origin1 + WIN, 16)
        for window in range(2):
            rows = slice(window * TOK + row * WIN, window * TOK + (row + 1) * WIN)
            target_out[rows, :] = part[window * WIN : (window + 1) * WIN]


def vmem():
    return pl.BlockSpec(memory_space=pltpu.VMEM)


def smem():
    return pl.BlockSpec(memory_space=pltpu.SMEM)


def anywhere():
    return pl.BlockSpec(memory_space=pl.ANY)


def forward(shifts, initial, target, noise, east, west, gain, noise_scale, w_qkv, w_out):
    rows = 2 * TOK
    saved = [
        jax.ShapeDtypeStruct((rows, 3 * C), BF16),
        jax.ShapeDtypeStruct((2 * GROUPS, TOK, SPAN), BF16),
        jax.ShapeDtypeStruct((rows, C), F32),
        jax.ShapeDtypeStruct((rows, 128), F32),
    ]
    out_shape = [
        jax.ShapeDtypeStruct((rows, C), F32),
        jax.ShapeDtypeStruct((rows, C), BF16),
        jax.ShapeDtypeStruct((rows, C), F32),
        jax.ShapeDtypeStruct((2, rows, C), F32),
    ] + saved * 2
    return pl.pallas_call(
        forward_kernel,
        out_shape=out_shape,
        in_specs=[smem()] + [vmem()] * 7 + [anywhere()] * 2,
        out_specs=[vmem()] * len(out_shape),
        scratch_shapes=[
            pltpu.VMEM((C, 3 * C), BF16),
            pltpu.VMEM((C, C), BF16),
            pltpu.VMEM((LAT, 32, C), F32),
            pltpu.VMEM((3 * TOK, C), F32),
            pltpu.VMEM((3 * TOK, C), BF16),
            pltpu.VMEM((3 * TOK, 3 * C), BF16),
            pltpu.VMEM((3 * TOK, C), BF16),
            pltpu.SemaphoreType.DMA((7,)),
        ],
        compiler_params=pltpu.CompilerParams(vmem_limit_bytes=VMEM_LIMIT),
        name="forward",
    )(shifts, initial, target, noise, east, west, gain, noise_scale, w_qkv, w_out)


def attend_back(packed, weights_ref, d_mixed, d_packed):
    masks = head_masks()

    def group(at, _):
        for window in range(2):
            rows = slice(window * TOK, (window + 1) * TOK)
            here = lanes(at * LANES, LANES)
            queries = packed[rows, here]
            keys = packed[rows, lanes(C + at * LANES, LANES)]
            values = packed[rows, lanes(2 * C + at * LANES, LANES)]
            d_mixed_blocks = by_head(d_mixed[rows, here], masks)
            weights = weights_ref[window * GROUPS + at]
            d_weights = dot_nt(values, d_mixed_blocks)
            d_values = dot(weights, d_mixed_blocks)
            probs = weights.astype(F32)
            centred = d_weights - jnp.sum(d_weights * probs, axis=0, keepdims=True)
            d_scores = (probs * centred * SCALE).astype(BF16)
            d_keys = dot(d_scores, by_head(queries, masks))
            d_queries = fold_heads(dot_tn(d_scores, keys), masks)
            d_packed[rows, here] = d_queries.astype(BF16)
            d_packed[rows, lanes(C + at * LANES, LANES)] = d_keys.astype(BF16)
            d_packed[rows, lanes(2 * C + at * LANES, LANES)] = d_values.astype(BF16)
        return 0

    lax.fori_loop(0, GROUPS, group, 0)


def slope(difference):
    return difference * lax.rsqrt(difference * difference + SMOOTH * SMOOTH)


def start_weights(w_qkv_hbm, w_out_hbm, w_qkv, w_out, sems):
    copies = [pltpu.make_async_copy(w_out_hbm, w_out, sems.at[4])]
    for part in range(4):
        at = pl.ds(part * 256, 256)
        copies.append(pltpu.make_async_copy(w_qkv_hbm.at[at], w_qkv.at[at], sems.at[part]))
    for copy in copies:
        copy.start()
    return copies


def step_back(
    copies, d_next, packed, weights, scaled, spread, gain, w_qkv, w_out, d_mixed, d_packed, d_normed
):
    copies[0].wait()
    d_branch = d_next[...].astype(BF16)
    for part in range(4):
        at = slice(part * 256, (part + 1) * 256)
        d_mixed[:, at] = dot_nt(d_branch, w_out[at, :]).astype(BF16)
    attend_back(packed, weights, d_mixed, d_packed)
    for part in range(4):
        at = slice(part * 256, (part + 1) * 256)
        copies[1 + part].wait()
        d_normed[:, at] = dot_nt(d_packed[...], w_qkv[at, :])


def norm_back(at, d_next, scaled_ref, spread_ref, d_normed, gain):
    rows = slice(at, at + 32)
    scaled = scaled_ref[rows, :]
    d_here = d_normed[rows, :]
    d_hat = d_here * gain
    spread = spread_ref[rows, 0:1]
    d_fields = spread * (
        d_hat
        - jnp.mean(d_hat, axis=-1, keepdims=True)
        - scaled * jnp.mean(d_hat * scaled, axis=-1, keepdims=True)
    )
    return d_next[rows, :] + d_fields, eight_rows(d_here * scaled)


def eight_rows(value):
    out = value[0:8]
    for at in range(8, value.shape[0], 8):
        out = out + value[at : at + 8]
    return out


def backward1_kernel(
    final,
    near,
    far,
    far_near,
    target,
    noise,
    packed,
    weights,
    scaled,
    spread,
    gain,
    w_qkv_hbm,
    w_out_hbm,
    d_out,
    head_out,
    gain_out,
    scale_out,
    w_qkv,
    w_out,
    d_next,
    d_mixed,
    d_packed,
    d_normed,
    sems,
):
    copies = start_weights(w_qkv_hbm, w_out_hbm, w_qkv, w_out, sems)
    scale_total = jnp.zeros((8, C), F32)
    for at in range(0, 2 * TOK, 32):
        rows = slice(at, at + 32)
        here = final[rows, :]
        pairs = (
            slope(here - near[rows, :].astype(F32))
            + slope(here - far[rows, :].astype(F32))
            + slope(here - far_near[rows, :].astype(F32))
        )
        seed = slope(here - target[rows, :]) - pairs * (1.0 / 3.0)
        d_next[rows, :] = seed
        scale_total = scale_total + eight_rows(seed * noise[1, rows, :])
    step_back(
        copies, d_next, packed, weights, scaled, spread, gain, w_qkv, w_out, d_mixed, d_packed, d_normed
    )
    gain_total = jnp.zeros((8, C), F32)
    for at in range(0, 2 * TOK, 32):
        rows = slice(at, at + 32)
        d_here, gain_part = norm_back(at, d_next, scaled, spread, d_normed, gain[...])
        d_out[rows, :] = d_here
        if at < TOK:
            head_out[rows, :] = d_here.astype(BF16)
        gain_total = gain_total + gain_part
        scale_total = scale_total + eight_rows(d_here * noise[0, rows, :])
    gain_out[...] = gain_total
    scale_out[...] = scale_total


def backward0_kernel(
    shifts,
    d_in,
    d_east,
    packed,
    weights,
    scaled,
    spread,
    gain,
    gain_in,
    scale_in,
    w_qkv_hbm,
    w_out_hbm,
    own_out,
    tail_out,
    sums_out,
    w_qkv,
    w_out,
    ext,
    d_next,
    d_mixed,
    d_packed,
    d_normed,
    sems,
):
    copies = start_weights(w_qkv_hbm, w_out_hbm, w_qkv, w_out, sems)
    lon0, lon1 = shifts[0, 1], shifts[1, 1]
    origin1 = jnp.where(lon1 <= lon0, lon1, lon1 - WIN)
    east = d_east[...].astype(F32)
    for row in range(LAT):
        ext[row, 0:8, :] = d_in[row * WIN : (row + 1) * WIN, :]
        ext[row, 8:16, :] = d_in[TOK + row * WIN : TOK + (row + 1) * WIN, :]
        ext[row, 16:24, :] = east[row * WIN : (row + 1) * WIN]
    for row in range(LAT):
        part = frame(ext, row, lon0 - origin1, 16)
        for window in range(2):
            rows = slice(window * TOK + row * WIN, window * TOK + (row + 1) * WIN)
            d_next[rows, :] = part[window * WIN : (window + 1) * WIN]
    step_back(
        copies, d_next, packed, weights, scaled, spread, gain, w_qkv, w_out, d_mixed, d_packed, d_normed
    )
    gain_total = gain_in[...]
    for at in range(0, 2 * TOK, 32):
        d_here, gain_part = norm_back(at, d_next, scaled, spread, d_normed, gain[...])
        gain_total = gain_total + gain_part
        for piece in range(4):
            token = at + piece * WIN
            row, window = (token % TOK) // WIN, token // TOK
            ext[row, 8 + window * WIN : 16 + window * WIN, :] = d_here[
                piece * WIN : (piece + 1) * WIN
            ]
    sums_out[0:1, :] = jnp.sum(gain_total, axis=0, keepdims=True)
    sums_out[1:2, :] = jnp.sum(scale_in[...], axis=0, keepdims=True)
    tails = []
    for row in range(LAT):
        own_out[row] = frame(ext, row, WIN - lon0, 16)
        tails.append(frame(ext, row, 24 - lon0, WIN))
    tail_out[...] = jnp.concatenate(tails, axis=0).astype(BF16)


def backward_scratch():
    rows = 2 * TOK
    return [
        pltpu.VMEM((rows, C), F32),
        pltpu.VMEM((rows, C), BF16),
        pltpu.VMEM((rows, 3 * C), BF16),
        pltpu.VMEM((rows, C), F32),
        pltpu.SemaphoreType.DMA((5,)),
    ]


def backward1(final, others, target, noise, saved, gain, w_qkv, w_out):
    rows = 2 * TOK
    return pl.pallas_call(
        backward1_kernel,
        out_shape=[
            jax.ShapeDtypeStruct((rows, C), F32),
            jax.ShapeDtypeStruct((TOK, C), BF16),
            jax.ShapeDtypeStruct((8, C), F32),
            jax.ShapeDtypeStruct((8, C), F32),
        ],
        in_specs=[vmem()] * 11 + [anywhere()] * 2,
        out_specs=[vmem()] * 4,
        scratch_shapes=[pltpu.VMEM((C, 3 * C), BF16), pltpu.VMEM((C, C), BF16)]
        + backward_scratch(),
        compiler_params=pltpu.CompilerParams(vmem_limit_bytes=VMEM_LIMIT),
        name="backward1",
    )(final, *others, target, noise, *saved, gain, w_qkv, w_out)


def backward0(shifts, d_in, d_east, saved, gain, gain_in, scale_in, w_qkv, w_out):
    return pl.pallas_call(
        backward0_kernel,
        out_shape=[
            jax.ShapeDtypeStruct((LAT, 16, C), F32),
            jax.ShapeDtypeStruct((TOK, C), BF16),
            jax.ShapeDtypeStruct((2, C), F32),
        ],
        in_specs=[smem()] + [vmem()] * 9 + [anywhere()] * 2,
        out_specs=[vmem()] * 3,
        scratch_shapes=[
            pltpu.VMEM((C, 3 * C), BF16),
            pltpu.VMEM((C, C), BF16),
            pltpu.VMEM((LAT, 32, C), F32),
        ]
        + backward_scratch(),
        compiler_params=pltpu.CompilerParams(vmem_limit_bytes=VMEM_LIMIT),
        name="backward0",
    )(shifts, d_in, d_east, *saved, gain, gain_in, scale_in, w_qkv, w_out)


def along(value, axis, steps):
    count = lax.axis_size(axis)
    return lax.ppermute(value, axis, [(at, (at + steps) % count) for at in range(count)])


def swapped(value, axis, bit):
    count = lax.axis_size(axis)
    return lax.ppermute(value, axis, [(at, at ^ bit) for at in range(count)])


def total_over_devices(value):
    for axis in ("member", "tile"):
        bit = 1
        while bit < lax.axis_size(axis):
            value = value + swapped(value, axis, bit)
            bit *= 2
    return value


def local(initial, target, noise, w_qkv, w_out, gain, noise_scale, shifts):
    initial, noise = initial[0], noise[:, 0]

    def border(at):
        parts = [
            part[:, at].reshape(TOK, C).astype(BF16)
            for part in (initial, noise[0], noise[1], target)
        ]
        return jnp.stack(parts)

    east = along(border(slice(0, WIN)), "tile", -1)
    west = along(border(slice(WIN, 2 * WIN)), "tile", 1)
    gain_row, scale_row = gain[None], noise_scale[None]
    final, sent, target_here, noise_here, *saved = forward(
        shifts, initial, target, noise, east, west, gain_row, scale_row, w_qkv, w_out
    )
    far = swapped(sent, "member", 2)
    near = swapped(sent, "member", 1)
    far_near = swapped(far, "member", 1)
    d_one, head, gain_part, scale_part = backward1(
        final, (near, far, far_near), target_here, noise_here, saved[4:], gain_row, w_qkv, w_out
    )
    own, tail, sums = backward0(
        shifts,
        d_one,
        along(head, "tile", -1),
        saved[:4],
        gain_row,
        gain_part,
        scale_part,
        w_qkv,
        w_out,
    )
    arrived = along(tail, "tile", 1).reshape(LAT, WIN, C).astype(F32)
    column = jnp.arange(WIN)[None, :, None]
    first = jnp.where(column < shifts[0, 1], arrived, own[:, :WIN])
    state_grad = jnp.concatenate([first, own[:, WIN:]], axis=1)[None]
    sums = total_over_devices(sums)
    members = lax.axis_size("member")
    factor = (members * LAT * initial.shape[1] * lax.axis_size("tile")) ** (-0.5)
    return (state_grad, sums[0] * factor, sums[1] * factor)


def solution(mesh):
    in_specs = (
        P("member", None, "tile", None),
        P(None, "tile", None),
        P(None, "member", None, "tile", None),
        P(),
        P(),
        P(),
        P(),
        P(),
    )
    out_specs = (P("member", None, "tile", None), P(), P())
    return jax.shard_map(local, mesh=mesh, in_specs=in_specs, out_specs=out_specs, check_vma=False)
```

profile of v0, /device:TPU:32, one launch (start us, length us, event | category | flops | bytes accessed | tf_op | source)
XLA Modules:
  0.0 136.3 jit_solution(14427967343791884705)
XLA Ops:
  0.6 0.0 copy-start.3
  0.6 0.0 copy-start.1
  0.7 0.0 copy-start.2
  0.7 0.0 copy-start.4
  0.7 0.0 copy-start.5
  0.7 0.0 copy-start
  0.7 0.0 copy-start.6
  0.7 1.2 slice_bitcast_fusion.1
  1.9 1.1 bitcast_convert_fusion
  3.0 1.1 convert.10
  4.2 0.1 pad_maximum_fusion.1
  4.3 0.0 slice-start
  4.3 3.3 %collective-permute-start.1 = (bf16[4,64,1024]{2,1,0:T(8,128)(2,1)S(1)}, bf16[4,64,1024]{2,1,0:T(8,128)(2,1)S(1)}, u32[]{:S(2)}, u32[]{:S(2)}) collective-permute-start(bf16[4,64,1024]{2,1,0:T(8,128)(2,1)S(1)} %pad_maximum_fusion.1), channel_id=1, source_target_pairs={{0,1},{1,2},{2,3},{3,4},{4,5},{5,6},{6,7},{7,8},{8,9},{9,10},{10,1... | collective-permute-start | bytes 1572872 | tf_op jit(solution)/shard_map/ppermute | solution.py:513
  7.5 0.1 pad_maximum_fusion
  7.6 3.4 %collective-permute-start = (bf16[4,64,1024]{2,1,0:T(8,128)(2,1)S(1)}, bf16[4,64,1024]{2,1,0:T(8,128)(2,1)S(1)}, u32[]{:S(2)}, u32[]{:S(2)}) collective-permute-start(bf16[4,64,1024]{2,1,0:T(8,128)(2,1)S(1)} %pad_maximum_fusion), channel_id=1, source_target_pairs={{0,63},{1,0},{2,1},{3,2},{4,3},{5,4},{6,5},{7,6},{8,7},{9,8},{10,9... | collective-permute-start | bytes 1572872 | tf_op jit(solution)/shard_map/ppermute | solution.py:513
  11.0 18.9 %collective-permute-done.1.west = bf16[4,64,1024]{2,1,0:T(8,128)(2,1)S(1)} collective-permute-done((bf16[4,64,1024]{2,1,0:T(8,128)(2,1)S(1)}, bf16[4,64,1024]{2,1,0:T(8,128)(2,1)S(1)}, u32[]{:S(2)}, u32[]{:S(2)}) %collective-permute-start.1) | collective-permute-done | bytes 524320 | tf_op jit(solution)/shard_map/ppermute | solution.py:513
  30.0 3.8 %collective-permute-done.east = bf16[4,64,1024]{2,1,0:T(8,128)(2,1)S(1)} collective-permute-done((bf16[4,64,1024]{2,1,0:T(8,128)(2,1)S(1)}, bf16[4,64,1024]{2,1,0:T(8,128)(2,1)S(1)}, u32[]{:S(2)}, u32[]{:S(2)}) %collective-permute-start) | collective-permute-done | bytes 524320 | tf_op jit(solution)/shard_map/ppermute | solution.py:513
  33.8 0.0 copy-done.3
  33.8 0.0 copy-done.1
  33.8 0.0 copy-done.2
  33.8 0.0 copy-done.4
  33.8 0.0 copy-done.5
  33.8 0.0 copy-done
  33.8 0.0 copy-done.6
  33.8 0.0 slice-start.1
  33.8 18.0 %forward.1 = (f32[128,1024]{1,0:T(8,128)S(1)}, bf16[128,1024]{1,0:T(8,128)(2,1)S(1)}, f32[128,1024]{1,0:T(8,128)S(1)}, f32[2,128,1024]{2,1,0:T(8,128)S(1)}, bf16...) custom-call(s32[2,2]{1,0:T(2,128)S(1)} %copy-done.6, ...), custom_call_target="tpu_custom_call" | custom-call | tf_op jit(solution)/shard_map/forward/pallas_call | solution.py:248
  51.8 0.8 collective-permute-start.3
  52.6 0.0 collective-permute-start.2
  52.6 7.5 %collective-permute-done.3.far = bf16[128,1024]{1,0:T(8,128)(2,1)S(1)} collective-permute-done((bf16[128,1024]{1,0:T(8,128)(2,1)S(1)}, bf16[128,1024]{1,0:T(8,128)(2,1)S(1)}, u32[]{:S(2)}, u32[]{:S(2)}) %collective-permute-start.3) | collective-permute-done | bytes 262176 | tf_op jit(solution)/shard_map/ppermute | solution.py:518
  60.1 0.0 collective-permute-start.4
  60.1 0.0 collective-permute-done.2.near
  60.1 1.5 %collective-permute-done.4.far_near = bf16[128,1024]{1,0:T(8,128)(2,1)S(1)} collective-permute-done((bf16[128,1024]{1,0:T(8,128)(2,1)S(1)}, bf16[128,1024]{1,0:T(8,128)(2,1)S(1)}, u32[]{:S(2)}, u32[]{:S(2)}) %collective-permute-start.4) | collective-permute-done | bytes 262176 | tf_op jit(solution)/shard_map/ppermute | solution.py:518
  61.6 0.0 slice-done
  61.7 0.0 slice-done.1
  61.7 11.2 %backward1.1 = (f32[128,1024]{1,0:T(8,128)S(1)}, bf16[64,1024]{1,0:T(8,128)(2,1)S(1)}, f32[8,1024]{1,0:T(8,128)S(1)}, f32[8,1024]{1,0:T(8,128)S(1)}) custom-call(f32[128,1024]{1,0:T(8,128)S(1)} %get-tuple-element.22.final, bf16[128,1024]{1,0:T(8,128)(2,1)S(1)} %collective-permute-done.2.near, bf16[128,1024]{1,0:T(8,128)(2,1)S(1)} %collective-permute-done.3.far, ...), custom_call_target="tpu_custom_call" | custom-call | tf_op jit(solution)/shard_map/backward1/pallas_call | solution.py:473
  72.8 1.1 collective-permute-start.5
  74.0 6.2 %collective-permute-done.5.d_east = bf16[64,1024]{1,0:T(8,128)(2,1)S(1)} collective-permute-done((bf16[64,1024]{1,0:T(8,128)(2,1)S(1)}, bf16[64,1024]{1,0:T(8,128)(2,1)S(1)}, u32[]{:S(2)}, u32[]{:S(2)}) %collective-permute-start.5) | collective-permute-done | bytes 131104 | tf_op jit(solution)/shard_map/ppermute | solution.py:513
  80.1 11.6 %backward0.1 = (f32[8,16,1024]{2,1,0:T(8,128)S(1)}, bf16[64,1024]{1,0:T(8,128)(2,1)S(1)}, f32[2,1024]{1,0:T(2,128)S(1)}) custom-call(s32[2,2]{1,0:T(2,128)S(1)} %copy-done.6, f32[128,1024]{1,0:T(8,128)S(1)} %get-tuple-element.30.d_in, bf16[64,1024]{1,0:T(8,128)(2,1)S(1)} %collective-permute-done.5.d_east, bf16[128,3072]{1,0:T(8,128)(2,1)S(1)} %get-tuple-element.32.packed, ...), custom_call_target="tpu_custom_call" | custom-call | tf_op jit(solution)/shard_map/backward0/pallas_call | solution.py:491
  91.7 0.1 collective-permute-start.7
  91.8 1.2 collective-permute-done.7
  93.0 0.3 collective-permute-start.8
  93.3 3.4 %collective-permute-done.8 = f32[2,1024]{1,0:T(2,128)S(1)} collective-permute-done((f32[2,1024]{1,0:T(2,128)S(1)}, f32[2,1024]{1,0:T(2,128)S(1)}, u32[]{:S(2)}, u32[]{:S(2)}) %collective-permute-start.8) | collective-permute-done | bytes 8224 | tf_op jit(solution)/shard_map/ppermute | solution.py:518
  96.6 0.4 collective-permute-start.9
  97.1 4.7 %collective-permute-done.9 = f32[2,1024]{1,0:T(2,128)S(1)} collective-permute-done((f32[2,1024]{1,0:T(2,128)S(1)}, f32[2,1024]{1,0:T(2,128)S(1)}, u32[]{:S(2)}, u32[]{:S(2)}) %collective-permute-start.9) | collective-permute-done | bytes 8224 | tf_op jit(solution)/shard_map/ppermute | solution.py:518
  101.8 0.0 collective-permute-start.10
  101.8 3.6 %collective-permute-done.10 = f32[2,1024]{1,0:T(2,128)S(1)} collective-permute-done((f32[2,1024]{1,0:T(2,128)S(1)}, f32[2,1024]{1,0:T(2,128)S(1)}, u32[]{:S(2)}, u32[]{:S(2)}) %collective-permute-start.10) | collective-permute-done | bytes 8224 | tf_op jit(solution)/shard_map/ppermute | solution.py:518
  105.5 0.9 collective-permute-start.11
  106.4 4.2 %collective-permute-done.11 = f32[2,1024]{1,0:T(2,128)S(1)} collective-permute-done((f32[2,1024]{1,0:T(2,128)S(1)}, f32[2,1024]{1,0:T(2,128)S(1)}, u32[]{:S(2)}, u32[]{:S(2)}) %collective-permute-start.11) | collective-permute-done | bytes 8224 | tf_op jit(solution)/shard_map/ppermute | solution.py:518
  110.6 2.7 %collective-permute-start.12 = (f32[2,1024]{1,0:T(2,128)S(1)}, f32[2,1024]{1,0:T(2,128)S(1)}, u32[]{:S(2)}, u32[]{:S(2)}) collective-permute-start(f32[2,1024]{1,0:T(2,128)S(1)} %add.28), channel_id=1, source_target_pairs={{0,8},{1,9},{2,10},{3,11},{4,12},{5,13},{6,14},{7,15},{8,0},{9,1},... | collective-permute-start | bytes 24584 | tf_op jit(solution)/shard_map/ppermute | solution.py:518
  113.4 1.6 %collective-permute-done.12 = f32[2,1024]{1,0:T(2,128)S(1)} collective-permute-done((f32[2,1024]{1,0:T(2,128)S(1)}, f32[2,1024]{1,0:T(2,128)S(1)}, u32[]{:S(2)}, u32[]{:S(2)}) %collective-permute-start.12) | collective-permute-done | bytes 8224 | tf_op jit(solution)/shard_map/ppermute | solution.py:518
  115.0 2.5 %collective-permute-start.13 = (f32[2,1024]{1,0:T(2,128)S(1)}, f32[2,1024]{1,0:T(2,128)S(1)}, u32[]{:S(2)}, u32[]{:S(2)}) collective-permute-start(f32[2,1024]{1,0:T(2,128)S(1)} %add.29), channel_id=1, source_target_pairs={{0,16},{1,17},{2,18},{3,19},{4,20},{5,21},{6,22},{7,23},{8,24},{9,... | collective-permute-start | bytes 24584 | tf_op jit(solution)/shard_map/ppermute | solution.py:518
  117.6 0.6 slice.53
  118.1 1.4 %collective-permute-done.13 = f32[2,1024]{1,0:T(2,128)S(1)} collective-permute-done((f32[2,1024]{1,0:T(2,128)S(1)}, f32[2,1024]{1,0:T(2,128)S(1)}, u32[]{:S(2)}, u32[]{:S(2)}) %collective-permute-start.13) | collective-permute-done | bytes 8224 | tf_op jit(solution)/shard_map/ppermute | solution.py:518
  119.6 5.6 %collective-permute-start.14 = (f32[2,1024]{1,0:T(2,128)S(1)}, f32[2,1024]{1,0:T(2,128)S(1)}, u32[]{:S(2)}, u32[]{:S(2)}) collective-permute-start(f32[2,1024]{1,0:T(2,128)S(1)} %add.30), channel_id=1, source_target_pairs={{0,32},{1,33},{2,34},{3,35},{4,36},{5,37},{6,38},{7,39},{8,40},{9,... | collective-permute-start | bytes 24584 | tf_op jit(solution)/shard_map/ppermute | solution.py:518
  125.1 0.6 iota_compare_fusion
  125.8 0.9 collective-permute-start.6
  126.7 0.4 collective-permute-done.14
  127.1 0.6 slice_multiply_fusion
  127.7 7.6 %collective-permute-done.6 = bf16[64,1024]{1,0:T(8,128)(2,1)S(1)} collective-permute-done((bf16[64,1024]{1,0:T(8,128)(2,1)S(1)}, bf16[64,1024]{1,0:T(8,128)(2,1)S(1)}, u32[]{:S(2)}, u32[]{:S(2)}) %collective-permute-start.6) | collective-permute-done | bytes 131104 | tf_op jit(solution)/shard_map/ppermute | solution.py:513
  135.4 0.1 convert_select_fusion
  135.4 0.8 maximum_bitcast_fusion
  (11 shorter events, 0.1 us)
Async XLA Ops:
  0.6 33.1 %copy-start.3 = (bf16[2,1,8,16,1024]{4,3,2,1,0:T(8,128)(2,1)S(1)}, bf16[2,1,8,16,1024]{4,3,2,1,0:T(8,128)(2,1)}, u32[]{:S(2)}) copy-start(bf16[2,1,8,16,1024]{4,3,2,1,0:T(8,128)(2,1)} %param.10) | copy-start | bytes 1572868
  0.6 33.1 %copy-start.1 = (f32[1,8,16,1024]{3,2,1,0:T(8,128)S(1)}, f32[1,8,16,1024]{3,2,1,0:T(8,128)}, u32[]{:S(2)}) copy-start(f32[1,8,16,1024]{3,2,1,0:T(8,128)} %param.8) | copy-start | bytes 1572868
  0.7 33.1 %copy-start.2 = (f32[8,16,1024]{2,1,0:T(8,128)S(1)}, f32[8,16,1024]{2,1,0:T(8,128)}, u32[]{:S(2)}) copy-start(f32[8,16,1024]{2,1,0:T(8,128)} %target.1) | copy-start | bytes 1572868
  0.7 33.1 %copy-start.4 = (f32[1024]{0:T(1024)S(1)}, f32[1024]{0:T(1024)}, u32[]{:S(2)}) copy-start(f32[1024]{0:T(1024)} %param.13) | copy-start | bytes 12292
  0.7 33.1 %copy-start.5 = (f32[1024]{0:T(1024)S(1)}, f32[1024]{0:T(1024)}, u32[]{:S(2)}) copy-start(f32[1024]{0:T(1024)} %param.14) | copy-start | bytes 12292
  0.7 33.1 %copy-start = (bf16[1024,1024]{1,0:T(8,128)(2,1)S(1)}, bf16[1024,1024]{1,0:T(8,128)(2,1)}, u32[]{:S(2)}) copy-start(bf16[1024,1024]{1,0:T(8,128)(2,1)} %w_out_hbm.5) | copy-start | bytes 6291460
  0.7 33.1 %copy-start.6 = (s32[2,2]{1,0:T(2,128)S(1)}, s32[2,2]{1,0:T(2,128)}, u32[]{:S(2)}) copy-start(s32[2,2]{1,0:T(2,128)} %shifts.3) | copy-start | bytes 52
  4.3 57.4 %slice-start = ((s8[6291456]{0:T(1024)(128)(4,1)}), s8[4194304]{0:T(1024)(128)(4,1)S(1)}, s32[]{:S(2)}) async-start(s8[6291456]{0:T(1024)(128)(4,1)} %bitcast.33), calls=%async_computation | async-start | bytes 8388608
  4.3 25.7 %collective-permute-start.1 = (bf16[4,64,1024]{2,1,0:T(8,128)(2,1)S(1)}, bf16[4,64,1024]{2,1,0:T(8,128)(2,1)S(1)}, u32[]{:S(2)}, u32[]{:S(2)}) collective-permute-start(bf16[4,64,1024]{2,1,0:T(8,128)(2,1)S(1)} %pad_maximum_fusion.1), channel_id=1, source_target_pairs={{0,1},{1,2},{2,3},{3,4},{4,5},{5,6},{6,7},{7,8},{8,9},{9,10},{10,1... | collective-permute-start | bytes 1572872 | tf_op jit(solution)/shard_map/ppermute | solution.py:513
  7.6 26.1 %collective-permute-start = (bf16[4,64,1024]{2,1,0:T(8,128)(2,1)S(1)}, bf16[4,64,1024]{2,1,0:T(8,128)(2,1)S(1)}, u32[]{:S(2)}, u32[]{:S(2)}) collective-permute-start(bf16[4,64,1024]{2,1,0:T(8,128)(2,1)S(1)} %pad_maximum_fusion), channel_id=1, source_target_pairs={{0,63},{1,0},{2,1},{3,2},{4,3},{5,4},{6,5},{7,6},{8,7},{9,8},{10,9... | collective-permute-start | bytes 1572872 | tf_op jit(solution)/shard_map/ppermute | solution.py:513
  33.8 27.8 %slice-start.1 = ((s8[6291456]{0:T(1024)(128)(4,1)}), s8[2097152]{0:T(1024)(128)(4,1)S(1)}, s32[]{:S(2)}) async-start(s8[6291456]{0:T(1024)(128)(4,1)} %bitcast.33), calls=%async_computation.1 | async-start | bytes 4194304
  51.8 8.3 %collective-permute-start.3 = (bf16[128,1024]{1,0:T(8,128)(2,1)S(1)}, bf16[128,1024]{1,0:T(8,128)(2,1)S(1)}, u32[]{:S(2)}, u32[]{:S(2)}) collective-permute-start(bf16[128,1024]{1,0:T(8,128)(2,1)S(1)} %get-tuple-element.23), channel_id=1, source_target_pairs={{0,128},{64,192},{128,0},{192,64},{1,129},{65,193},{129,1},{193,65... | collective-permute-start | bytes 786440 | tf_op jit(solution)/shard_map/ppermute | solution.py:518
  52.6 7.5 %collective-permute-start.2 = (bf16[128,1024]{1,0:T(8,128)(2,1)S(1)}, bf16[128,1024]{1,0:T(8,128)(2,1)S(1)}, u32[]{:S(2)}, u32[]{:S(2)}) collective-permute-start(bf16[128,1024]{1,0:T(8,128)(2,1)S(1)} %get-tuple-element.23), channel_id=1, source_target_pairs={{0,64},{64,0},{128,192},{192,128},{1,65},{65,1},{129,193},{193,129... | collective-permute-start | bytes 786440 | tf_op jit(solution)/shard_map/ppermute | solution.py:518
  60.1 1.5 %collective-permute-start.4 = (bf16[128,1024]{1,0:T(8,128)(2,1)S(1)}, bf16[128,1024]{1,0:T(8,128)(2,1)S(1)}, u32[]{:S(2)}, u32[]{:S(2)}) collective-permute-start(bf16[128,1024]{1,0:T(8,128)(2,1)S(1)} %collective-permute-done.3.far), channel_id=1, source_target_pairs={{0,64},{64,0},{128,192},{192,128},{1,65},{65,1},{129,193},{193,129... | collective-permute-start | bytes 786440 | tf_op jit(solution)/shard_map/ppermute | solution.py:518
  72.8 7.3 %collective-permute-start.5 = (bf16[64,1024]{1,0:T(8,128)(2,1)S(1)}, bf16[64,1024]{1,0:T(8,128)(2,1)S(1)}, u32[]{:S(2)}, u32[]{:S(2)}) collective-permute-start(bf16[64,1024]{1,0:T(8,128)(2,1)S(1)} %get-tuple-element.31), channel_id=1, source_target_pairs={{0,63},{1,0},{2,1},{3,2},{4,3},{5,4},{6,5},{7,6},{8,7},{9,8},{10,9... | collective-permute-start | bytes 393224 | tf_op jit(solution)/shard_map/ppermute | solution.py:513
  91.7 1.3 collective-permute-start.7
  93.0 3.7 %collective-permute-start.8 = (f32[2,1024]{1,0:T(2,128)S(1)}, f32[2,1024]{1,0:T(2,128)S(1)}, u32[]{:S(2)}, u32[]{:S(2)}) collective-permute-start(f32[2,1024]{1,0:T(2,128)S(1)} %add.24), channel_id=1, source_target_pairs={{0,128},{64,192},{128,0},{192,64},{1,129},{65,193},{129,1},{193,65... | collective-permute-start | bytes 24584 | tf_op jit(solution)/shard_map/ppermute | solution.py:518
  96.6 5.2 %collective-permute-start.9 = (f32[2,1024]{1,0:T(2,128)S(1)}, f32[2,1024]{1,0:T(2,128)S(1)}, u32[]{:S(2)}, u32[]{:S(2)}) collective-permute-start(f32[2,1024]{1,0:T(2,128)S(1)} %add.25), channel_id=1, source_target_pairs={{0,1},{1,0},{2,3},{3,2},{4,5},{5,4},{6,7},{7,6},{8,9},{9,8},{10,11... | collective-permute-start | bytes 24584 | tf_op jit(solution)/shard_map/ppermute | solution.py:518
  101.8 3.7 %collective-permute-start.10 = (f32[2,1024]{1,0:T(2,128)S(1)}, f32[2,1024]{1,0:T(2,128)S(1)}, u32[]{:S(2)}, u32[]{:S(2)}) collective-permute-start(f32[2,1024]{1,0:T(2,128)S(1)} %add.26), channel_id=1, source_target_pairs={{0,2},{1,3},{2,0},{3,1},{4,6},{5,7},{6,4},{7,5},{8,10},{9,11},{10,... | collective-permute-start | bytes 24584 | tf_op jit(solution)/shard_map/ppermute | solution.py:518
  105.5 5.2 %collective-permute-start.11 = (f32[2,1024]{1,0:T(2,128)S(1)}, f32[2,1024]{1,0:T(2,128)S(1)}, u32[]{:S(2)}, u32[]{:S(2)}) collective-permute-start(f32[2,1024]{1,0:T(2,128)S(1)} %add.27), channel_id=1, source_target_pairs={{0,4},{1,5},{2,6},{3,7},{4,0},{5,1},{6,2},{7,3},{8,12},{9,13},{10,... | collective-permute-start | bytes 24584 | tf_op jit(solution)/shard_map/ppermute | solution.py:518
  110.6 4.4 %collective-permute-start.12 = (f32[2,1024]{1,0:T(2,128)S(1)}, f32[2,1024]{1,0:T(2,128)S(1)}, u32[]{:S(2)}, u32[]{:S(2)}) collective-permute-start(f32[2,1024]{1,0:T(2,128)S(1)} %add.28), channel_id=1, source_target_pairs={{0,8},{1,9},{2,10},{3,11},{4,12},{5,13},{6,14},{7,15},{8,0},{9,1},... | collective-permute-start | bytes 24584 | tf_op jit(solution)/shard_map/ppermute | solution.py:518
  115.0 4.5 %collective-permute-start.13 = (f32[2,1024]{1,0:T(2,128)S(1)}, f32[2,1024]{1,0:T(2,128)S(1)}, u32[]{:S(2)}, u32[]{:S(2)}) collective-permute-start(f32[2,1024]{1,0:T(2,128)S(1)} %add.29), channel_id=1, source_target_pairs={{0,16},{1,17},{2,18},{3,19},{4,20},{5,21},{6,22},{7,23},{8,24},{9,... | collective-permute-start | bytes 24584 | tf_op jit(solution)/shard_map/ppermute | solution.py:518
  119.6 7.6 %collective-permute-start.14 = (f32[2,1024]{1,0:T(2,128)S(1)}, f32[2,1024]{1,0:T(2,128)S(1)}, u32[]{:S(2)}, u32[]{:S(2)}) collective-permute-start(f32[2,1024]{1,0:T(2,128)S(1)} %add.30), channel_id=1, source_target_pairs={{0,32},{1,33},{2,34},{3,35},{4,36},{5,37},{6,38},{7,39},{8,40},{9,... | collective-permute-start | bytes 24584 | tf_op jit(solution)/shard_map/ppermute | solution.py:518
  125.8 9.6 %collective-permute-start.6 = (bf16[64,1024]{1,0:T(8,128)(2,1)S(1)}, bf16[64,1024]{1,0:T(8,128)(2,1)S(1)}, u32[]{:S(2)}, u32[]{:S(2)}) collective-permute-start(bf16[64,1024]{1,0:T(8,128)(2,1)S(1)} %get-tuple-element.38), channel_id=1, source_target_pairs={{0,1},{1,2},{2,3},{3,4},{4,5},{5,6},{6,7},{7,8},{8,9},{9,10},{10,1... | collective-permute-start | bytes 393224 | tf_op jit(solution)/shard_map/ppermute | solution.py:513
where the time goes:
time: 136 us
  waiting for transfers between devices  66.1 us (49%)
  Pallas kernels  40.7 us (30%)
  starting transfers between devices  22.1 us (16%)
  other arithmetic  4.51 us (3%)
  local copies, waits for them, and re-layouts  1.92 us (1%)
    ppermute x4, waiting for transfers between devices, along(): lax.ppermute(value, axis, [(at, (at + steps) % count) for at in range(cou...  36.5 us
    ppermute x11, waiting for transfers between devices, swapped(): return lax.ppermute(value, axis, [(at, at ^ bit) for at in range(count)])  29.6 us
    pallas_call x1, Pallas kernels, forward(): pl.pallas_call(forward_kernel, out_shape=out_shape, in_specs=[smem()] + [...  18 us
    ppermute x11, starting transfers between devices, swapped(): return lax.ppermute(value, axis, [(at, at ^ bit) for at in range(count)])  13.4 us
    pallas_call x1, Pallas kernels, backward0(): pl.pallas_call(backward0_kernel, out_shape=[jax.ShapeDtypeStruct((LAT, 16...  11.6 us
    pallas_call x1, Pallas kernels, backward1(): pl.pallas_call(backward1_kernel, out_shape=[jax.ShapeDtypeStruct((rows, C...  11.2 us
    ppermute x4, starting transfers between devices, along(): lax.ppermute(value, axis, [(at, (at + steps) % count) for at in range(cou...  8.73 us
  transfers between devices with their start and end apart: 15, of which 14 were waited for; matrix products, arithmetic and copies ran while one was open for 1% of the time, Pallas kernels for 0%

commit v1 on v0

v1 whole, which is shorter than its diff:
```python
import functools

import jax
import jax.numpy as jnp
from jax import lax
from jax.experimental import pallas as pl
from jax.experimental.pallas import tpu as pltpu
from jax.sharding import PartitionSpec as P

C = 1024
HEAD = 32
WIN = 8
LAT = 8
TOK = LAT * WIN
GROUP = 4
LANES = GROUP * HEAD
GROUPS = C // LANES
SPAN = GROUP * TOK
SCALE = HEAD ** (-0.5)
SMOOTH = 0.25
F32 = jnp.float32
BF16 = jnp.bfloat16
VMEM_LIMIT = 16 * 1024 * 1024


def dot(left, right):
    return lax.dot_general(left, right, (((1,), (0,)), ((), ())), preferred_element_type=F32)


def dot_nt(left, right):
    return lax.dot_general(left, right, (((1,), (1,)), ((), ())), preferred_element_type=F32)


def dot_tn(left, right):
    return lax.dot_general(left, right, (((0,), (0,)), ((), ())), preferred_element_type=F32)


def head_masks():
    lane = lax.broadcasted_iota(jnp.int32, (TOK, LANES), 1) // HEAD
    return [lane == head for head in range(GROUP)]


def by_head(value, masks):
    zero = jnp.zeros_like(value)
    return jnp.concatenate([jnp.where(mask, value, zero) for mask in masks], axis=0)


def fold_heads(stacked, masks):
    out = stacked[:TOK]
    for head in range(1, GROUP):
        out = jnp.where(masks[head], stacked[head * TOK : (head + 1) * TOK], out)
    return out


def lat_mask(lat_shift):
    key_lat = lax.broadcasted_iota(jnp.int32, (TOK, SPAN), 0) // WIN
    query_lat = (lax.broadcasted_iota(jnp.int32, (TOK, SPAN), 1) % TOK) // WIN
    return (key_lat < lat_shift) == (query_lat < lat_shift)


def lanes(start, size):
    return pl.ds(pl.multiple_of(start, 128), size)


def fill(ext, own_ref, west, east):
    for row in range(LAT):
        ext[row, 0:8, :] = west[row * WIN : (row + 1) * WIN]
        ext[row, 8:24, :] = own_ref[row].astype(F32)
        ext[row, 24:32, :] = east[row * WIN : (row + 1) * WIN]


def frame(ext, row, start, columns):
    held = ext.shape[1]
    return pltpu.roll(ext[row], lax.rem(held - start, held), 0)[:columns]


def norm_rows(x_ref, rows, gain, normed_ref, scaled_ref, spread_ref, saved_from):
    for at in range(0, rows, 32):
        x = x_ref[at : at + 32, :]
        centre = jnp.mean(x, axis=-1, keepdims=True)
        offset = x - centre
        spread = lax.rsqrt(jnp.mean(offset * offset, axis=-1, keepdims=True) + 1e-05)
        scaled = offset * spread
        normed_ref[at : at + 32, :] = (scaled * gain).astype(BF16)
        if at >= saved_from:
            scaled_ref[at - saved_from : at - saved_from + 32, :] = scaled
            spread_ref[at - saved_from : at - saved_from + 32, :] = jnp.broadcast_to(
                spread, (32, 128)
            )


def attend(windows, packed_ref, weights_ref, mixed_ref, lat_shift, saved_from):
    masks = head_masks()
    allowed = lat_mask(lat_shift)

    def group(at, _):
        for window in range(windows):
            rows = slice(window * TOK, (window + 1) * TOK)
            queries = packed_ref[rows, lanes(at * LANES, LANES)]
            keys = packed_ref[rows, lanes(C + at * LANES, LANES)]
            values = packed_ref[rows, lanes(2 * C + at * LANES, LANES)]
            scores = dot_nt(keys, by_head(queries, masks))
            scores = jnp.where(allowed, scores, -1e9 / SCALE)
            highest = jnp.max(scores, axis=0, keepdims=True)
            raised = jnp.exp((scores - highest) * SCALE)
            total = jnp.sum(raised, axis=0, keepdims=True)
            weights = (raised * (1.0 / total)).astype(BF16)
            if window >= saved_from:
                weights_ref[(window - saved_from) * GROUPS + at] = weights
            mixed = fold_heads(dot_tn(weights, values), masks)
            mixed_ref[rows, lanes(at * LANES, LANES)] = mixed.astype(BF16)
        return 0

    lax.fori_loop(0, GROUPS, group, 0, unroll=GROUPS)


def window_rows(window, row):
    start = window * TOK + row * WIN
    return slice(start, start + WIN)


def forward0_kernel(
    shifts,
    initial,
    east,
    west,
    gain,
    w_qkv,
    w_out,
    following_out,
    packed_out,
    weights_out,
    scaled_out,
    spread_out,
    ext,
    state,
    normed,
    packed,
    mixed,
):
    lat_shift, lon_shift = shifts[0, 0], shifts[0, 1]
    fill(ext, initial, west[...].astype(F32), east[...].astype(F32))
    for row in range(LAT):
        part = frame(ext, row, lon_shift, 24)
        for window in range(3):
            state[window_rows(window, row), :] = part[window * WIN : (window + 1) * WIN]
    norm_rows(state, 3 * TOK, gain[...], normed, scaled_out, spread_out, TOK)
    for part in range(6):
        at = slice(part * 512, (part + 1) * 512)
        packed[:, at] = dot(normed[...], w_qkv[:, at]).astype(BF16)
    packed_out[...] = packed[TOK:, :]
    attend(3, packed, weights_out, mixed, lat_shift, 1)
    for part in range(4):
        at = slice(part * 256, (part + 1) * 256)
        following = state[:, at] + dot(mixed[...], w_out[:, at])
        for row in range(LAT):
            for window in range(3):
                following_out[row, window * WIN : (window + 1) * WIN, at] = following[
                    window_rows(window, row)
                ]


def forward1_kernel(
    shifts,
    before,
    noise,
    east,
    west,
    gain,
    noise_scale,
    w_qkv,
    w_out,
    final_out,
    sent_out,
    noise_out,
    packed_out,
    weights_out,
    scaled_out,
    spread_out,
    ext,
    state,
    normed,
    mixed,
):
    lat_shift = shifts[1, 0]
    lon0, origin1 = shifts[0, 1], origin(shifts)
    scale = noise_scale[...]
    for step in range(2):
        fill(ext, noise.at[step], west[step].astype(F32), east[step].astype(F32))
        for row in range(LAT):
            part = frame(ext, row, origin1 + WIN, 16)
            fields = frame(before, row, origin1 - lon0 + WIN, 16)
            for window in range(2):
                rows = window_rows(window, row)
                here = part[window * WIN : (window + 1) * WIN]
                if step == 0:
                    state[rows, :] = fields[window * WIN : (window + 1) * WIN] + scale * here
                else:
                    final_out[rows, :] = state[rows, :] + scale * here
                noise_out[step, rows, :] = here
    norm_rows(state, 2 * TOK, gain[...], normed, scaled_out, spread_out, 0)
    for part in range(6):
        at = slice(part * 512, (part + 1) * 512)
        packed_out[:, at] = dot(normed[...], w_qkv[:, at]).astype(BF16)
    attend(2, packed_out, weights_out, mixed, lat_shift, 0)
    for part in range(4):
        at = slice(part * 256, (part + 1) * 256)
        final = final_out[:, at] + dot(mixed[...], w_out[:, at])
        final_out[:, at] = final
        sent_out[:, at] = final.astype(BF16)


def origin(shifts):
    lon0, lon1 = shifts[0, 1], shifts[1, 1]
    return jnp.where(lon1 <= lon0, lon1, lon1 - WIN)


def vmem():
    return pl.BlockSpec(memory_space=pltpu.VMEM)


def smem():
    return pl.BlockSpec(memory_space=pltpu.SMEM)


def compiler_params():
    return pltpu.CompilerParams(vmem_limit_bytes=VMEM_LIMIT)


def saved_shapes():
    rows = 2 * TOK
    return [
        jax.ShapeDtypeStruct((rows, 3 * C), BF16),
        jax.ShapeDtypeStruct((2 * GROUPS, TOK, SPAN), BF16),
        jax.ShapeDtypeStruct((rows, C), F32),
        jax.ShapeDtypeStruct((rows, 128), F32),
    ]


def forward0(shifts, initial, east, west, gain, w_qkv, w_out):
    rows = 3 * TOK
    out_shape = [jax.ShapeDtypeStruct((LAT, 24, C), F32)] + saved_shapes()
    return pl.pallas_call(
        forward0_kernel,
        out_shape=out_shape,
        in_specs=[smem()] + [vmem()] * 6,
        out_specs=[vmem()] * len(out_shape),
        scratch_shapes=[
            pltpu.VMEM((LAT, 32, C), F32),
            pltpu.VMEM((rows, C), F32),
            pltpu.VMEM((rows, C), BF16),
            pltpu.VMEM((rows, 3 * C), BF16),
            pltpu.VMEM((rows, C), BF16),
        ],
        compiler_params=compiler_params(),
        name="forward0",
    )(shifts, initial, east, west, gain, w_qkv, w_out)


def forward1(shifts, before, noise, east, west, gain, noise_scale, w_qkv, w_out):
    rows = 2 * TOK
    out_shape = [
        jax.ShapeDtypeStruct((rows, C), F32),
        jax.ShapeDtypeStruct((rows, C), BF16),
        jax.ShapeDtypeStruct((2, rows, C), F32),
    ] + saved_shapes()
    return pl.pallas_call(
        forward1_kernel,
        out_shape=out_shape,
        in_specs=[smem()] + [vmem()] * 8,
        out_specs=[vmem()] * len(out_shape),
        scratch_shapes=[
            pltpu.VMEM((LAT, 32, C), F32),
            pltpu.VMEM((rows, C), F32),
            pltpu.VMEM((rows, C), BF16),
            pltpu.VMEM((rows, C), BF16),
        ],
        compiler_params=compiler_params(),
        name="forward1",
    )(shifts, before, noise, east, west, gain, noise_scale, w_qkv, w_out)


def attend_back(packed, weights_ref, d_mixed, d_packed):
    masks = head_masks()

    def group(at, _):
        for window in range(2):
            rows = slice(window * TOK, (window + 1) * TOK)
            here = lanes(at * LANES, LANES)
            queries = packed[rows, here]
            keys = packed[rows, lanes(C + at * LANES, LANES)]
            values = packed[rows, lanes(2 * C + at * LANES, LANES)]
            d_mixed_blocks = by_head(d_mixed[rows, here], masks)
            weights = weights_ref[window * GROUPS + at]
            d_weights = dot_nt(values, d_mixed_blocks)
            d_values = dot(weights, d_mixed_blocks)
            probs = weights.astype(F32)
            centred = d_weights - jnp.sum(d_weights * probs, axis=0, keepdims=True)
            d_scores = (probs * centred * SCALE).astype(BF16)
            d_keys = dot(d_scores, by_head(queries, masks))
            d_queries = fold_heads(dot_tn(d_scores, keys), masks)
            d_packed[rows, here] = d_queries.astype(BF16)
            d_packed[rows, lanes(C + at * LANES, LANES)] = d_keys.astype(BF16)
            d_packed[rows, lanes(2 * C + at * LANES, LANES)] = d_values.astype(BF16)
        return 0

    lax.fori_loop(0, GROUPS, group, 0, unroll=GROUPS)


def slope(difference):
    return difference * lax.rsqrt(difference * difference + SMOOTH * SMOOTH)


def step_back(
    d_next, packed, weights, w_qkv_t, w_out_t, d_mixed, d_packed, d_normed
):
    d_branch = d_next[...].astype(BF16)
    for part in range(4):
        at = slice(part * 256, (part + 1) * 256)
        d_mixed[:, at] = dot(d_branch, w_out_t[:, at]).astype(BF16)
    attend_back(packed, weights, d_mixed, d_packed)
    for part in range(4):
        at = slice(part * 256, (part + 1) * 256)
        d_normed[:, at] = dot(d_packed[...], w_qkv_t[:, at])


def norm_back(at, d_next, scaled_ref, spread_ref, d_normed, gain):
    rows = slice(at, at + 32)
    scaled = scaled_ref[rows, :]
    d_here = d_normed[rows, :]
    d_hat = d_here * gain
    spread = spread_ref[rows, 0:1]
    d_fields = spread * (
        d_hat
        - jnp.mean(d_hat, axis=-1, keepdims=True)
        - scaled * jnp.mean(d_hat * scaled, axis=-1, keepdims=True)
    )
    return d_next[rows, :] + d_fields, eight_rows(d_here * scaled)


def eight_rows(value):
    out = value[0:8]
    for at in range(8, value.shape[0], 8):
        out = out + value[at : at + 8]
    return out


def backward1_kernel(
    shifts,
    final,
    near,
    far,
    far_near,
    target,
    east,
    west,
    noise,
    packed,
    weights,
    scaled,
    spread,
    gain,
    w_qkv_t,
    w_out_t,
    d_out,
    head_out,
    gain_out,
    scale_out,
    ext,
    d_next,
    d_mixed,
    d_packed,
    d_normed,
):
    fill(ext, target, west[...].astype(F32), east[...].astype(F32))
    for row in range(LAT):
        part = frame(ext, row, origin(shifts) + WIN, 16)
        for window in range(2):
            d_normed[window_rows(window, row), :] = part[window * WIN : (window + 1) * WIN]
    scale_total = jnp.zeros((8, C), F32)
    for at in range(0, 2 * TOK, 32):
        rows = slice(at, at + 32)
        here = final[rows, :]
        pairs = (
            slope(here - near[rows, :].astype(F32))
            + slope(here - far[rows, :].astype(F32))
            + slope(here - far_near[rows, :].astype(F32))
        )
        seed = slope(here - d_normed[rows, :]) - pairs * (1.0 / 3.0)
        d_next[rows, :] = seed
        scale_total = scale_total + eight_rows(seed * noise[1, rows, :])
    step_back(d_next, packed, weights, w_qkv_t, w_out_t, d_mixed, d_packed, d_normed)
    gain_total = jnp.zeros((8, C), F32)
    for at in range(0, 2 * TOK, 32):
        rows = slice(at, at + 32)
        d_here, gain_part = norm_back(at, d_next, scaled, spread, d_normed, gain[...])
        d_out[rows, :] = d_here
        if at < TOK:
            head_out[rows, :] = d_here.astype(BF16)
        gain_total = gain_total + gain_part
        scale_total = scale_total + eight_rows(d_here * noise[0, rows, :])
    gain_out[...] = gain_total
    scale_out[...] = scale_total


def backward0_kernel(
    shifts,
    d_in,
    d_east,
    packed,
    weights,
    scaled,
    spread,
    gain,
    gain_in,
    scale_in,
    w_qkv_t,
    w_out_t,
    own_out,
    tail_out,
    sums_out,
    ext,
    d_next,
    d_mixed,
    d_packed,
    d_normed,
):
    lon0, origin1 = shifts[0, 1], origin(shifts)
    east = d_east[...].astype(F32)
    for row in range(LAT):
        ext[row, 0:8, :] = d_in[row * WIN : (row + 1) * WIN, :]
        ext[row, 8:16, :] = d_in[TOK + row * WIN : TOK + (row + 1) * WIN, :]
        ext[row, 16:24, :] = east[row * WIN : (row + 1) * WIN]
    for row in range(LAT):
        part = frame(ext, row, lon0 - origin1, 16)
        for window in range(2):
            d_next[window_rows(window, row), :] = part[window * WIN : (window + 1) * WIN]
    step_back(d_next, packed, weights, w_qkv_t, w_out_t, d_mixed, d_packed, d_normed)
    gain_total = gain_in[...]
    for at in range(0, 2 * TOK, 32):
        d_here, gain_part = norm_back(at, d_next, scaled, spread, d_normed, gain[...])
        gain_total = gain_total + gain_part
        for piece in range(4):
            token = at + piece * WIN
            row, window = (token % TOK) // WIN, token // TOK
            ext[row, 8 + window * WIN : 16 + window * WIN, :] = d_here[
                piece * WIN : (piece + 1) * WIN
            ]
    sums_out[0:1, :] = jnp.sum(gain_total, axis=0, keepdims=True)
    sums_out[1:2, :] = jnp.sum(scale_in[...], axis=0, keepdims=True)
    tails = []
    for row in range(LAT):
        own_out[row] = frame(ext, row, WIN - lon0, 16)
        tails.append(frame(ext, row, 24 - lon0, WIN))
    tail_out[...] = jnp.concatenate(tails, axis=0).astype(BF16)


def backward_scratch():
    rows = 2 * TOK
    return [
        pltpu.VMEM((LAT, 32, C), F32),
        pltpu.VMEM((rows, C), F32),
        pltpu.VMEM((rows, C), BF16),
        pltpu.VMEM((rows, 3 * C), BF16),
        pltpu.VMEM((rows, C), F32),
    ]


def backward1(shifts, final, others, target, east, west, noise, saved, gain, w_qkv_t, w_out_t):
    rows = 2 * TOK
    return pl.pallas_call(
        backward1_kernel,
        out_shape=[
            jax.ShapeDtypeStruct((rows, C), F32),
            jax.ShapeDtypeStruct((TOK, C), BF16),
            jax.ShapeDtypeStruct((8, C), F32),
            jax.ShapeDtypeStruct((8, C), F32),
        ],
        in_specs=[smem()] + [vmem()] * 15,
        out_specs=[vmem()] * 4,
        scratch_shapes=backward_scratch(),
        compiler_params=compiler_params(),
        name="backward1",
    )(shifts, final, *others, target, east, west, noise, *saved, gain, w_qkv_t, w_out_t)


def backward0(shifts, d_in, d_east, saved, gain, gain_in, scale_in, w_qkv_t, w_out_t):
    return pl.pallas_call(
        backward0_kernel,
        out_shape=[
            jax.ShapeDtypeStruct((LAT, 16, C), F32),
            jax.ShapeDtypeStruct((TOK, C), BF16),
            jax.ShapeDtypeStruct((2, C), F32),
        ],
        in_specs=[smem()] + [vmem()] * 11,
        out_specs=[vmem()] * 3,
        scratch_shapes=backward_scratch(),
        compiler_params=compiler_params(),
        name="backward0",
    )(shifts, d_in, d_east, *saved, gain, gain_in, scale_in, w_qkv_t, w_out_t)


def along(value, axis, steps):
    count = lax.axis_size(axis)
    return lax.ppermute(value, axis, [(at, (at + steps) % count) for at in range(count)])


def swapped(value, axis, bit):
    count = lax.axis_size(axis)
    return lax.ppermute(value, axis, [(at, at ^ bit) for at in range(count)])


def total_over_devices(value, axis):
    bit = 1
    while bit < lax.axis_size(axis):
        value = value + swapped(value, axis, bit)
        bit *= 2
    return value


def local(initial, target, noise, w_qkv, w_out, gain, noise_scale, shifts):
    initial, noise = initial[0], noise[:, 0]

    def both_ways(part):
        shape = part.shape[:-3] + (TOK, C)
        first = part[..., :WIN, :].reshape(shape).astype(BF16)
        last = part[..., WIN:, :].reshape(shape).astype(BF16)
        return along(first, "tile", -1), along(last, "tile", 1)

    initial_sides = both_ways(initial)
    noise_sides = both_ways(noise)
    target_sides = both_ways(target)
    w_qkv_t, w_out_t = w_qkv.T, w_out.T
    gain_row, scale_row = gain[None], noise_scale[None]
    before, *saved0 = forward0(shifts, initial, *initial_sides, gain_row, w_qkv, w_out)
    final, sent, noise_here, *saved1 = forward1(
        shifts, before, noise, *noise_sides, gain_row, scale_row, w_qkv, w_out
    )
    far = swapped(sent, "member", 2)
    near = swapped(sent, "member", 1)
    far_near = swapped(far, "member", 1)
    d_one, head, gain_part, scale_part = backward1(
        shifts,
        final,
        (near, far, far_near),
        target,
        *target_sides,
        noise_here,
        saved1,
        gain_row,
        w_qkv_t,
        w_out_t,
    )
    own, tail, sums = backward0(
        shifts,
        d_one,
        along(head, "tile", -1),
        saved0,
        gain_row,
        gain_part,
        scale_part,
        w_qkv_t,
        w_out_t,
    )
    arrived = along(tail, "tile", 1)
    sums = total_over_devices(sums, "member")
    sums, arrived = lax.optimization_barrier((sums, arrived))
    column = jnp.arange(WIN)[None, :, None]
    first = jnp.where(
        column < shifts[0, 1], arrived.reshape(LAT, WIN, C).astype(F32), own[:, :WIN]
    )
    state_grad = jnp.concatenate([first, own[:, WIN:]], axis=1)[None]
    sums = total_over_devices(sums, "tile")
    members = lax.axis_size("member")
    factor = (members * LAT * initial.shape[1] * lax.axis_size("tile")) ** (-0.5)
    return (state_grad, sums[0] * factor, sums[1] * factor)


def solution(mesh):
    in_specs = (
        P("member", None, "tile", None),
        P(None, "tile", None),
        P(None, "member", None, "tile", None),
        P(),
        P(),
        P(),
        P(),
        P(),
    )
    out_specs = (P("member", None, "tile", None), P(), P())
    return jax.shard_map(local, mesh=mesh, in_specs=in_specs, out_specs=out_specs, check_vma=False)
```

time: 136 us -> 146 us (1.074); the launches traced: 136 us -> 144 us
  local copies, waits for them, and re-layouts: 1.92 us -> 33.9 us
  Pallas kernels: 40.7 us -> 19.3 us
  waiting for transfers between devices: 66.1 us -> 48 us
  starting transfers between devices: 22.1 us -> 38.9 us
    unnamed x18 -> x60, local copies, waits for them, and re-layouts: 0.05 us -> 31.5 us
    ppermute x4 -> x8, waiting for transfers between devices: 36.5 us -> 14.7 us  [along(): lax.ppermute(value, axis, [(at, (at + steps) % count) for at in range(cou...]
    ppermute x4 -> x8, starting transfers between devices: 8.73 us -> 25.3 us  [along(): lax.ppermute(value, axis, [(at, (at + steps) % count) for at in range(cou...]
    pallas_call x1 -> x2, Pallas kernels: 18 us -> 7.86 us  [the longest x1 3.93 us: forward0(): pl.pallas_call(forward0_kernel, out_shape=out_shape, in_specs=[smem()] +...]
    pallas_call x1, Pallas kernels: 11.6 us -> 5.24 us  [backward0(): pl.pallas_call(backward0_kernel, out_shape=[jax.ShapeDtypeStruct((LAT, 16...]
    pallas_call x1, Pallas kernels: 11.2 us -> 6.22 us  [backward1(): pl.pallas_call(backward1_kernel, out_shape=[jax.ShapeDtypeStruct((rows, C...]
    ppermute x11, waiting for transfers between devices: 29.6 us -> 33.4 us  [swapped(): return lax.ppermute(value, axis, [(at, at ^ bit) for at in range(count)])]
  transfers between devices with their start and end apart: 15 -> 19, of which waited for: 14 -> 13; matrix products, arithmetic and copies ran while one was open for 1% -> 11% of each run, Pallas kernels for 0% -> 3%
where the time goes in v1:
time: 146 us; the launch traced here: 144 us
  waiting for transfers between devices  48 us (33%)
  starting transfers between devices  38.9 us (27%)
  local copies, waits for them, and re-layouts  33.9 us (23%)
  Pallas kernels  19.3 us (13%)
  other arithmetic  3.34 us (2%)
    ppermute x11, waiting for transfers between devices, swapped(): return lax.ppermute(value, axis, [(at, at ^ bit) for at in range(count)])  33.4 us
    unnamed x60, local copies, waits for them, and re-layouts  31.5 us
    ppermute x8, starting transfers between devices, along(): lax.ppermute(value, axis, [(at, (at + steps) % count) for at in range(cou...  25.3 us
    ppermute x8, waiting for transfers between devices, along(): lax.ppermute(value, axis, [(at, (at + steps) % count) for at in range(cou...  14.7 us
    ppermute x11, starting transfers between devices, swapped(): return lax.ppermute(value, axis, [(at, at ^ bit) for at in range(count)])  13.6 us
    pallas_call x1, Pallas kernels, backward1(): pl.pallas_call(backward1_kernel, out_shape=[jax.ShapeDtypeStruct((rows, C...  6.22 us
    pallas_call x1, Pallas kernels, backward0(): pl.pallas_call(backward0_kernel, out_shape=[jax.ShapeDtypeStruct((LAT, 16...  5.24 us
    pallas_call x1, Pallas kernels, forward0(): pl.pallas_call(forward0_kernel, out_shape=out_shape, in_specs=[smem()] +...  3.93 us
  transfers between devices with their start and end apart: 19, of which 13 were waited for; matrix products, arithmetic and copies ran while one was open for 11% of the time, Pallas kernels for 3%

profile of v1, /device:TPU:32, one launch (start us, length us, event | category | flops | bytes accessed | tf_op | source)
XLA Modules:
  0.0 144.4 jit_solution(7394009956216226012)
XLA Ops:
  0.7 1.1 slice_bitcast_fusion
  1.8 5.0 %collective-permute-start.2 = (bf16[2,64,1024]{2,1,0:T(8,128)(2,1)S(1)}, bf16[2,64,1024]{2,1,0:T(8,128)(2,1)S(1)}, u32[]{:S(2)}, u32[]{:S(2)}) collective-permute-start(bf16[2,64,1024]{2,1,0:T(8,128)(2,1)S(1)} %get-tuple-element.48), channel_id=1, source_target_pairs={{0,63},{1,0},{2,1},{3,2},{4,3},{5,4},{6,5},{7,6},{8,7},{9,8},{10,9... | collective-permute-start | bytes 786440 | tf_op jit(solution)/shard_map/ppermute | solution.py:505
  6.8 1.1 bitcast_convert_fusion
  7.9 6.6 %collective-permute-start = (bf16[64,1024]{1,0:T(8,128)(2,1)S(1)}, bf16[64,1024]{1,0:T(8,128)(2,1)S(1)}, u32[]{:S(2)}, u32[]{:S(2)}) collective-permute-start(bf16[64,1024]{1,0:T(8,128)(2,1)S(1)} %get-tuple-element.52), channel_id=1, source_target_pairs={{0,63},{1,0},{2,1},{3,2},{4,3},{5,4},{6,5},{7,6},{8,7},{9,8},{10,9... | collective-permute-start | bytes 393224 | tf_op jit(solution)/shard_map/ppermute | solution.py:505
  14.5 5.6 %collective-permute-done.east = bf16[64,1024]{1,0:T(8,128)(2,1)S(1)} collective-permute-done((bf16[64,1024]{1,0:T(8,128)(2,1)S(1)}, bf16[64,1024]{1,0:T(8,128)(2,1)S(1)}, u32[]{:S(2)}, u32[]{:S(2)}) %collective-permute-start) | collective-permute-done | bytes 131104 | tf_op jit(solution)/shard_map/ppermute | solution.py:505
  20.1 3.9 %collective-permute-done.1.west = bf16[64,1024]{1,0:T(8,128)(2,1)S(1)} collective-permute-done((bf16[64,1024]{1,0:T(8,128)(2,1)S(1)}, bf16[64,1024]{1,0:T(8,128)(2,1)S(1)}, u32[]{:S(2)}, u32[]{:S(2)}) %collective-permute-start.1) | collective-permute-done | bytes 131104 | tf_op jit(solution)/shard_map/ppermute | solution.py:505
  24.0 2.8 %copy-done = bf16[1024,3072]{1,0:T(8,128)(2,1)S(1)} copy-done((bf16[1024,3072]{1,0:T(8,128)(2,1)S(1)}, bf16[1024,3072]{1,0:T(8,128)(2,1)}, u32[]{:S(2)}) %copy-start) | copy-done | bytes 6291480
  26.8 1.6 %copy-done.2 = bf16[1024,1024]{1,0:T(8,128)(2,1)S(1)} copy-done((bf16[1024,1024]{1,0:T(8,128)(2,1)S(1)}, bf16[1024,1024]{1,0:T(8,128)(2,1)}, u32[]{:S(2)}) %copy-start.2) | copy-done | bytes 2097176
  28.4 1.0 copy-done.3
  29.4 0.7 copy-done.20
  30.1 0.7 copy-done.26
  30.8 3.9 %forward0.1 = (f32[8,24,1024]{2,1,0:T(8,128)S(1)}, bf16[128,3072]{1,0:T(8,128)(2,1)S(1)}, bf16[16,64,256]{2,1,0:T(8,128)(2,1)S(1)}, f32[128,1024]{1,0:T(8,128)S(1)}, f32[128,128]{1,0:T(8,128)S(1)}) custom-call(s32[2,2]{1,0:T(2,128)S(1)} %copy-done.26, f32[8,16,1024]{2,1,0:T(8,128)S(1)} %bitcast.31, bf16[64,1024]{1,0:T(8,128)(2,1)S(1)} %collective-permute-done.east, ...), custom_call_target="tpu_custom_call" | custom-call | tf_op jit(solution)/shard_map/forward0/pallas_call | solution.py:243
  34.7 0.9 copy-done.8
  35.7 0.8 copy-done.16
  36.5 0.0 collective-permute-done.2.east
  36.6 3.9 %forward1.1 = (f32[128,1024]{1,0:T(8,128)S(1)}, bf16[128,1024]{1,0:T(8,128)(2,1)}, f32[2,128,1024]{2,1,0:T(8,128)S(1)}, bf16[128,3072]{1,0:T(8,128)(2,1)S(1)}, b...) custom-call(s32[2,2]{1,0:T(2,128)S(1)} %copy-done.26, ...), custom_call_target="tpu_custom_call" | custom-call | tf_op jit(solution)/shard_map/forward1/pallas_call | solution.py:267
  40.5 1.0 copy-done.6
  41.5 0.8 copy-done.10
  42.3 0.8 copy-done.12
  43.0 0.8 copy-done.14
  43.9 0.7 collective-permute-start.5
  44.6 0.1 collective-permute-start.4
  44.7 6.5 %collective-permute-done.5.far = bf16[128,1024]{1,0:T(8,128)(2,1)} collective-permute-done((bf16[128,1024]{1,0:T(8,128)(2,1)}, bf16[128,1024]{1,0:T(8,128)(2,1)}, u32[]{:S(2)}, u32[]{:S(2)}) %collective-permute-start.5) | collective-permute-done | bytes 262176 | tf_op jit(solution)/shard_map/ppermute | solution.py:510
  51.2 0.0 collective-permute-start.6
  51.2 0.7 slice_bitcast_fusion.2
  51.9 4.0 %collective-permute-start.7 = (bf16[64,1024]{1,0:T(8,128)(2,1)}, bf16[64,1024]{1,0:T(8,128)(2,1)S(1)}, u32[]{:S(2)}, u32[]{:S(2)}) collective-permute-start(bf16[64,1024]{1,0:T(8,128)(2,1)} %get-tuple-element.50), channel_id=1, source_target_pairs={{0,63},{1,0},{2,1},{3,2},{4,3},{5,4},{6,5},{7,6},{8,7},{9,8},{10,9... | collective-permute-start | bytes 393224 | tf_op jit(solution)/shard_map/ppermute | solution.py:505
  55.9 0.3 collective-permute-start.8
  56.2 8.7 %copy.11 = bf16[1024,3072]{0,1:T(8,128)(2,1)} copy(bf16[1024,3072]{1,0:T(8,128)(2,1)} %w_qkv.3) | data formatting | bytes 12582912 | tf_op args[3]
  64.8 2.9 %copy.12 = bf16[1024,1024]{0,1:T(8,128)(2,1)S(1)} copy(bf16[1024,1024]{1,0:T(8,128)(2,1)} %w_out.3) | data formatting | bytes 4194304 | tf_op args[4]
  67.7 0.0 collective-permute-done.7.east
  67.7 0.0 collective-permute-done.8.west
  67.7 0.0 collective-permute-done.6.far_near
  67.8 2.8 %copy-done.1 = bf16[1024,3072]{0,1:T(8,128)(2,1)S(1)} copy-done((bf16[1024,3072]{0,1:T(8,128)(2,1)S(1)}, bf16[1024,3072]{0,1:T(8,128)(2,1)}, u32[]{:S(2)}) %copy-start.1) | copy-done | bytes 6291480
  70.6 1.2 copy-done.7
  71.8 1.0 copy-done.11
  72.8 1.0 copy-done.13
  73.9 1.0 copy-done.15
  74.9 0.8 copy-done.25
  75.8 6.2 %backward1.1 = (f32[128,1024]{1,0:T(8,128)S(1)}, bf16[64,1024]{1,0:T(8,128)(2,1)S(1)}, f32[8,1024]{1,0:T(8,128)S(1)}, f32[8,1024]{1,0:T(8,128)S(1)}) custom-call(s32[2,2]{1,0:T(2,128)S(1)} %copy-done.27, f32[128,1024]{1,0:T(8,128)S(1)} %copy-done.11, bf16[128,1024]{1,0:T(8,128)(2,1)} %collective-permute-done.4.near, ...), custom_call_target="tpu_custom_call" | custom-call | tf_op jit(solution)/shard_map/backward1/pallas_call | solution.py:471
  82.0 6.6 %collective-permute-start.9 = (bf16[64,1024]{1,0:T(8,128)(2,1)S(1)}, bf16[64,1024]{1,0:T(8,128)(2,1)S(1)}, u32[]{:S(2)}, u32[]{:S(2)}) collective-permute-start(bf16[64,1024]{1,0:T(8,128)(2,1)S(1)} %get-tuple-element.33), channel_id=1, source_target_pairs={{0,63},{1,0},{2,1},{3,2},{4,3},{5,4},{6,5},{7,6},{8,7},{9,8},{10,9... | collective-permute-start | bytes 393224 | tf_op jit(solution)/shard_map/ppermute | solution.py:505
  88.6 2.9 %collective-permute-done.9.d_east = bf16[64,1024]{1,0:T(8,128)(2,1)S(1)} collective-permute-done((bf16[64,1024]{1,0:T(8,128)(2,1)S(1)}, bf16[64,1024]{1,0:T(8,128)(2,1)S(1)}, u32[]{:S(2)}, u32[]{:S(2)}) %collective-permute-start.9) | collective-permute-done | bytes 131104 | tf_op jit(solution)/shard_map/ppermute | solution.py:505
  91.4 5.2 %backward0.1 = (f32[8,16,1024]{2,1,0:T(8,128)S(1)}, bf16[64,1024]{1,0:T(8,128)(2,1)S(1)}, f32[2,1024]{1,0:T(2,128)S(1)}) custom-call(s32[2,2]{1,0:T(2,128)S(1)} %copy-done.27, f32[128,1024]{1,0:T(8,128)S(1)} %get-tuple-element.32.d_in, bf16[64,1024]{1,0:T(8,128)(2,1)S(1)} %collective-permute-done.9.d_east, bf16[128,3072]{1,0:T(8,128)(2,1)S(1)} %copy-done.9, ...), custom_call_target="tpu_custom_call" | custom-call | tf_op jit(solution)/shard_map/backward0/pallas_call | solution.py:488
  96.7 2.9 %collective-permute-start.12 = (bf16[64,1024]{1,0:T(8,128)(2,1)S(1)}, bf16[64,1024]{1,0:T(8,128)(2,1)S(1)}, u32[]{:S(2)}, u32[]{:S(2)}) collective-permute-start(bf16[64,1024]{1,0:T(8,128)(2,1)S(1)} %get-tuple-element.41), channel_id=1, source_target_pairs={{0,1},{1,2},{2,3},{3,4},{4,5},{5,6},{6,7},{7,8},{8,9},{9,10},{10,1... | collective-permute-start | bytes 393224 | tf_op jit(solution)/shard_map/ppermute | solution.py:505
  99.6 0.0 collective-permute-start.10
  99.6 1.2 collective-permute-done.10
  100.8 0.7 collective-permute-start.11
  101.4 3.0 %collective-permute-done.11 = f32[2,1024]{1,0:T(2,128)S(1)} collective-permute-done((f32[2,1024]{1,0:T(2,128)S(1)}, f32[2,1024]{1,0:T(2,128)S(1)}, u32[]{:S(2)}, u32[]{:S(2)}) %collective-permute-start.11) | collective-permute-done | bytes 8224 | tf_op jit(solution)/shard_map/ppermute | solution.py:510
  104.4 2.3 %collective-permute-done.12 = bf16[64,1024]{1,0:T(8,128)(2,1)S(1)} collective-permute-done((bf16[64,1024]{1,0:T(8,128)(2,1)S(1)}, bf16[64,1024]{1,0:T(8,128)(2,1)S(1)}, u32[]{:S(2)}, u32[]{:S(2)}) %collective-permute-start.12) | collective-permute-done | bytes 131104 | tf_op jit(solution)/shard_map/ppermute | solution.py:505
  106.7 0.0 collective-permute-start.13
  106.7 5.2 %collective-permute-done.13 = f32[2,1024]{1,0:T(2,128)S(1)} collective-permute-done((f32[2,1024]{1,0:T(2,128)S(1)}, f32[2,1024]{1,0:T(2,128)S(1)}, u32[]{:S(2)}, u32[]{:S(2)}) %collective-permute-start.13) | collective-permute-done | bytes 8224 | tf_op jit(solution)/shard_map/ppermute | solution.py:510
  111.9 0.0 collective-permute-start.14
  111.9 3.6 %collective-permute-done.14 = f32[2,1024]{1,0:T(2,128)S(1)} collective-permute-done((f32[2,1024]{1,0:T(2,128)S(1)}, f32[2,1024]{1,0:T(2,128)S(1)}, u32[]{:S(2)}, u32[]{:S(2)}) %collective-permute-start.14) | collective-permute-done | bytes 8224 | tf_op jit(solution)/shard_map/ppermute | solution.py:510
  115.5 2.4 %collective-permute-start.15 = (f32[2,1024]{1,0:T(2,128)S(1)}, f32[2,1024]{1,0:T(2,128)S(1)}, u32[]{:S(2)}, u32[]{:S(2)}) collective-permute-start(f32[2,1024]{1,0:T(2,128)S(1)} %add.27), channel_id=1, source_target_pairs={{0,4},{1,5},{2,6},{3,7},{4,0},{5,1},{6,2},{7,3},{8,12},{9,13},{10,... | collective-permute-start | bytes 24584 | tf_op jit(solution)/shard_map/ppermute | solution.py:510
  118.0 0.6 slice.37
  118.6 2.1 %collective-permute-done.15 = f32[2,1024]{1,0:T(2,128)S(1)} collective-permute-done((f32[2,1024]{1,0:T(2,128)S(1)}, f32[2,1024]{1,0:T(2,128)S(1)}, u32[]{:S(2)}, u32[]{:S(2)}) %collective-permute-start.15) | collective-permute-done | bytes 8224 | tf_op jit(solution)/shard_map/ppermute | solution.py:510
  120.7 9.4 %collective-permute-start.16 = (f32[2,1024]{1,0:T(2,128)S(1)}, f32[2,1024]{1,0:T(2,128)S(1)}, u32[]{:S(2)}, u32[]{:S(2)}) collective-permute-start(f32[2,1024]{1,0:T(2,128)S(1)} %add.28), channel_id=1, source_target_pairs={{0,8},{1,9},{2,10},{3,11},{4,12},{5,13},{6,14},{7,15},{8,0},{9,1},... | collective-permute-start | bytes 24584 | tf_op jit(solution)/shard_map/ppermute | solution.py:510
  130.1 0.6 iota_compare_fusion
  130.7 1.0 collective-permute-done.16
  131.7 0.1 convert_select_fusion
  131.8 4.5 %collective-permute-done.17 = f32[2,1024]{1,0:T(2,128)S(1)} collective-permute-done((f32[2,1024]{1,0:T(2,128)S(1)}, f32[2,1024]{1,0:T(2,128)S(1)}, u32[]{:S(2)}, u32[]{:S(2)}) %collective-permute-start.17) | collective-permute-done | bytes 8224 | tf_op jit(solution)/shard_map/ppermute | solution.py:510
  136.3 0.3 collective-permute-start.18
  136.6 0.8 maximum_bitcast_fusion
  137.4 6.4 %collective-permute-done.18 = f32[2,1024]{1,0:T(2,128)S(1)} collective-permute-done((f32[2,1024]{1,0:T(2,128)S(1)}, f32[2,1024]{1,0:T(2,128)S(1)}, u32[]{:S(2)}, u32[]{:S(2)}) %collective-permute-start.18) | collective-permute-done | bytes 8224 | tf_op jit(solution)/shard_map/ppermute | solution.py:510
  143.8 0.6 slice_multiply_fusion
  (56 shorter events, 0.2 us)
Async XLA Ops:
  0.6 35.9 %copy-start.4 = (bf16[2,1,8,16,1024]{4,3,2,1,0:T(8,128)(2,1)S(1)}, bf16[2,1,8,16,1024]{4,3,2,1,0:T(8,128)(2,1)}, u32[]{:S(2)}) copy-start(bf16[2,1,8,16,1024]{4,3,2,1,0:T(8,128)(2,1)} %param.10) | copy-start | bytes 1572868
  0.6 35.9 %copy-start.28 = (f32[1024]{0:T(1024)S(1)}, f32[1024]{0:T(1024)}, u32[]{:S(2)}) copy-start(f32[1024]{0:T(1024)} %param.14) | copy-start | bytes 12292
  1.8 34.7 %collective-permute-start.2 = (bf16[2,64,1024]{2,1,0:T(8,128)(2,1)S(1)}, bf16[2,64,1024]{2,1,0:T(8,128)(2,1)S(1)}, u32[]{:S(2)}, u32[]{:S(2)}) collective-permute-start(bf16[2,64,1024]{2,1,0:T(8,128)(2,1)S(1)} %get-tuple-element.48), channel_id=1, source_target_pairs={{0,63},{1,0},{2,1},{3,2},{4,3},{5,4},{6,5},{7,6},{8,7},{9,8},{10,9... | collective-permute-start | bytes 786440 | tf_op jit(solution)/shard_map/ppermute | solution.py:505
  6.8 29.7 %collective-permute-start.3 = (bf16[2,64,1024]{2,1,0:T(8,128)(2,1)S(1)}, bf16[2,64,1024]{2,1,0:T(8,128)(2,1)S(1)}, u32[]{:S(2)}, u32[]{:S(2)}) collective-permute-start(bf16[2,64,1024]{2,1,0:T(8,128)(2,1)S(1)} %get-tuple-element.47), channel_id=1, source_target_pairs={{0,1},{1,2},{2,3},{3,4},{4,5},{5,6},{6,7},{7,8},{8,9},{9,10},{10,1... | collective-permute-start | bytes 786440 | tf_op jit(solution)/shard_map/ppermute | solution.py:505
  7.9 12.2 %collective-permute-start = (bf16[64,1024]{1,0:T(8,128)(2,1)S(1)}, bf16[64,1024]{1,0:T(8,128)(2,1)S(1)}, u32[]{:S(2)}, u32[]{:S(2)}) collective-permute-start(bf16[64,1024]{1,0:T(8,128)(2,1)S(1)} %get-tuple-element.52), channel_id=1, source_target_pairs={{0,63},{1,0},{2,1},{3,2},{4,3},{5,4},{6,5},{7,6},{8,7},{9,8},{10,9... | collective-permute-start | bytes 393224 | tf_op jit(solution)/shard_map/ppermute | solution.py:505
  14.5 9.5 %collective-permute-start.1 = (bf16[64,1024]{1,0:T(8,128)(2,1)S(1)}, bf16[64,1024]{1,0:T(8,128)(2,1)S(1)}, u32[]{:S(2)}, u32[]{:S(2)}) collective-permute-start(bf16[64,1024]{1,0:T(8,128)(2,1)S(1)} %get-tuple-element.51), channel_id=1, source_target_pairs={{0,1},{1,2},{2,3},{3,4},{4,5},{5,6},{6,7},{7,8},{8,9},{9,10},{10,1... | collective-permute-start | bytes 393224 | tf_op jit(solution)/shard_map/ppermute | solution.py:505
  24.0 2.8 %copy-start = (bf16[1024,3072]{1,0:T(8,128)(2,1)S(1)}, bf16[1024,3072]{1,0:T(8,128)(2,1)}, u32[]{:S(2)}) copy-start(bf16[1024,3072]{1,0:T(8,128)(2,1)} %w_qkv.3) | copy-start | bytes 18874372
  26.8 1.6 %copy-start.2 = (bf16[1024,1024]{1,0:T(8,128)(2,1)S(1)}, bf16[1024,1024]{1,0:T(8,128)(2,1)}, u32[]{:S(2)}) copy-start(bf16[1024,1024]{1,0:T(8,128)(2,1)} %w_out.3) | copy-start | bytes 6291460
  28.4 1.0 copy-start.3
  29.4 0.7 copy-start.20
  30.1 0.7 copy-start.26
  34.7 0.9 copy-start.8
  35.7 0.8 copy-start.16
  36.5 4.0 %copy-start.18 = (f32[128,1024]{1,0:T(8,128)}, f32[128,1024]{1,0:T(8,128)S(1)}, u32[]{:S(2)}) copy-start(f32[128,1024]{1,0:T(8,128)S(1)} %get-tuple-element.36.scaled) | copy-start | bytes 1572868
  36.5 19.3 %copy-start.22 = (f32[128,128]{1,0:T(8,128)}, f32[128,128]{1,0:T(8,128)S(1)}, u32[]{:S(2)}) copy-start(f32[128,128]{1,0:T(8,128)S(1)} %get-tuple-element.37.spread) | copy-start | bytes 196612
  36.5 8.0 %copy-start.5 = (f32[8,16,1024]{2,1,0:T(8,128)S(1)}, f32[8,16,1024]{2,1,0:T(8,128)}, u32[]{:S(2)}) copy-start(f32[8,16,1024]{2,1,0:T(8,128)} %target.1) | copy-start | bytes 1572868
  40.5 1.0 copy-start.6
  41.5 0.8 copy-start.10
  42.3 0.8 copy-start.12
  43.0 0.8 copy-start.14
  43.9 12.0 %copy-start.24 = (f32[128,128]{1,0:T(8,128)}, f32[128,128]{1,0:T(8,128)S(1)}, u32[]{:S(2)}) copy-start(f32[128,128]{1,0:T(8,128)S(1)} %get-tuple-element.31.spread) | copy-start | bytes 196612
  43.9 7.3 %collective-permute-start.5 = (bf16[128,1024]{1,0:T(8,128)(2,1)}, bf16[128,1024]{1,0:T(8,128)(2,1)}, u32[]{:S(2)}, u32[]{:S(2)}) collective-permute-start(bf16[128,1024]{1,0:T(8,128)(2,1)} %get-tuple-element.26), channel_id=1, source_target_pairs={{0,128},{64,192},{128,0},{192,64},{1,129},{65,193},{129,1},{193,65... | collective-permute-start | bytes 786440 | tf_op jit(solution)/shard_map/ppermute | solution.py:510
  44.6 23.1 %collective-permute-start.4 = (bf16[128,1024]{1,0:T(8,128)(2,1)}, bf16[128,1024]{1,0:T(8,128)(2,1)}, u32[]{:S(2)}, u32[]{:S(2)}) collective-permute-start(bf16[128,1024]{1,0:T(8,128)(2,1)} %get-tuple-element.26), channel_id=1, source_target_pairs={{0,64},{64,0},{128,192},{192,128},{1,65},{65,1},{129,193},{193,129... | collective-permute-start | bytes 786440 | tf_op jit(solution)/shard_map/ppermute | solution.py:510
  51.2 16.6 %collective-permute-start.6 = (bf16[128,1024]{1,0:T(8,128)(2,1)}, bf16[128,1024]{1,0:T(8,128)(2,1)}, u32[]{:S(2)}, u32[]{:S(2)}) collective-permute-start(bf16[128,1024]{1,0:T(8,128)(2,1)} %collective-permute-done.5.far), channel_id=1, source_target_pairs={{0,64},{64,0},{128,192},{192,128},{1,65},{65,1},{129,193},{193,129... | collective-permute-start | bytes 786440 | tf_op jit(solution)/shard_map/ppermute | solution.py:510
  51.9 15.8 %collective-permute-start.7 = (bf16[64,1024]{1,0:T(8,128)(2,1)}, bf16[64,1024]{1,0:T(8,128)(2,1)S(1)}, u32[]{:S(2)}, u32[]{:S(2)}) collective-permute-start(bf16[64,1024]{1,0:T(8,128)(2,1)} %get-tuple-element.50), channel_id=1, source_target_pairs={{0,63},{1,0},{2,1},{3,2},{4,3},{5,4},{6,5},{7,6},{8,7},{9,8},{10,9... | collective-permute-start | bytes 393224 | tf_op jit(solution)/shard_map/ppermute | solution.py:505
  55.9 11.9 %copy-start.21 = (f32[1024]{0:T(1024)S(1)}, f32[1024]{0:T(1024)}, u32[]{:S(2)}) copy-start(f32[1024]{0:T(1024)} %param.13) | copy-start | bytes 12292
  55.9 11.9 %copy-start.27 = (s32[2,2]{1,0:T(2,128)S(1)}, s32[2,2]{1,0:T(2,128)}, u32[]{:S(2)}) copy-start(s32[2,2]{1,0:T(2,128)} %shifts.7) | copy-start | bytes 52
  55.9 11.8 %collective-permute-start.8 = (bf16[64,1024]{1,0:T(8,128)(2,1)}, bf16[64,1024]{1,0:T(8,128)(2,1)}, u32[]{:S(2)}, u32[]{:S(2)}) collective-permute-start(bf16[64,1024]{1,0:T(8,128)(2,1)} %get-tuple-element.49), channel_id=1, source_target_pairs={{0,1},{1,2},{2,3},{3,4},{4,5},{5,6},{6,7},{7,8},{8,9},{9,10},{10,1... | collective-permute-start | bytes 393224 | tf_op jit(solution)/shard_map/ppermute | solution.py:505
  67.8 2.8 %copy-start.1 = (bf16[1024,3072]{0,1:T(8,128)(2,1)S(1)}, bf16[1024,3072]{0,1:T(8,128)(2,1)}, u32[]{:S(2)}) copy-start(bf16[1024,3072]{0,1:T(8,128)(2,1)} %copy.11) | copy-start | bytes 18874372
  70.6 1.2 copy-start.7
  71.8 1.0 copy-start.11
  72.8 1.0 copy-start.13
  73.9 1.0 copy-start.15
  74.9 0.8 copy-start.25
  75.7 15.7 %copy-start.9 = (bf16[128,3072]{1,0:T(8,128)(2,1)S(1)}, bf16[128,3072]{1,0:T(8,128)(2,1)}, u32[]{:S(2)}) copy-start(bf16[128,3072]{1,0:T(8,128)(2,1)} %copy-done.8) | copy-start | bytes 2359300
  75.7 15.7 %copy-start.17 = (bf16[16,64,256]{2,1,0:T(8,128)(2,1)S(1)}, bf16[16,64,256]{2,1,0:T(8,128)(2,1)}, u32[]{:S(2)}) copy-start(bf16[16,64,256]{2,1,0:T(8,128)(2,1)} %copy-done.16) | copy-start | bytes 1572868
  75.8 15.7 %copy-start.19 = (f32[128,1024]{1,0:T(8,128)S(1)}, f32[128,1024]{1,0:T(8,128)}, u32[]{:S(2)}) copy-start(f32[128,1024]{1,0:T(8,128)} %copy-done.18) | copy-start | bytes 1572868
  75.8 15.7 %copy-start.23 = (f32[128,128]{1,0:T(8,128)S(1)}, f32[128,128]{1,0:T(8,128)}, u32[]{:S(2)}) copy-start(f32[128,128]{1,0:T(8,128)} %copy-done.22) | copy-start | bytes 196612
  82.0 9.4 %collective-permute-start.9 = (bf16[64,1024]{1,0:T(8,128)(2,1)S(1)}, bf16[64,1024]{1,0:T(8,128)(2,1)S(1)}, u32[]{:S(2)}, u32[]{:S(2)}) collective-permute-start(bf16[64,1024]{1,0:T(8,128)(2,1)S(1)} %get-tuple-element.33), channel_id=1, source_target_pairs={{0,63},{1,0},{2,1},{3,2},{4,3},{5,4},{6,5},{7,6},{8,7},{9,8},{10,9... | collective-permute-start | bytes 393224 | tf_op jit(solution)/shard_map/ppermute | solution.py:505
  96.7 10.0 %collective-permute-start.12 = (bf16[64,1024]{1,0:T(8,128)(2,1)S(1)}, bf16[64,1024]{1,0:T(8,128)(2,1)S(1)}, u32[]{:S(2)}, u32[]{:S(2)}) collective-permute-start(bf16[64,1024]{1,0:T(8,128)(2,1)S(1)} %get-tuple-element.41), channel_id=1, source_target_pairs={{0,1},{1,2},{2,3},{3,4},{4,5},{5,6},{6,7},{7,8},{8,9},{9,10},{10,1... | collective-permute-start | bytes 393224 | tf_op jit(solution)/shard_map/ppermute | solution.py:505
  99.6 1.2 collective-permute-start.10
  100.8 3.7 %collective-permute-start.11 = (f32[2,1024]{1,0:T(2,128)S(1)}, f32[2,1024]{1,0:T(2,128)S(1)}, u32[]{:S(2)}, u32[]{:S(2)}) collective-permute-start(f32[2,1024]{1,0:T(2,128)S(1)} %add.24), channel_id=1, source_target_pairs={{0,128},{64,192},{128,0},{192,64},{1,129},{65,193},{129,1},{193,65... | collective-permute-start | bytes 24584 | tf_op jit(solution)/shard_map/ppermute | solution.py:510
  106.7 5.2 %collective-permute-start.13 = (f32[2,1024]{1,0:T(2,128)S(1)}, f32[2,1024]{1,0:T(2,128)S(1)}, u32[]{:S(2)}, u32[]{:S(2)}) collective-permute-start(f32[2,1024]{1,0:T(2,128)S(1)} %add.25), channel_id=1, source_target_pairs={{0,1},{1,0},{2,3},{3,2},{4,5},{5,4},{6,7},{7,6},{8,9},{9,8},{10,11... | collective-permute-start | bytes 24584 | tf_op jit(solution)/shard_map/ppermute | solution.py:510
  111.9 3.7 %collective-permute-start.14 = (f32[2,1024]{1,0:T(2,128)S(1)}, f32[2,1024]{1,0:T(2,128)S(1)}, u32[]{:S(2)}, u32[]{:S(2)}) collective-permute-start(f32[2,1024]{1,0:T(2,128)S(1)} %add.26), channel_id=1, source_target_pairs={{0,2},{1,3},{2,0},{3,1},{4,6},{5,7},{6,4},{7,5},{8,10},{9,11},{10,... | collective-permute-start | bytes 24584 | tf_op jit(solution)/shard_map/ppermute | solution.py:510
  115.5 5.2 %collective-permute-start.15 = (f32[2,1024]{1,0:T(2,128)S(1)}, f32[2,1024]{1,0:T(2,128)S(1)}, u32[]{:S(2)}, u32[]{:S(2)}) collective-permute-start(f32[2,1024]{1,0:T(2,128)S(1)} %add.27), channel_id=1, source_target_pairs={{0,4},{1,5},{2,6},{3,7},{4,0},{5,1},{6,2},{7,3},{8,12},{9,13},{10,... | collective-permute-start | bytes 24584 | tf_op jit(solution)/shard_map/ppermute | solution.py:510
  120.7 11.0 %collective-permute-start.16 = (f32[2,1024]{1,0:T(2,128)S(1)}, f32[2,1024]{1,0:T(2,128)S(1)}, u32[]{:S(2)}, u32[]{:S(2)}) collective-permute-start(f32[2,1024]{1,0:T(2,128)S(1)} %add.28), channel_id=1, source_target_pairs={{0,8},{1,9},{2,10},{3,11},{4,12},{5,13},{6,14},{7,15},{8,0},{9,1},... | collective-permute-start | bytes 24584 | tf_op jit(solution)/shard_map/ppermute | solution.py:510
  131.7 4.6 %collective-permute-start.17 = (f32[2,1024]{1,0:T(2,128)S(1)}, f32[2,1024]{1,0:T(2,128)S(1)}, u32[]{:S(2)}, u32[]{:S(2)}) collective-permute-start(f32[2,1024]{1,0:T(2,128)S(1)} %add.29), channel_id=1, source_target_pairs={{0,16},{1,17},{2,18},{3,19},{4,20},{5,21},{6,22},{7,23},{8,24},{9,... | collective-permute-start | bytes 24584 | tf_op jit(solution)/shard_map/ppermute | solution.py:510
  136.3 7.6 %collective-permute-start.18 = (f32[2,1024]{1,0:T(2,128)S(1)}, f32[2,1024]{1,0:T(2,128)S(1)}, u32[]{:S(2)}, u32[]{:S(2)}) collective-permute-start(f32[2,1024]{1,0:T(2,128)S(1)} %add.30), channel_id=1, source_target_pairs={{0,32},{1,33},{2,34},{3,35},{4,36},{5,37},{6,38},{7,39},{8,40},{9,... | collective-permute-start | bytes 24584 | tf_op jit(solution)/shard_map/ppermute | solution.py:510

commit v2 on v1

--- a/solution.py
+++ b/solution.py
@@ -20,7 +20,7 @@
 SMOOTH = 0.25
 F32 = jnp.float32
 BF16 = jnp.bfloat16
-VMEM_LIMIT = 16 * 1024 * 1024
+VMEM_LIMIT = 28 * 1024 * 1024
 
 
 def dot(left, right):
@@ -83,7 +83,7 @@
         scaled = offset * spread
         normed_ref[at : at + 32, :] = (scaled * gain).astype(BF16)
         if at >= saved_from:
-            scaled_ref[at - saved_from : at - saved_from + 32, :] = scaled
+            scaled_ref[at - saved_from : at - saved_from + 32, :] = scaled.astype(BF16)
             spread_ref[at - saved_from : at - saved_from + 32, :] = jnp.broadcast_to(
                 spread, (32, 128)
             )
@@ -119,37 +119,78 @@
     return slice(start, start + WIN)
 
 
+def start_copies(sems, first, pairs):
+    copies = []
+    for at, (source, destination) in enumerate(pairs):
+        copy = pltpu.make_async_copy(source, destination, sems.at[first + at])
+        copy.start()
+        copies.append(copy)
+    return copies
+
+
+def wait_all(copies):
+    for copy in copies:
+        copy.wait()
+
+
+def column_parts(source, destination, parts):
+    width = source.shape[1] // parts
+    return [
+        (source.at[:, pl.ds(at * width, width)], destination.at[:, pl.ds(at * width, width)])
+        for at in range(parts)
+    ]
+
+
 def forward0_kernel(
-    shifts,
-    initial,
+    initial_hbm,
+    shifts_hbm,
+    gain_hbm,
+    w_qkv_hbm,
+    w_out_hbm,
     east,
     west,
+    following_out,
+    packed_hbm,
+    weights_hbm,
+    scaled_hbm,
+    spread_hbm,
+    initial,
+    shifts,
     gain,
     w_qkv,
     w_out,
-    following_out,
-    packed_out,
-    weights_out,
-    scaled_out,
-    spread_out,
     ext,
     state,
     normed,
     packed,
     mixed,
+    weights,
+    scaled,
+    spread,
+    sems,
 ):
+    small = start_copies(
+        sems, 0, [(shifts_hbm, shifts), (initial_hbm, initial), (gain_hbm, gain)]
+    )
+    parts = start_copies(sems, 3, column_parts(w_qkv_hbm, w_qkv, 6))
+    late = start_copies(sems, 9, [(w_out_hbm, w_out)])
+    wait_all(small)
     lat_shift, lon_shift = shifts[0, 0], shifts[0, 1]
     fill(ext, initial, west[...].astype(F32), east[...].astype(F32))
     for row in range(LAT):
         part = frame(ext, row, lon_shift, 24)
         for window in range(3):
             state[window_rows(window, row), :] = part[window * WIN : (window + 1) * WIN]
-    norm_rows(state, 3 * TOK, gain[...], normed, scaled_out, spread_out, TOK)
+    norm_rows(state, 3 * TOK, gain[...], normed, scaled, spread, TOK)
+    saves = start_copies(sems, 10, [(scaled, scaled_hbm), (spread, spread_hbm)])
     for part in range(6):
         at = slice(part * 512, (part + 1) * 512)
+        parts[part].wait()
         packed[:, at] = dot(normed[...], w_qkv[:, at]).astype(BF16)
-    packed_out[...] = packed[TOK:, :]
-    attend(3, packed, weights_out, mixed, lat_shift, 1)
+    saves += start_copies(sems, 12, [(packed.at[pl.ds(TOK, 2 * TOK)], packed_hbm)])
+    attend(3, packed, weights, mixed, lat_shift, 1)
+    saves += start_copies(sems, 13, [(weights, weights_hbm)])
+    wait_all(late)
     for part in range(4):
         at = slice(part * 256, (part + 1) * 256)
         following = state[:, at] + dot(mixed[...], w_out[:, at])
@@ -158,30 +199,52 @@
                 following_out[row, window * WIN : (window + 1) * WIN, at] = following[
                     window_rows(window, row)
                 ]
+    wait_all(saves)
 
 
 def forward1_kernel(
-    shifts,
+    noise_hbm,
+    shifts_hbm,
+    gain_hbm,
+    scale_hbm,
+    w_qkv_hbm,
+    w_out_hbm,
     before,
-    noise,
     east,
     west,
+    sent_out,
+    final_hbm,
+    noise_out_hbm,
+    packed_hbm,
+    weights_hbm,
+    scaled_hbm,
+    spread_hbm,
+    noise,
+    shifts,
     gain,
     noise_scale,
     w_qkv,
     w_out,
-    final_out,
-    sent_out,
-    noise_out,
-    packed_out,
-    weights_out,
-    scaled_out,
-    spread_out,
     ext,
     state,
+    final,
+    noise_here,
     normed,
+    packed,
     mixed,
+    weights,
+    scaled,
+    spread,
+    sems,
 ):
+    small = start_copies(
+        sems,
+        0,
+        [(shifts_hbm, shifts), (noise_hbm, noise), (gain_hbm, gain), (scale_hbm, noise_scale)],
+    )
+    parts = start_copies(sems, 4, column_parts(w_qkv_hbm, w_qkv, 6))
+    late = start_copies(sems, 10, [(w_out_hbm, w_out)])
+    wait_all(small)
     lat_shift = shifts[1, 0]
     lon0, origin1 = shifts[0, 1], origin(shifts)
     scale = noise_scale[...]
@@ -189,25 +252,34 @@
         fill(ext, noise.at[step], west[step].astype(F32), east[step].astype(F32))
         for row in range(LAT):
             part = frame(ext, row, origin1 + WIN, 16)
-            fields = frame(before, row, origin1 - lon0 + WIN, 16)
+            if step == 0:
+                fields = frame(before, row, origin1 - lon0 + WIN, 16)
             for window in range(2):
                 rows = window_rows(window, row)
                 here = part[window * WIN : (window + 1) * WIN]
                 if step == 0:
                     state[rows, :] = fields[window * WIN : (window + 1) * WIN] + scale * here
                 else:
-                    final_out[rows, :] = state[rows, :] + scale * here
-                noise_out[step, rows, :] = here
-    norm_rows(state, 2 * TOK, gain[...], normed, scaled_out, spread_out, 0)
+                    final[rows, :] = state[rows, :] + scale * here
+                noise_here[step, rows, :] = here
+    saves = start_copies(sems, 11, [(noise_here, noise_out_hbm)])
+    norm_rows(state, 2 * TOK, gain[...], normed, scaled, spread, 0)
+    saves += start_copies(sems, 12, [(scaled, scaled_hbm), (spread, spread_hbm)])
     for part in range(6):
         at = slice(part * 512, (part + 1) * 512)
-        packed_out[:, at] = dot(normed[...], w_qkv[:, at]).astype(BF16)
-    attend(2, packed_out, weights_out, mixed, lat_shift, 0)
+        parts[part].wait()
+        packed[:, at] = dot(normed[...], w_qkv[:, at]).astype(BF16)
+    saves += start_copies(sems, 14, [(packed, packed_hbm)])
+    attend(2, packed, weights, mixed, lat_shift, 0)
+    saves += start_copies(sems, 15, [(weights, weights_hbm)])
+    wait_all(late)
     for part in range(4):
         at = slice(part * 256, (part + 1) * 256)
-        final = final_out[:, at] + dot(mixed[...], w_out[:, at])
-        final_out[:, at] = final
-        sent_out[:, at] = final.astype(BF16)
+        last = final[:, at] + dot(mixed[...], w_out[:, at])
+        final[:, at] = last
+        sent_out[:, at] = last.astype(BF16)
+    saves += start_copies(sems, 16, [(final, final_hbm)])
+    wait_all(saves)
 
 
 def origin(shifts):
@@ -219,65 +291,109 @@
     return pl.BlockSpec(memory_space=pltpu.VMEM)
 
 
-def smem():
-    return pl.BlockSpec(memory_space=pltpu.SMEM)
+def hbm():
+    return pl.BlockSpec(memory_space=pltpu.HBM)
 
 
 def compiler_params():
     return pltpu.CompilerParams(vmem_limit_bytes=VMEM_LIMIT)
 
 
-def saved_shapes():
-    rows = 2 * TOK
-    return [
-        jax.ShapeDtypeStruct((rows, 3 * C), BF16),
-        jax.ShapeDtypeStruct((2 * GROUPS, TOK, SPAN), BF16),
-        jax.ShapeDtypeStruct((rows, C), F32),
-        jax.ShapeDtypeStruct((rows, 128), F32),
-    ]
+ROWS = 2 * TOK
+SAVED = [
+    ((ROWS, 3 * C), BF16),
+    ((2 * GROUPS, TOK, SPAN), BF16),
+    ((ROWS, C), BF16),
+    ((ROWS, 128), F32),
+]
+
+
+def shapes(entries):
+    return [jax.ShapeDtypeStruct(shape, dtype) for shape, dtype in entries]
+
+
+def buffers(entries):
+    return [pltpu.VMEM(shape, dtype) for shape, dtype in entries]
+
+
+WEIGHTS = [((C, 3 * C), BF16), ((C, C), BF16)]
 
 
 def forward0(shifts, initial, east, west, gain, w_qkv, w_out):
     rows = 3 * TOK
-    out_shape = [jax.ShapeDtypeStruct((LAT, 24, C), F32)] + saved_shapes()
     return pl.pallas_call(
         forward0_kernel,
-        out_shape=out_shape,
-        in_specs=[smem()] + [vmem()] * 6,
-        out_specs=[vmem()] * len(out_shape),
+        out_shape=shapes([((LAT, 24, C), F32)] + SAVED),
+        in_specs=[hbm()] * 5 + [vmem()] * 2,
+        out_specs=[vmem()] + [hbm()] * 4,
         scratch_shapes=[
-            pltpu.VMEM((LAT, 32, C), F32),
-            pltpu.VMEM((rows, C), F32),
-            pltpu.VMEM((rows, C), BF16),
-            pltpu.VMEM((rows, 3 * C), BF16),
-            pltpu.VMEM((rows, C), BF16),
-        ],
+            pltpu.VMEM((LAT, 16, C), F32),
+            pltpu.SMEM((2, 2), jnp.int32),
+            pltpu.VMEM((1, C), F32),
+        ]
+        + buffers(WEIGHTS)
+        + buffers(
+            [
+                ((LAT, 32, C), F32),
+                ((rows, C), F32),
+                ((rows, C), BF16),
+                ((rows, 3 * C), BF16),
+                ((rows, C), BF16),
+            ]
+        )
+        + buffers(SAVED[1:])
+        + [pltpu.SemaphoreType.DMA((14,))],
         compiler_params=compiler_params(),
         name="forward0",
-    )(shifts, initial, east, west, gain, w_qkv, w_out)
+    )(initial, shifts, gain, w_qkv, w_out, east, west)
 
 
 def forward1(shifts, before, noise, east, west, gain, noise_scale, w_qkv, w_out):
-    rows = 2 * TOK
-    out_shape = [
-        jax.ShapeDtypeStruct((rows, C), F32),
-        jax.ShapeDtypeStruct((rows, C), BF16),
-        jax.ShapeDtypeStruct((2, rows, C), F32),
-    ] + saved_shapes()
     return pl.pallas_call(
         forward1_kernel,
-        out_shape=out_shape,
-        in_specs=[smem()] + [vmem()] * 8,
-        out_specs=[vmem()] * len(out_shape),
+        out_shape=shapes([((ROWS, C), BF16), ((ROWS, C), F32), ((2, ROWS, C), F32)] + SAVED),
+        in_specs=[hbm()] * 6 + [vmem()] * 3,
+        out_specs=[vmem()] + [hbm()] * 6,
         scratch_shapes=[
-            pltpu.VMEM((LAT, 32, C), F32),
-            pltpu.VMEM((rows, C), F32),
-            pltpu.VMEM((rows, C), BF16),
-            pltpu.VMEM((rows, C), BF16),
-        ],
+            pltpu.VMEM((2, LAT, 16, C), BF16),
+            pltpu.SMEM((2, 2), jnp.int32),
+            pltpu.VMEM((1, C), F32),
+            pltpu.VMEM((1, C), F32),
+        ]
+        + buffers(WEIGHTS)
+        + buffers(
+            [
+                ((LAT, 32, C), F32),
+                ((ROWS, C), F32),
+                ((ROWS, C), F32),
+                ((2, ROWS, C), F32),
+                ((ROWS, C), BF16),
+                ((ROWS, 3 * C), BF16),
+                ((ROWS, C), BF16),
+            ]
+        )
+        + buffers(SAVED[1:])
+        + [pltpu.SemaphoreType.DMA((17,))],
         compiler_params=compiler_params(),
         name="forward1",
-    )(shifts, before, noise, east, west, gain, noise_scale, w_qkv, w_out)
+    )(noise, shifts, gain, noise_scale, w_qkv, w_out, before, east, west)
+
+
+def transpose_kernel(source, out):
+    out[...] = source[...].T
+
+
+def transposed(matrix):
+    columns = matrix.shape[1]
+    return pl.pallas_call(
+        transpose_kernel,
+        grid=(columns // 256,),
+        out_shape=jax.ShapeDtypeStruct((columns, C), BF16),
+        in_specs=[pl.BlockSpec((C, 256), lambda at: (0, at))],
+        out_specs=pl.BlockSpec((256, C), lambda at: (at, 0)),
+        compiler_params=compiler_params(),
+        name="transposed",
+    )(matrix)
 
 
 def attend_back(packed, weights_ref, d_mixed, d_packed):
@@ -312,21 +428,26 @@
 
 
 def step_back(
-    d_next, packed, weights, w_qkv_t, w_out_t, d_mixed, d_packed, d_normed
+    copies, d_next, packed, weights, w_qkv_t, w_out_t, d_mixed, d_packed, d_normed
 ):
+    out_t, packed_copy, weights_copy, *qkv_t = copies
+    out_t.wait()
     d_branch = d_next[...].astype(BF16)
     for part in range(4):
         at = slice(part * 256, (part + 1) * 256)
         d_mixed[:, at] = dot(d_branch, w_out_t[:, at]).astype(BF16)
+    packed_copy.wait()
+    weights_copy.wait()
     attend_back(packed, weights, d_mixed, d_packed)
     for part in range(4):
         at = slice(part * 256, (part + 1) * 256)
+        qkv_t[part].wait()
         d_normed[:, at] = dot(d_packed[...], w_qkv_t[:, at])
 
 
 def norm_back(at, d_next, scaled_ref, spread_ref, d_normed, gain):
     rows = slice(at, at + 32)
-    scaled = scaled_ref[rows, :]
+    scaled = scaled_ref[rows, :].astype(F32)
     d_here = d_normed[rows, :]
     d_hat = d_here * gain
     spread = spread_ref[rows, 0:1]
@@ -346,39 +467,77 @@
 
 
 def backward1_kernel(
+    shifts_hbm,
+    final_hbm,
+    near_hbm,
+    far_hbm,
+    far_near_hbm,
+    target_hbm,
+    gain_hbm,
+    noise_hbm,
+    w_out_t_hbm,
+    packed_hbm,
+    weights_hbm,
+    scaled_hbm,
+    spread_hbm,
+    w_qkv_t_hbm,
+    east,
+    west,
+    d_out,
+    head_out,
+    gain_out,
+    scale_out,
     shifts,
     final,
     near,
     far,
     far_near,
     target,
-    east,
-    west,
+    gain,
     noise,
+    w_out_t,
     packed,
     weights,
     scaled,
     spread,
-    gain,
     w_qkv_t,
-    w_out_t,
-    d_out,
-    head_out,
-    gain_out,
-    scale_out,
     ext,
     d_next,
     d_mixed,
     d_packed,
     d_normed,
+    sems,
 ):
+    early = start_copies(
+        sems,
+        0,
+        [
+            (shifts_hbm, shifts),
+            (target_hbm, target),
+            (final_hbm, final),
+            (near_hbm, near),
+            (far_hbm, far),
+            (far_near_hbm, far_near),
+            (noise_hbm, noise),
+        ],
+    )
+    copies = start_copies(
+        sems,
+        7,
+        [(w_out_t_hbm, w_out_t), (packed_hbm, packed), (weights_hbm, weights)]
+        + column_parts(w_qkv_t_hbm, w_qkv_t, 4),
+    )
+    late = start_copies(
+        sems, 14, [(scaled_hbm, scaled), (spread_hbm, spread), (gain_hbm, gain)]
+    )
+    wait_all(early)
     fill(ext, target, west[...].astype(F32), east[...].astype(F32))
     for row in range(LAT):
         part = frame(ext, row, origin(shifts) + WIN, 16)
         for window in range(2):
             d_normed[window_rows(window, row), :] = part[window * WIN : (window + 1) * WIN]
     scale_total = jnp.zeros((8, C), F32)
-    for at in range(0, 2 * TOK, 32):
+    for at in range(0, ROWS, 32):
         rows = slice(at, at + 32)
         here = final[rows, :]
         pairs = (
@@ -389,9 +548,10 @@
         seed = slope(here - d_normed[rows, :]) - pairs * (1.0 / 3.0)
         d_next[rows, :] = seed
         scale_total = scale_total + eight_rows(seed * noise[1, rows, :])
-    step_back(d_next, packed, weights, w_qkv_t, w_out_t, d_mixed, d_packed, d_normed)
+    step_back(copies, d_next, packed, weights, w_qkv_t, w_out_t, d_mixed, d_packed, d_normed)
+    wait_all(late)
     gain_total = jnp.zeros((8, C), F32)
-    for at in range(0, 2 * TOK, 32):
+    for at in range(0, ROWS, 32):
         rows = slice(at, at + 32)
         d_here, gain_part = norm_back(at, d_next, scaled, spread, d_normed, gain[...])
         d_out[rows, :] = d_here
@@ -404,27 +564,45 @@
 
 
 def backward0_kernel(
-    shifts,
+    shifts_hbm,
+    gain_hbm,
+    w_out_t_hbm,
+    packed_hbm,
+    weights_hbm,
+    scaled_hbm,
+    spread_hbm,
+    w_qkv_t_hbm,
     d_in,
     d_east,
+    gain_in,
+    scale_in,
+    own_out,
+    tail_out,
+    sums_out,
+    shifts,
+    gain,
+    w_out_t,
     packed,
     weights,
     scaled,
     spread,
-    gain,
-    gain_in,
-    scale_in,
     w_qkv_t,
-    w_out_t,
-    own_out,
-    tail_out,
-    sums_out,
     ext,
     d_next,
     d_mixed,
     d_packed,
     d_normed,
+    sems,
 ):
+    early = start_copies(sems, 0, [(shifts_hbm, shifts)])
+    copies = start_copies(
+        sems,
+        1,
+        [(w_out_t_hbm, w_out_t), (packed_hbm, packed), (weights_hbm, weights)]
+        + column_parts(w_qkv_t_hbm, w_qkv_t, 4),
+    )
+    late = start_copies(sems, 8, [(scaled_hbm, scaled), (spread_hbm, spread), (gain_hbm, gain)])
+    wait_all(early)
     lon0, origin1 = shifts[0, 1], origin(shifts)
     east = d_east[...].astype(F32)
     for row in range(LAT):
@@ -435,9 +613,10 @@
         part = frame(ext, row, lon0 - origin1, 16)
         for window in range(2):
             d_next[window_rows(window, row), :] = part[window * WIN : (window + 1) * WIN]
-    step_back(d_next, packed, weights, w_qkv_t, w_out_t, d_mixed, d_packed, d_normed)
+    step_back(copies, d_next, packed, weights, w_qkv_t, w_out_t, d_mixed, d_packed, d_normed)
+    wait_all(late)
     gain_total = gain_in[...]
-    for at in range(0, 2 * TOK, 32):
+    for at in range(0, ROWS, 32):
         d_here, gain_part = norm_back(at, d_next, scaled, spread, d_normed, gain[...])
         gain_total = gain_total + gain_part
         for piece in range(4):
@@ -455,49 +634,52 @@
     tail_out[...] = jnp.concatenate(tails, axis=0).astype(BF16)
 
 
-def backward_scratch():
-    rows = 2 * TOK
-    return [
-        pltpu.VMEM((LAT, 32, C), F32),
-        pltpu.VMEM((rows, C), F32),
-        pltpu.VMEM((rows, C), BF16),
-        pltpu.VMEM((rows, 3 * C), BF16),
-        pltpu.VMEM((rows, C), F32),
+WORK = [
+    ((LAT, 32, C), F32),
+    ((ROWS, C), F32),
+    ((ROWS, C), BF16),
+    ((ROWS, 3 * C), BF16),
+    ((ROWS, C), F32),
+]
+SUMS = [((8, C), F32)] * 2
+
+
+def backward1(shifts, final, others, target, east, west, noise, saved, gain, w_qkv_t, w_out_t):
+    held = [
+        ((ROWS, C), F32),
+        ((ROWS, C), BF16),
+        ((ROWS, C), BF16),
+        ((ROWS, C), BF16),
+        ((LAT, 16, C), F32),
+        ((1, C), F32),
+        ((2, ROWS, C), F32),
+        ((C, C), BF16),
     ]
-
-
-def backward1(shifts, final, others, target, east, west, noise, saved, gain, w_qkv_t, w_out_t):
-    rows = 2 * TOK
     return pl.pallas_call(
         backward1_kernel,
-        out_shape=[
-            jax.ShapeDtypeStruct((rows, C), F32),
-            jax.ShapeDtypeStruct((TOK, C), BF16),
-            jax.ShapeDtypeStruct((8, C), F32),
-            jax.ShapeDtypeStruct((8, C), F32),
-        ],
-        in_specs=[smem()] + [vmem()] * 15,
+        out_shape=shapes([((ROWS, C), F32), ((TOK, C), BF16)] + SUMS),
+        in_specs=[hbm()] * 14 + [vmem()] * 2,
         out_specs=[vmem()] * 4,
-        scratch_shapes=backward_scratch(),
+        scratch_shapes=[pltpu.SMEM((2, 2), jnp.int32)]
+        + buffers(held + SAVED + [((3 * C, C), BF16)] + WORK)
+        + [pltpu.SemaphoreType.DMA((17,))],
         compiler_params=compiler_params(),
         name="backward1",
-    )(shifts, final, *others, target, east, west, noise, *saved, gain, w_qkv_t, w_out_t)
+    )(shifts, final, *others, target, gain, noise, w_out_t, *saved, w_qkv_t, east, west)
 
 
 def backward0(shifts, d_in, d_east, saved, gain, gain_in, scale_in, w_qkv_t, w_out_t):
     return pl.pallas_call(
         backward0_kernel,
-        out_shape=[
-            jax.ShapeDtypeStruct((LAT, 16, C), F32),
-            jax.ShapeDtypeStruct((TOK, C), BF16),
-            jax.ShapeDtypeStruct((2, C), F32),
-        ],
-        in_specs=[smem()] + [vmem()] * 11,
+        out_shape=shapes([((LAT, 16, C), F32), ((TOK, C), BF16), ((2, C), F32)]),
+        in_specs=[hbm()] * 8 + [vmem()] * 4,
         out_specs=[vmem()] * 3,
-        scratch_shapes=backward_scratch(),
+        scratch_shapes=[pltpu.SMEM((2, 2), jnp.int32), pltpu.VMEM((1, C), F32)]
+        + buffers([((C, C), BF16)] + SAVED + [((3 * C, C), BF16)] + WORK)
+        + [pltpu.SemaphoreType.DMA((11,))],
         compiler_params=compiler_params(),
         name="backward0",
-    )(shifts, d_in, d_east, *saved, gain, gain_in, scale_in, w_qkv_t, w_out_t)
+    )(shifts, gain, w_out_t, *saved, w_qkv_t, d_in, d_east, gain_in, scale_in)
 
 
 def along(value, axis, steps):
@@ -529,11 +711,13 @@
 
     initial_sides = both_ways(initial)
     noise_sides = both_ways(noise)
-    target_sides = both_ways(target)
-    w_qkv_t, w_out_t = w_qkv.T, w_out.T
+    w_qkv_t, w_out_t = transposed(w_qkv), transposed(w_out)
+    initial_sides, w_qkv_t, w_out_t = lax.optimization_barrier((initial_sides, w_qkv_t, w_out_t))
     gain_row, scale_row = gain[None], noise_scale[None]
     before, *saved0 = forward0(shifts, initial, *initial_sides, gain_row, w_qkv, w_out)
-    final, sent, noise_here, *saved1 = forward1(
+    noise_sides, target_now = lax.optimization_barrier((noise_sides, target))
+    target_sides = both_ways(target_now)
+    sent, final, noise_here, *saved1 = forward1(
         shifts, before, noise, *noise_sides, gain_row, scale_row, w_qkv, w_out
     )
     far = swapped(sent, "member", 2)

time: 146 us -> 130 us (0.89)
  local copies, waits for them, and re-layouts: 33.9 us -> 4.51 us
  Pallas kernels: 19.3 us -> 32.2 us
  waiting for transfers between devices: 48 us -> 55 us
  starting transfers between devices: 38.9 us -> 32.9 us
    unnamed x60 -> x18, local copies, waits for them, and re-layouts: 31.5 us -> 2.82 us
    pallas_call x4 -> x6, Pallas kernels: 19.3 us -> 32.2 us  [the longest x1 8.3 us: backward1(): pl.pallas_call(backward1_kernel, out_shape=shapes([((ROWS, C), F32), ((TO...]
    ppermute x8, starting transfers between devices: 25.3 us -> 18.9 us  [along(): lax.ppermute(value, axis, [(at, (at + steps) % count) for at in range(cou...]
    ppermute x8, waiting for transfers between devices: 14.7 us -> 21 us  [along(): lax.ppermute(value, axis, [(at, (at + steps) % count) for at in range(cou...]
  transfers between devices with their start and end apart: 19 -> 19, of which waited for: 13 -> 14; matrix products, arithmetic and copies ran while one was open for 11% -> 3% of each run, Pallas kernels for 3% -> 8%
where the time goes in v2:
time: 130 us; the launch traced here: 129 us
  waiting for transfers between devices  55 us (42%)
  starting transfers between devices  32.9 us (25%)
  Pallas kernels  32.2 us (25%)
  local copies, waits for them, and re-layouts  4.51 us (3%)
  other arithmetic  3.32 us (3%)
    ppermute x11, waiting for transfers between devices, swapped(): return lax.ppermute(value, axis, [(at, at ^ bit) for at in range(count)])  34 us
    ppermute x8, waiting for transfers between devices, along(): lax.ppermute(value, axis, [(at, (at + steps) % count) for at in range(cou...  21 us
    ppermute x8, starting transfers between devices, along(): lax.ppermute(value, axis, [(at, (at + steps) % count) for at in range(cou...  18.9 us
    ppermute x11, starting transfers between devices, swapped(): return lax.ppermute(value, axis, [(at, at ^ bit) for at in range(count)])  14.1 us
    pallas_call x1, Pallas kernels, backward1(): pl.pallas_call(backward1_kernel, out_shape=shapes([((ROWS, C), F32), ((TO...  8.3 us
    pallas_call x1, Pallas kernels, backward0(): pl.pallas_call(backward0_kernel, out_shape=shapes([((LAT, 16, C), F32), (...  7.74 us
    pallas_call x1, Pallas kernels, forward0(): pl.pallas_call(forward0_kernel, out_shape=shapes([((LAT, 24, C), F32)] +...  6.04 us
    pallas_call x1, Pallas kernels, forward1(): pl.pallas_call(forward1_kernel, out_shape=shapes([((ROWS, C), BF16), ((RO...  5.67 us
  transfers between devices with their start and end apart: 19, of which 14 were waited for; matrix products, arithmetic and copies ran while one was open for 3% of the time, Pallas kernels for 8%

profile of v2, /device:TPU:32, one launch (start us, length us, event | category | flops | bytes accessed | tf_op | source)
XLA Modules:
  0.0 128.8 jit_solution(7968225163693638358)
XLA Ops:
  0.6 1.1 slice_bitcast_fusion
  1.7 5.0 %collective-permute-start.2 = (bf16[2,64,1024]{2,1,0:T(8,128)(2,1)S(1)}, bf16[2,64,1024]{2,1,0:T(8,128)(2,1)S(1)}, u32[]{:S(2)}, u32[]{:S(2)}) collective-permute-start(bf16[2,64,1024]{2,1,0:T(8,128)(2,1)S(1)} %get-tuple-element.62), channel_id=1, source_target_pairs={{0,63},{1,0},{2,1},{3,2},{4,3},{5,4},{6,5},{7,6},{8,7},{9,8},{10,9... | collective-permute-start | bytes 786440 | tf_op jit(solution)/shard_map/ppermute | solution.py:687
  6.7 0.0 collective-permute-start.3
  6.7 1.1 bitcast_convert_fusion
  7.8 6.6 %collective-permute-start = (bf16[64,1024]{1,0:T(8,128)(2,1)S(1)}, bf16[64,1024]{1,0:T(8,128)(2,1)S(1)}, u32[]{:S(2)}, u32[]{:S(2)}) collective-permute-start(bf16[64,1024]{1,0:T(8,128)(2,1)S(1)} %get-tuple-element.66), channel_id=1, source_target_pairs={{0,63},{1,0},{2,1},{3,2},{4,3},{5,4},{6,5},{7,6},{8,7},{9,8},{10,9... | collective-permute-start | bytes 393224 | tf_op jit(solution)/shard_map/ppermute | solution.py:687
  14.4 0.0 collective-permute-start.1
  14.4 2.8 %copy-done = bf16[1024,3072]{1,0:T(8,128)(2,1)S(1)} copy-done((bf16[1024,3072]{1,0:T(8,128)(2,1)S(1)}, bf16[1024,3072]{1,0:T(8,128)(2,1)}, u32[]{:S(2)}) %copy-start) | copy-done | bytes 6291480
  17.2 0.0 copy-start.7
  17.2 3.3 %transposed.2.w_qkv_t_hbm = bf16[3072,1024]{1,0:T(8,128)(2,1)S(1)} custom-call(bf16[1024,3072]{1,0:T(8,128)(2,1)S(1)} %copy-done), custom_call_target="tpu_custom_call" | custom-call | tf_op jit(solution)/shard_map/transposed/pallas_call | solution.py:388
  20.6 0.0 copy-done.2
  20.6 0.0 copy-start.4
  20.6 0.0 copy-start.8
  20.6 1.1 transposed.3.w_out_t_hbm
  21.7 0.0 collective-permute-done.east
  21.7 2.2 %collective-permute-done.1.west = bf16[64,1024]{1,0:T(8,128)(2,1)S(1)} collective-permute-done((bf16[64,1024]{1,0:T(8,128)(2,1)S(1)}, bf16[64,1024]{1,0:T(8,128)(2,1)S(1)}, u32[]{:S(2)}, u32[]{:S(2)}) %collective-permute-start.1) | collective-permute-done | bytes 131104 | tf_op jit(solution)/shard_map/ppermute | solution.py:687
  23.9 0.0 copy-done.1
  23.9 0.0 copy-done.3
  23.9 0.0 copy-done.6
  23.9 0.0 copy-done.7
  23.9 6.0 %forward0.1 = (f32[8,24,1024]{2,1,0:T(8,128)S(1)}, bf16[128,3072]{1,0:T(8,128)(2,1)S(1)}, bf16[16,64,256]{2,1,0:T(8,128)(2,1)S(1)}, bf16[128,1024]{1,0:T(8,128)(2,1)S(1)}, f32[128,128]{1,0:T(8,128)S(1)}) custom-call(f32[8,16,1024]{2,1,0:T(8,128)S(1)} %bitcast.25, s32[2,2]{1,0:T(2,128)S(1)} %copy-done.7, f32[1,1024]{1,0:T(1,128)S(1)} %bitcast.28, ...), custom_call_target="tpu_custom_call" | custom-call | tf_op jit(solution)/shard_map/forward0/pallas_call | solution.py:324
  30.0 0.0 copy-start.5
  30.0 0.0 collective-permute-done.2.east
  30.0 0.0 collective-permute-done.3.west
  30.0 0.0 copy-done.4
  30.0 0.0 copy-done.8
  30.0 5.7 %forward1.1 = (bf16[128,1024]{1,0:T(8,128)(2,1)S(1)}, f32[128,1024]{1,0:T(8,128)S(1)}, f32[2,128,1024]{2,1,0:T(8,128)S(1)}, bf16[128,3072]{1,0:T(8,128)(2,1)S(1)...) custom-call(bf16[2,8,16,1024]{3,2,1,0:T(8,128)(2,1)S(1)} %bitcast.27, ...), custom_call_target="tpu_custom_call" | custom-call | tf_op jit(solution)/shard_map/forward1/pallas_call | solution.py:352
  35.7 0.8 collective-permute-start.5
  36.5 0.0 collective-permute-start.4
  36.5 0.0 copy-done.5
  36.5 6.3 %collective-permute-done.5.far_hbm = bf16[128,1024]{1,0:T(8,128)(2,1)S(1)} collective-permute-done((bf16[128,1024]{1,0:T(8,128)(2,1)S(1)}, bf16[128,1024]{1,0:T(8,128)(2,1)S(1)}, u32[]{:S(2)}, u32[]{:S(2)}) %collective-permute-start.5) | collective-permute-done | bytes 262176 | tf_op jit(solution)/shard_map/ppermute | solution.py:692
  42.8 0.0 collective-permute-start.6
  42.8 4.4 %collective-permute-start.7 = (bf16[64,1024]{1,0:T(8,128)(2,1)S(1)}, bf16[64,1024]{1,0:T(8,128)(2,1)S(1)}, u32[]{:S(2)}, u32[]{:S(2)}) collective-permute-start(bf16[64,1024]{1,0:T(8,128)(2,1)S(1)} %get-tuple-element.64), channel_id=1, source_target_pairs={{0,63},{1,0},{2,1},{3,2},{4,3},{5,4},{6,5},{7,6},{8,7},{9,8},{10,9... | collective-permute-start | bytes 393224 | tf_op jit(solution)/shard_map/ppermute | solution.py:687
  47.2 0.0 collective-permute-start.8
  47.2 3.8 %collective-permute-done.7.east = bf16[64,1024]{1,0:T(8,128)(2,1)S(1)} collective-permute-done((bf16[64,1024]{1,0:T(8,128)(2,1)S(1)}, bf16[64,1024]{1,0:T(8,128)(2,1)S(1)}, u32[]{:S(2)}, u32[]{:S(2)}) %collective-permute-start.7) | collective-permute-done | bytes 131104 | tf_op jit(solution)/shard_map/ppermute | solution.py:687
  51.1 6.3 %collective-permute-done.8.west = bf16[64,1024]{1,0:T(8,128)(2,1)S(1)} collective-permute-done((bf16[64,1024]{1,0:T(8,128)(2,1)S(1)}, bf16[64,1024]{1,0:T(8,128)(2,1)S(1)}, u32[]{:S(2)}, u32[]{:S(2)}) %collective-permute-start.8) | collective-permute-done | bytes 131104 | tf_op jit(solution)/shard_map/ppermute | solution.py:687
  57.4 0.0 collective-permute-done.4.near_hbm
  57.4 0.0 collective-permute-done.6.far_near_hbm
  57.4 8.3 %backward1.1 = (f32[128,1024]{1,0:T(8,128)S(1)}, bf16[64,1024]{1,0:T(8,128)(2,1)S(1)}, f32[8,1024]{1,0:T(8,128)S(1)}, f32[8,1024]{1,0:T(8,128)S(1)}) custom-call(s32[2,2]{1,0:T(2,128)S(1)} %copy-done.7, f32[128,1024]{1,0:T(8,128)S(1)} %get-tuple-element.42.final_hbm, bf16[128,1024]{1,0:T(8,128)(2,1)S(1)} %collective-permute-done.4.near_hbm, ...), custom_call_target="tpu_custom_call" | custom-call | tf_op jit(solution)/shard_map/backward1/pallas_call | solution.py:658
  65.7 1.6 %collective-permute-start.9 = (bf16[64,1024]{1,0:T(8,128)(2,1)S(1)}, bf16[64,1024]{1,0:T(8,128)(2,1)S(1)}, u32[]{:S(2)}, u32[]{:S(2)}) collective-permute-start(bf16[64,1024]{1,0:T(8,128)(2,1)S(1)} %get-tuple-element.51), channel_id=1, source_target_pairs={{0,63},{1,0},{2,1},{3,2},{4,3},{5,4},{6,5},{7,6},{8,7},{9,8},{10,9... | collective-permute-start | bytes 393224 | tf_op jit(solution)/shard_map/ppermute | solution.py:687
  67.3 5.2 %collective-permute-done.9.d_east = bf16[64,1024]{1,0:T(8,128)(2,1)S(1)} collective-permute-done((bf16[64,1024]{1,0:T(8,128)(2,1)S(1)}, bf16[64,1024]{1,0:T(8,128)(2,1)S(1)}, u32[]{:S(2)}, u32[]{:S(2)}) %collective-permute-start.9) | collective-permute-done | bytes 131104 | tf_op jit(solution)/shard_map/ppermute | solution.py:687
  72.4 7.7 %backward0.1 = (f32[8,16,1024]{2,1,0:T(8,128)S(1)}, bf16[64,1024]{1,0:T(8,128)(2,1)S(1)}, f32[2,1024]{1,0:T(2,128)S(1)}) custom-call(s32[2,2]{1,0:T(2,128)S(1)} %copy-done.7, f32[1,1024]{1,0:T(1,128)S(1)} %bitcast.31, bf16[1024,1024]{1,0:T(8,128)(2,1)S(1)} %transposed.3.w_out_t_hbm, bf16[128,3072]{1,0:T(8,128)(2,1)S(1)} %get-tuple-element.34.packed_hbm, ...), custom_call_target="tpu_custom_call" | custom-call | tf_op jit(solution)/shard_map/backward0/pallas_call | solution.py:672
  80.2 1.2 collective-permute-start.12
  81.4 0.0 collective-permute-start.10
  81.4 1.2 collective-permute-done.10
  82.6 0.8 collective-permute-start.11
  83.4 2.9 %collective-permute-done.11 = f32[2,1024]{1,0:T(2,128)S(1)} collective-permute-done((f32[2,1024]{1,0:T(2,128)S(1)}, f32[2,1024]{1,0:T(2,128)S(1)}, u32[]{:S(2)}, u32[]{:S(2)}) %collective-permute-start.11) | collective-permute-done | bytes 8224 | tf_op jit(solution)/shard_map/ppermute | solution.py:692
  86.2 3.5 %collective-permute-done.12 = bf16[64,1024]{1,0:T(8,128)(2,1)S(1)} collective-permute-done((bf16[64,1024]{1,0:T(8,128)(2,1)S(1)}, bf16[64,1024]{1,0:T(8,128)(2,1)S(1)}, u32[]{:S(2)}, u32[]{:S(2)}) %collective-permute-start.12) | collective-permute-done | bytes 131104 | tf_op jit(solution)/shard_map/ppermute | solution.py:687
  89.7 0.0 collective-permute-start.13
  89.7 5.2 %collective-permute-done.13 = f32[2,1024]{1,0:T(2,128)S(1)} collective-permute-done((f32[2,1024]{1,0:T(2,128)S(1)}, f32[2,1024]{1,0:T(2,128)S(1)}, u32[]{:S(2)}, u32[]{:S(2)}) %collective-permute-start.13) | collective-permute-done | bytes 8224 | tf_op jit(solution)/shard_map/ppermute | solution.py:692
  94.9 0.0 collective-permute-start.14
  94.9 3.6 %collective-permute-done.14 = f32[2,1024]{1,0:T(2,128)S(1)} collective-permute-done((f32[2,1024]{1,0:T(2,128)S(1)}, f32[2,1024]{1,0:T(2,128)S(1)}, u32[]{:S(2)}, u32[]{:S(2)}) %collective-permute-start.14) | collective-permute-done | bytes 8224 | tf_op jit(solution)/shard_map/ppermute | solution.py:692
  98.6 0.4 collective-permute-start.15
  98.9 0.6 slice.37
  99.5 4.2 %collective-permute-done.15 = f32[2,1024]{1,0:T(2,128)S(1)} collective-permute-done((f32[2,1024]{1,0:T(2,128)S(1)}, f32[2,1024]{1,0:T(2,128)S(1)}, u32[]{:S(2)}, u32[]{:S(2)}) %collective-permute-start.15) | collective-permute-done | bytes 8224 | tf_op jit(solution)/shard_map/ppermute | solution.py:692
  103.7 10.7 %collective-permute-start.16 = (f32[2,1024]{1,0:T(2,128)S(1)}, f32[2,1024]{1,0:T(2,128)S(1)}, u32[]{:S(2)}, u32[]{:S(2)}) collective-permute-start(f32[2,1024]{1,0:T(2,128)S(1)} %add.28), channel_id=1, source_target_pairs={{0,8},{1,9},{2,10},{3,11},{4,12},{5,13},{6,14},{7,15},{8,0},{9,1},... | collective-permute-start | bytes 24584 | tf_op jit(solution)/shard_map/ppermute | solution.py:692
  114.4 0.6 iota_compare_fusion
  115.1 1.0 collective-permute-done.16
  116.1 0.0 collective-permute-start.17
  116.1 0.1 convert_select_fusion
  116.2 4.4 %collective-permute-done.17 = f32[2,1024]{1,0:T(2,128)S(1)} collective-permute-done((f32[2,1024]{1,0:T(2,128)S(1)}, f32[2,1024]{1,0:T(2,128)S(1)}, u32[]{:S(2)}, u32[]{:S(2)}) %collective-permute-start.17) | collective-permute-done | bytes 8224 | tf_op jit(solution)/shard_map/ppermute | solution.py:692
  120.6 1.4 %collective-permute-start.18 = (f32[2,1024]{1,0:T(2,128)S(1)}, f32[2,1024]{1,0:T(2,128)S(1)}, u32[]{:S(2)}, u32[]{:S(2)}) collective-permute-start(f32[2,1024]{1,0:T(2,128)S(1)} %add.30), channel_id=1, source_target_pairs={{0,32},{1,33},{2,34},{3,35},{4,36},{5,37},{6,38},{7,39},{8,40},{9,... | collective-permute-start | bytes 24584 | tf_op jit(solution)/shard_map/ppermute | solution.py:692
  122.0 0.8 maximum_bitcast_fusion
  122.9 5.3 %collective-permute-done.18 = f32[2,1024]{1,0:T(2,128)S(1)} collective-permute-done((f32[2,1024]{1,0:T(2,128)S(1)}, f32[2,1024]{1,0:T(2,128)S(1)}, u32[]{:S(2)}, u32[]{:S(2)}) %collective-permute-start.18) | collective-permute-done | bytes 8224 | tf_op jit(solution)/shard_map/ppermute | solution.py:692
  128.2 0.6 slice_multiply_fusion
  (16 shorter events, 0.1 us)
Async XLA Ops:
  1.7 28.3 %collective-permute-start.2 = (bf16[2,64,1024]{2,1,0:T(8,128)(2,1)S(1)}, bf16[2,64,1024]{2,1,0:T(8,128)(2,1)S(1)}, u32[]{:S(2)}, u32[]{:S(2)}) collective-permute-start(bf16[2,64,1024]{2,1,0:T(8,128)(2,1)S(1)} %get-tuple-element.62), channel_id=1, source_target_pairs={{0,63},{1,0},{2,1},{3,2},{4,3},{5,4},{6,5},{7,6},{8,7},{9,8},{10,9... | collective-permute-start | bytes 786440 | tf_op jit(solution)/shard_map/ppermute | solution.py:687
  6.7 23.3 %collective-permute-start.3 = (bf16[2,64,1024]{2,1,0:T(8,128)(2,1)S(1)}, bf16[2,64,1024]{2,1,0:T(8,128)(2,1)S(1)}, u32[]{:S(2)}, u32[]{:S(2)}) collective-permute-start(bf16[2,64,1024]{2,1,0:T(8,128)(2,1)S(1)} %get-tuple-element.61), channel_id=1, source_target_pairs={{0,1},{1,2},{2,3},{3,4},{4,5},{5,6},{6,7},{7,8},{8,9},{9,10},{10,1... | collective-permute-start | bytes 786440 | tf_op jit(solution)/shard_map/ppermute | solution.py:687
  7.8 13.9 %collective-permute-start = (bf16[64,1024]{1,0:T(8,128)(2,1)S(1)}, bf16[64,1024]{1,0:T(8,128)(2,1)S(1)}, u32[]{:S(2)}, u32[]{:S(2)}) collective-permute-start(bf16[64,1024]{1,0:T(8,128)(2,1)S(1)} %get-tuple-element.66), channel_id=1, source_target_pairs={{0,63},{1,0},{2,1},{3,2},{4,3},{5,4},{6,5},{7,6},{8,7},{9,8},{10,9... | collective-permute-start | bytes 393224 | tf_op jit(solution)/shard_map/ppermute | solution.py:687
  14.4 9.5 %collective-permute-start.1 = (bf16[64,1024]{1,0:T(8,128)(2,1)S(1)}, bf16[64,1024]{1,0:T(8,128)(2,1)S(1)}, u32[]{:S(2)}, u32[]{:S(2)}) collective-permute-start(bf16[64,1024]{1,0:T(8,128)(2,1)S(1)} %get-tuple-element.65), channel_id=1, source_target_pairs={{0,1},{1,2},{2,3},{3,4},{4,5},{5,6},{6,7},{7,8},{8,9},{9,10},{10,1... | collective-permute-start | bytes 393224 | tf_op jit(solution)/shard_map/ppermute | solution.py:687
  14.4 2.8 %copy-start = (bf16[1024,3072]{1,0:T(8,128)(2,1)S(1)}, bf16[1024,3072]{1,0:T(8,128)(2,1)}, u32[]{:S(2)}) copy-start(bf16[1024,3072]{1,0:T(8,128)(2,1)} %w_qkv_hbm.3) | copy-start | bytes 18874372
  17.2 3.3 %copy-start.2 = (bf16[1024,1024]{1,0:T(8,128)(2,1)S(1)}, bf16[1024,1024]{1,0:T(8,128)(2,1)}, u32[]{:S(2)}) copy-start(bf16[1024,1024]{1,0:T(8,128)(2,1)} %w_out_hbm.3) | copy-start | bytes 6291460
  17.2 6.7 %copy-start.1 = (bf16[1024,3072]{1,0:T(8,128)(2,1)S(1)}, bf16[1024,3072]{1,0:T(8,128)(2,1)}, u32[]{:S(2)}) copy-start(bf16[1024,3072]{1,0:T(8,128)(2,1)} %w_qkv_hbm.3) | copy-start | bytes 18874372
  17.2 6.7 %copy-start.3 = (f32[1,8,16,1024]{3,2,1,0:T(8,128)S(1)}, f32[1,8,16,1024]{3,2,1,0:T(8,128)}, u32[]{:S(2)}) copy-start(f32[1,8,16,1024]{3,2,1,0:T(8,128)} %param.8) | copy-start | bytes 1572868
  17.2 6.7 %copy-start.6 = (f32[1024]{0:T(1024)S(1)}, f32[1024]{0:T(1024)}, u32[]{:S(2)}) copy-start(f32[1024]{0:T(1024)} %param.13) | copy-start | bytes 12292
  17.2 6.7 %copy-start.7 = (s32[2,2]{1,0:T(2,128)S(1)}, s32[2,2]{1,0:T(2,128)}, u32[]{:S(2)}) copy-start(s32[2,2]{1,0:T(2,128)} %shifts_hbm.7) | copy-start | bytes 52
  20.6 9.5 %copy-start.4 = (bf16[2,1,8,16,1024]{4,3,2,1,0:T(8,128)(2,1)S(1)}, bf16[2,1,8,16,1024]{4,3,2,1,0:T(8,128)(2,1)}, u32[]{:S(2)}) copy-start(bf16[2,1,8,16,1024]{4,3,2,1,0:T(8,128)(2,1)} %param.10) | copy-start | bytes 1572868
  20.6 9.5 %copy-start.8 = (f32[1024]{0:T(1024)S(1)}, f32[1024]{0:T(1024)}, u32[]{:S(2)}) copy-start(f32[1024]{0:T(1024)} %param.14) | copy-start | bytes 12292
  30.0 6.5 %copy-start.5 = (f32[8,16,1024]{2,1,0:T(8,128)S(1)}, f32[8,16,1024]{2,1,0:T(8,128)}, u32[]{:S(2)}) copy-start(f32[8,16,1024]{2,1,0:T(8,128)} %target_hbm.1) | copy-start | bytes 1572868
  35.7 7.1 %collective-permute-start.5 = (bf16[128,1024]{1,0:T(8,128)(2,1)S(1)}, bf16[128,1024]{1,0:T(8,128)(2,1)S(1)}, u32[]{:S(2)}, u32[]{:S(2)}) collective-permute-start(bf16[128,1024]{1,0:T(8,128)(2,1)S(1)} %get-tuple-element.43), channel_id=1, source_target_pairs={{0,128},{64,192},{128,0},{192,64},{1,129},{65,193},{129,1},{193,65... | collective-permute-start | bytes 786440 | tf_op jit(solution)/shard_map/ppermute | solution.py:692
  36.5 20.9 %collective-permute-start.4 = (bf16[128,1024]{1,0:T(8,128)(2,1)S(1)}, bf16[128,1024]{1,0:T(8,128)(2,1)S(1)}, u32[]{:S(2)}, u32[]{:S(2)}) collective-permute-start(bf16[128,1024]{1,0:T(8,128)(2,1)S(1)} %get-tuple-element.43), channel_id=1, source_target_pairs={{0,64},{64,0},{128,192},{192,128},{1,65},{65,1},{129,193},{193,129... | collective-permute-start | bytes 786440 | tf_op jit(solution)/shard_map/ppermute | solution.py:692
  42.8 14.6 %collective-permute-start.6 = (bf16[128,1024]{1,0:T(8,128)(2,1)S(1)}, bf16[128,1024]{1,0:T(8,128)(2,1)S(1)}, u32[]{:S(2)}, u32[]{:S(2)}) collective-permute-start(bf16[128,1024]{1,0:T(8,128)(2,1)S(1)} %collective-permute-done.5.far_hbm), channel_id=1, source_target_pairs={{0,64},{64,0},{128,192},{192,128},{1,65},{65,1},{129,193},{193,129... | collective-permute-start | bytes 786440 | tf_op jit(solution)/shard_map/ppermute | solution.py:692
  42.8 8.2 %collective-permute-start.7 = (bf16[64,1024]{1,0:T(8,128)(2,1)S(1)}, bf16[64,1024]{1,0:T(8,128)(2,1)S(1)}, u32[]{:S(2)}, u32[]{:S(2)}) collective-permute-start(bf16[64,1024]{1,0:T(8,128)(2,1)S(1)} %get-tuple-element.64), channel_id=1, source_target_pairs={{0,63},{1,0},{2,1},{3,2},{4,3},{5,4},{6,5},{7,6},{8,7},{9,8},{10,9... | collective-permute-start | bytes 393224 | tf_op jit(solution)/shard_map/ppermute | solution.py:687
  47.2 10.1 %collective-permute-start.8 = (bf16[64,1024]{1,0:T(8,128)(2,1)S(1)}, bf16[64,1024]{1,0:T(8,128)(2,1)S(1)}, u32[]{:S(2)}, u32[]{:S(2)}) collective-permute-start(bf16[64,1024]{1,0:T(8,128)(2,1)S(1)} %get-tuple-element.63), channel_id=1, source_target_pairs={{0,1},{1,2},{2,3},{3,4},{4,5},{5,6},{6,7},{7,8},{8,9},{9,10},{10,1... | collective-permute-start | bytes 393224 | tf_op jit(solution)/shard_map/ppermute | solution.py:687
  65.7 6.8 %collective-permute-start.9 = (bf16[64,1024]{1,0:T(8,128)(2,1)S(1)}, bf16[64,1024]{1,0:T(8,128)(2,1)S(1)}, u32[]{:S(2)}, u32[]{:S(2)}) collective-permute-start(bf16[64,1024]{1,0:T(8,128)(2,1)S(1)} %get-tuple-element.51), channel_id=1, source_target_pairs={{0,63},{1,0},{2,1},{3,2},{4,3},{5,4},{6,5},{7,6},{8,7},{9,8},{10,9... | collective-permute-start | bytes 393224 | tf_op jit(solution)/shard_map/ppermute | solution.py:687
  80.2 9.6 %collective-permute-start.12 = (bf16[64,1024]{1,0:T(8,128)(2,1)S(1)}, bf16[64,1024]{1,0:T(8,128)(2,1)S(1)}, u32[]{:S(2)}, u32[]{:S(2)}) collective-permute-start(bf16[64,1024]{1,0:T(8,128)(2,1)S(1)} %get-tuple-element.55), channel_id=1, source_target_pairs={{0,1},{1,2},{2,3},{3,4},{4,5},{5,6},{6,7},{7,8},{8,9},{9,10},{10,1... | collective-permute-start | bytes 393224 | tf_op jit(solution)/shard_map/ppermute | solution.py:687
  81.4 1.2 collective-permute-start.10
  82.6 3.7 %collective-permute-start.11 = (f32[2,1024]{1,0:T(2,128)S(1)}, f32[2,1024]{1,0:T(2,128)S(1)}, u32[]{:S(2)}, u32[]{:S(2)}) collective-permute-start(f32[2,1024]{1,0:T(2,128)S(1)} %add.24), channel_id=1, source_target_pairs={{0,128},{64,192},{128,0},{192,64},{1,129},{65,193},{129,1},{193,65... | collective-permute-start | bytes 24584 | tf_op jit(solution)/shard_map/ppermute | solution.py:692
  89.7 5.2 %collective-permute-start.13 = (f32[2,1024]{1,0:T(2,128)S(1)}, f32[2,1024]{1,0:T(2,128)S(1)}, u32[]{:S(2)}, u32[]{:S(2)}) collective-permute-start(f32[2,1024]{1,0:T(2,128)S(1)} %add.25), channel_id=1, source_target_pairs={{0,1},{1,0},{2,3},{3,2},{4,5},{5,4},{6,7},{7,6},{8,9},{9,8},{10,11... | collective-permute-start | bytes 24584 | tf_op jit(solution)/shard_map/ppermute | solution.py:692
  94.9 3.7 %collective-permute-start.14 = (f32[2,1024]{1,0:T(2,128)S(1)}, f32[2,1024]{1,0:T(2,128)S(1)}, u32[]{:S(2)}, u32[]{:S(2)}) collective-permute-start(f32[2,1024]{1,0:T(2,128)S(1)} %add.26), channel_id=1, source_target_pairs={{0,2},{1,3},{2,0},{3,1},{4,6},{5,7},{6,4},{7,5},{8,10},{9,11},{10,... | collective-permute-start | bytes 24584 | tf_op jit(solution)/shard_map/ppermute | solution.py:692
  98.6 5.2 %collective-permute-start.15 = (f32[2,1024]{1,0:T(2,128)S(1)}, f32[2,1024]{1,0:T(2,128)S(1)}, u32[]{:S(2)}, u32[]{:S(2)}) collective-permute-start(f32[2,1024]{1,0:T(2,128)S(1)} %add.27), channel_id=1, source_target_pairs={{0,4},{1,5},{2,6},{3,7},{4,0},{5,1},{6,2},{7,3},{8,12},{9,13},{10,... | collective-permute-start | bytes 24584 | tf_op jit(solution)/shard_map/ppermute | solution.py:692
  103.7 12.3 %collective-permute-start.16 = (f32[2,1024]{1,0:T(2,128)S(1)}, f32[2,1024]{1,0:T(2,128)S(1)}, u32[]{:S(2)}, u32[]{:S(2)}) collective-permute-start(f32[2,1024]{1,0:T(2,128)S(1)} %add.28), channel_id=1, source_target_pairs={{0,8},{1,9},{2,10},{3,11},{4,12},{5,13},{6,14},{7,15},{8,0},{9,1},... | collective-permute-start | bytes 24584 | tf_op jit(solution)/shard_map/ppermute | solution.py:692
  116.1 4.5 %collective-permute-start.17 = (f32[2,1024]{1,0:T(2,128)S(1)}, f32[2,1024]{1,0:T(2,128)S(1)}, u32[]{:S(2)}, u32[]{:S(2)}) collective-permute-start(f32[2,1024]{1,0:T(2,128)S(1)} %add.29), channel_id=1, source_target_pairs={{0,16},{1,17},{2,18},{3,19},{4,20},{5,21},{6,22},{7,23},{8,24},{9,... | collective-permute-start | bytes 24584 | tf_op jit(solution)/shard_map/ppermute | solution.py:692
  120.6 7.6 %collective-permute-start.18 = (f32[2,1024]{1,0:T(2,128)S(1)}, f32[2,1024]{1,0:T(2,128)S(1)}, u32[]{:S(2)}, u32[]{:S(2)}) collective-permute-start(f32[2,1024]{1,0:T(2,128)S(1)} %add.30), channel_id=1, source_target_pairs={{0,32},{1,33},{2,34},{3,35},{4,36},{5,37},{6,38},{7,39},{8,40},{9,... | collective-permute-start | bytes 24584 | tf_op jit(solution)/shard_map/ppermute | solution.py:692

commit v3 on v2

--- a/solution.py
+++ b/solution.py
@@ -5,6 +5,7 @@
 from jax import lax
 from jax.experimental import pallas as pl
 from jax.experimental.pallas import tpu as pltpu
+from jax.sharding import Mesh
 from jax.sharding import PartitionSpec as P
 
 C = 1024
@@ -20,7 +21,7 @@
 SMOOTH = 0.25
 F32 = jnp.float32
 BF16 = jnp.bfloat16
-VMEM_LIMIT = 28 * 1024 * 1024
+VMEM_LIMIT = 14 * 1024 * 1024
 
 
 def dot(left, right):
@@ -62,11 +63,17 @@
     return pl.ds(pl.multiple_of(start, 128), size)
 
 
-def fill(ext, own_ref, west, east):
+def fill(ext, own_ref, side, start):
+    columns = side.shape[0] // LAT
     for row in range(LAT):
-        ext[row, 0:8, :] = west[row * WIN : (row + 1) * WIN]
-        ext[row, 8:24, :] = own_ref[row].astype(F32)
-        ext[row, 24:32, :] = east[row * WIN : (row + 1) * WIN]
+        ext[row, start : start + 16, :] = own_ref[row].astype(F32)
+        ext[row, start + 16 : start + 16 + columns, :] = side[
+            row * columns : (row + 1) * columns
+        ]
+
+
+def side_rows(ref, part):
+    return ref[part * TOK : (part + 1) * TOK, :].astype(F32)
 
 
 def frame(ext, row, start, columns):
@@ -145,8 +152,8 @@
     initial_hbm,
     shifts_hbm,
     gain_hbm,
-    w_qkv_hbm,
-    w_out_hbm,
+    w_qkv,
+    w_out,
     east,
     west,
     following_out,
@@ -157,8 +164,6 @@
     initial,
     shifts,
     gain,
-    w_qkv,
-    w_out,
     ext,
     state,
     normed,
@@ -172,25 +177,23 @@
     small = start_copies(
         sems, 0, [(shifts_hbm, shifts), (initial_hbm, initial), (gain_hbm, gain)]
     )
-    parts = start_copies(sems, 3, column_parts(w_qkv_hbm, w_qkv, 6))
-    late = start_copies(sems, 9, [(w_out_hbm, w_out)])
     wait_all(small)
-    lat_shift, lon_shift = shifts[0, 0], shifts[0, 1]
-    fill(ext, initial, west[...].astype(F32), east[...].astype(F32))
+    lat_shift = shifts[0, 0]
+    fill(ext, initial, east[0 : 2 * TOK, :].astype(F32), WIN)
+    before = west[...].astype(F32)
     for row in range(LAT):
-        part = frame(ext, row, lon_shift, 24)
+        ext[row, 0:WIN, :] = before[row * WIN : (row + 1) * WIN]
+        part = frame(ext, row, origin0(shifts) + WIN, 24)
         for window in range(3):
             state[window_rows(window, row), :] = part[window * WIN : (window + 1) * WIN]
     norm_rows(state, 3 * TOK, gain[...], normed, scaled, spread, TOK)
-    saves = start_copies(sems, 10, [(scaled, scaled_hbm), (spread, spread_hbm)])
+    saves = start_copies(sems, 3, [(scaled, scaled_hbm), (spread, spread_hbm)])
     for part in range(6):
         at = slice(part * 512, (part + 1) * 512)
-        parts[part].wait()
         packed[:, at] = dot(normed[...], w_qkv[:, at]).astype(BF16)
-    saves += start_copies(sems, 12, [(packed.at[pl.ds(TOK, 2 * TOK)], packed_hbm)])
+    saves += start_copies(sems, 5, [(packed.at[pl.ds(TOK, 2 * TOK)], packed_hbm)])
     attend(3, packed, weights, mixed, lat_shift, 1)
-    saves += start_copies(sems, 13, [(weights, weights_hbm)])
-    wait_all(late)
+    saves += start_copies(sems, 6, [(weights, weights_hbm)])
     for part in range(4):
         at = slice(part * 256, (part + 1) * 256)
         following = state[:, at] + dot(mixed[...], w_out[:, at])
@@ -207,11 +210,10 @@
     shifts_hbm,
     gain_hbm,
     scale_hbm,
-    w_qkv_hbm,
-    w_out_hbm,
+    w_qkv,
+    w_out,
     before,
     east,
-    west,
     sent_out,
     final_hbm,
     noise_out_hbm,
@@ -223,8 +225,6 @@
     shifts,
     gain,
     noise_scale,
-    w_qkv,
-    w_out,
     ext,
     state,
     final,
@@ -242,18 +242,16 @@
         0,
         [(shifts_hbm, shifts), (noise_hbm, noise), (gain_hbm, gain), (scale_hbm, noise_scale)],
     )
-    parts = start_copies(sems, 4, column_parts(w_qkv_hbm, w_qkv, 6))
-    late = start_copies(sems, 10, [(w_out_hbm, w_out)])
     wait_all(small)
     lat_shift = shifts[1, 0]
-    lon0, origin1 = shifts[0, 1], origin(shifts)
+    lon1 = shifts[1, 1]
     scale = noise_scale[...]
     for step in range(2):
-        fill(ext, noise.at[step], west[step].astype(F32), east[step].astype(F32))
+        fill(ext, noise.at[step], side_rows(east, 2 + step), 0)
         for row in range(LAT):
-            part = frame(ext, row, origin1 + WIN, 16)
+            part = frame(ext, row, lon1, 16)
             if step == 0:
-                fields = frame(before, row, origin1 - lon0 + WIN, 16)
+                fields = frame(before, row, lon1 - origin0(shifts), 16)
             for window in range(2):
                 rows = window_rows(window, row)
                 here = part[window * WIN : (window + 1) * WIN]
@@ -262,29 +260,27 @@
                 else:
                     final[rows, :] = state[rows, :] + scale * here
                 noise_here[step, rows, :] = here
-    saves = start_copies(sems, 11, [(noise_here, noise_out_hbm)])
+    saves = start_copies(sems, 4, [(noise_here, noise_out_hbm)])
     norm_rows(state, 2 * TOK, gain[...], normed, scaled, spread, 0)
-    saves += start_copies(sems, 12, [(scaled, scaled_hbm), (spread, spread_hbm)])
+    saves += start_copies(sems, 5, [(scaled, scaled_hbm), (spread, spread_hbm)])
     for part in range(6):
         at = slice(part * 512, (part + 1) * 512)
-        parts[part].wait()
         packed[:, at] = dot(normed[...], w_qkv[:, at]).astype(BF16)
-    saves += start_copies(sems, 14, [(packed, packed_hbm)])
+    saves += start_copies(sems, 7, [(packed, packed_hbm)])
     attend(2, packed, weights, mixed, lat_shift, 0)
-    saves += start_copies(sems, 15, [(weights, weights_hbm)])
-    wait_all(late)
+    saves += start_copies(sems, 8, [(weights, weights_hbm)])
     for part in range(4):
         at = slice(part * 256, (part + 1) * 256)
         last = final[:, at] + dot(mixed[...], w_out[:, at])
         final[:, at] = last
         sent_out[:, at] = last.astype(BF16)
-    saves += start_copies(sems, 16, [(final, final_hbm)])
+    saves += start_copies(sems, 9, [(final, final_hbm)])
     wait_all(saves)
 
 
-def origin(shifts):
+def origin0(shifts):
     lon0, lon1 = shifts[0, 1], shifts[1, 1]
-    return jnp.where(lon1 <= lon0, lon1, lon1 - WIN)
+    return jnp.where(lon0 <= lon1, lon0, lon0 - WIN)
 
 
 def vmem():
@@ -324,17 +320,16 @@
     return pl.pallas_call(
         forward0_kernel,
         out_shape=shapes([((LAT, 24, C), F32)] + SAVED),
-        in_specs=[hbm()] * 5 + [vmem()] * 2,
+        in_specs=[hbm()] * 3 + [vmem()] * 4,
         out_specs=[vmem()] + [hbm()] * 4,
         scratch_shapes=[
             pltpu.VMEM((LAT, 16, C), F32),
             pltpu.SMEM((2, 2), jnp.int32),
             pltpu.VMEM((1, C), F32),
         ]
-        + buffers(WEIGHTS)
         + buffers(
             [
-                ((LAT, 32, C), F32),
+                ((LAT, 40, C), F32),
                 ((rows, C), F32),
                 ((rows, C), BF16),
                 ((rows, 3 * C), BF16),
@@ -342,17 +337,17 @@
             ]
         )
         + buffers(SAVED[1:])
-        + [pltpu.SemaphoreType.DMA((14,))],
+        + [pltpu.SemaphoreType.DMA((7,))],
         compiler_params=compiler_params(),
         name="forward0",
     )(initial, shifts, gain, w_qkv, w_out, east, west)
 
 
-def forward1(shifts, before, noise, east, west, gain, noise_scale, w_qkv, w_out):
+def forward1(shifts, before, noise, east, gain, noise_scale, w_qkv, w_out):
     return pl.pallas_call(
         forward1_kernel,
         out_shape=shapes([((ROWS, C), BF16), ((ROWS, C), F32), ((2, ROWS, C), F32)] + SAVED),
-        in_specs=[hbm()] * 6 + [vmem()] * 3,
+        in_specs=[hbm()] * 4 + [vmem()] * 4,
         out_specs=[vmem()] + [hbm()] * 6,
         scratch_shapes=[
             pltpu.VMEM((2, LAT, 16, C), BF16),
@@ -360,10 +355,9 @@
             pltpu.VMEM((1, C), F32),
             pltpu.VMEM((1, C), F32),
         ]
-        + buffers(WEIGHTS)
         + buffers(
             [
-                ((LAT, 32, C), F32),
+                ((LAT, 24, C), F32),
                 ((ROWS, C), F32),
                 ((ROWS, C), F32),
                 ((2, ROWS, C), F32),
@@ -373,27 +367,66 @@
             ]
         )
         + buffers(SAVED[1:])
-        + [pltpu.SemaphoreType.DMA((17,))],
+        + [pltpu.SemaphoreType.DMA((10,))],
         compiler_params=compiler_params(),
         name="forward1",
-    )(noise, shifts, gain, noise_scale, w_qkv, w_out, before, east, west)
-
-
-def transpose_kernel(source, out):
-    out[...] = source[...].T
-
-
-def transposed(matrix):
-    columns = matrix.shape[1]
+    )(noise, shifts, gain, noise_scale, w_qkv, w_out, before, east)
+
+
+def prepare_kernel(w_qkv_hbm, w_out_hbm, w_qkv, w_out, w_qkv_t, w_out_t, sems):
+    copies = start_copies(sems, 0, column_parts(w_qkv_hbm, w_qkv, 6))
+    copies += start_copies(sems, 6, column_parts(w_out_hbm, w_out, 2))
+    for part in range(8):
+        copies[part].wait()
+        held, turned = (w_qkv, w_qkv_t) if part < 6 else (w_out, w_out_t)
+        at = part % 6 * 512
+        turned[at : at + 512, :] = held[:, at : at + 512].T
+
+
+def prepare(w_qkv, w_out):
     return pl.pallas_call(
-        transpose_kernel,
-        grid=(columns // 256,),
-        out_shape=jax.ShapeDtypeStruct((columns, C), BF16),
-        in_specs=[pl.BlockSpec((C, 256), lambda at: (0, at))],
-        out_specs=pl.BlockSpec((256, C), lambda at: (at, 0)),
+        prepare_kernel,
+        out_shape=shapes(WEIGHTS + [((3 * C, C), BF16), ((C, C), BF16)]),
+        in_specs=[hbm()] * 2,
+        out_specs=[vmem()] * 4,
+        scratch_shapes=[pltpu.SemaphoreType.DMA((8,))],
         compiler_params=compiler_params(),
-        name="transposed",
-    )(matrix)
+        name="prepare",
+    )(w_qkv, w_out)
+
+
+def borders_kernel(initial_hbm, noise_hbm, target_hbm, east, west, initial, noise, target, sems):
+    copies = start_copies(
+        sems, 0, [(initial_hbm, initial), (noise_hbm, noise), (target_hbm, target)]
+    )
+
+    def rows(held, first, columns):
+        parts = [held[row].astype(F32)[first : first + columns] for row in range(LAT)]
+        return jnp.concatenate(parts).astype(BF16)
+
+    copies[0].wait()
+    east[0 : 2 * TOK, :] = rows(initial, 0, 16)
+    west[...] = rows(initial, WIN, WIN)
+    copies[1].wait()
+    east[2 * TOK : 3 * TOK, :] = rows(noise.at[0], 0, WIN)
+    east[3 * TOK : 4 * TOK, :] = rows(noise.at[1], 0, WIN)
+    copies[2].wait()
+    east[4 * TOK : 5 * TOK, :] = rows(target, 0, WIN)
+
+
+def borders(initial, noise, target):
+    return pl.pallas_call(
+        borders_kernel,
+        out_shape=shapes([((5 * TOK, C), BF16), ((TOK, C), BF16)]),
+        in_specs=[hbm()] * 3,
+        out_specs=[vmem()] * 2,
+        scratch_shapes=buffers(
+            [((LAT, 16, C), F32), ((2, LAT, 16, C), BF16), ((LAT, 16, C), F32)]
+        )
+        + [pltpu.SemaphoreType.DMA((3,))],
+        compiler_params=pltpu.CompilerParams(vmem_limit_bytes=56 * 1024 * 1024),
+        name="borders",
+    )(initial, noise, target)
 
 
 def attend_back(packed, weights_ref, d_mixed, d_packed):
@@ -430,18 +463,14 @@
 def step_back(
     copies, d_next, packed, weights, w_qkv_t, w_out_t, d_mixed, d_packed, d_normed
 ):
-    out_t, packed_copy, weights_copy, *qkv_t = copies
-    out_t.wait()
     d_branch = d_next[...].astype(BF16)
     for part in range(4):
         at = slice(part * 256, (part + 1) * 256)
         d_mixed[:, at] = dot(d_branch, w_out_t[:, at]).astype(BF16)
-    packed_copy.wait()
-    weights_copy.wait()
+    wait_all(copies)
     attend_back(packed, weights, d_mixed, d_packed)
     for part in range(4):
         at = slice(part * 256, (part + 1) * 256)
-        qkv_t[part].wait()
         d_normed[:, at] = dot(d_packed[...], w_qkv_t[:, at])
 
 
@@ -475,14 +504,13 @@
     target_hbm,
     gain_hbm,
     noise_hbm,
-    w_out_t_hbm,
     packed_hbm,
     weights_hbm,
     scaled_hbm,
     spread_hbm,
-    w_qkv_t_hbm,
+    w_out_t,
+    w_qkv_t,
     east,
-    west,
     d_out,
     head_out,
     gain_out,
@@ -495,12 +523,10 @@
     target,
     gain,
     noise,
-    w_out_t,
     packed,
     weights,
     scaled,
     spread,
-    w_qkv_t,
     ext,
     d_next,
     d_mixed,
@@ -524,16 +550,15 @@
     copies = start_copies(
         sems,
         7,
-        [(w_out_t_hbm, w_out_t), (packed_hbm, packed), (weights_hbm, weights)]
-        + column_parts(w_qkv_t_hbm, w_qkv_t, 4),
+        [(packed_hbm, packed), (weights_hbm, weights)],
     )
     late = start_copies(
-        sems, 14, [(scaled_hbm, scaled), (spread_hbm, spread), (gain_hbm, gain)]
+        sems, 9, [(scaled_hbm, scaled), (spread_hbm, spread), (gain_hbm, gain)]
     )
     wait_all(early)
-    fill(ext, target, west[...].astype(F32), east[...].astype(F32))
+    fill(ext, target, side_rows(east, 4), 0)
     for row in range(LAT):
-        part = frame(ext, row, origin(shifts) + WIN, 16)
+        part = frame(ext, row, shifts[1, 1], 16)
         for window in range(2):
             d_normed[window_rows(window, row), :] = part[window * WIN : (window + 1) * WIN]
     scale_total = jnp.zeros((8, C), F32)
@@ -566,12 +591,12 @@
 def backward0_kernel(
     shifts_hbm,
     gain_hbm,
-    w_out_t_hbm,
     packed_hbm,
     weights_hbm,
     scaled_hbm,
     spread_hbm,
-    w_qkv_t_hbm,
+    w_out_t,
+    w_qkv_t,
     d_in,
     d_east,
     gain_in,
@@ -581,12 +606,10 @@
     sums_out,
     shifts,
     gain,
-    w_out_t,
     packed,
     weights,
     scaled,
     spread,
-    w_qkv_t,
     ext,
     d_next,
     d_mixed,
@@ -598,19 +621,18 @@
     copies = start_copies(
         sems,
         1,
-        [(w_out_t_hbm, w_out_t), (packed_hbm, packed), (weights_hbm, weights)]
-        + column_parts(w_qkv_t_hbm, w_qkv_t, 4),
-    )
-    late = start_copies(sems, 8, [(scaled_hbm, scaled), (spread_hbm, spread), (gain_hbm, gain)])
+        [(packed_hbm, packed), (weights_hbm, weights)],
+    )
+    late = start_copies(sems, 3, [(scaled_hbm, scaled), (spread_hbm, spread), (gain_hbm, gain)])
     wait_all(early)
-    lon0, origin1 = shifts[0, 1], origin(shifts)
+    start = origin0(shifts) + WIN
     east = d_east[...].astype(F32)
     for row in range(LAT):
         ext[row, 0:8, :] = d_in[row * WIN : (row + 1) * WIN, :]
         ext[row, 8:16, :] = d_in[TOK + row * WIN : TOK + (row + 1) * WIN, :]
         ext[row, 16:24, :] = east[row * WIN : (row + 1) * WIN]
     for row in range(LAT):
-        part = frame(ext, row, lon0 - origin1, 16)
+        part = frame(ext, row, start - shifts[1, 1], 16)
         for window in range(2):
             d_next[window_rows(window, row), :] = part[window * WIN : (window + 1) * WIN]
     step_back(copies, d_next, packed, weights, w_qkv_t, w_out_t, d_mixed, d_packed, d_normed)
@@ -622,20 +644,20 @@
         for piece in range(4):
             token = at + piece * WIN
             row, window = (token % TOK) // WIN, token // TOK
-            ext[row, 8 + window * WIN : 16 + window * WIN, :] = d_here[
+            ext[row, 16 + window * WIN : 24 + window * WIN, :] = d_here[
                 piece * WIN : (piece + 1) * WIN
             ]
     sums_out[0:1, :] = jnp.sum(gain_total, axis=0, keepdims=True)
     sums_out[1:2, :] = jnp.sum(scale_in[...], axis=0, keepdims=True)
     tails = []
     for row in range(LAT):
-        own_out[row] = frame(ext, row, WIN - lon0, 16)
-        tails.append(frame(ext, row, 24 - lon0, WIN))
+        own_out[row] = frame(ext, row, 16 - start, 16)
+        tails.append(frame(ext, row, 32 - start, 16))
     tail_out[...] = jnp.concatenate(tails, axis=0).astype(BF16)
 
 
 WORK = [
-    ((LAT, 32, C), F32),
+    ((LAT, 24, C), F32),
     ((ROWS, C), F32),
     ((ROWS, C), BF16),
     ((ROWS, 3 * C), BF16),
@@ -644,7 +666,7 @@
 SUMS = [((8, C), F32)] * 2
 
 
-def backward1(shifts, final, others, target, east, west, noise, saved, gain, w_qkv_t, w_out_t):
+def backward1(shifts, final, others, target, east, noise, saved, gain, w_qkv_t, w_out_t):
     held = [
         ((ROWS, C), F32),
         ((ROWS, C), BF16),
@@ -653,123 +675,107 @@
         ((LAT, 16, C), F32),
         ((1, C), F32),
         ((2, ROWS, C), F32),
-        ((C, C), BF16),
     ]
     return pl.pallas_call(
         backward1_kernel,
         out_shape=shapes([((ROWS, C), F32), ((TOK, C), BF16)] + SUMS),
-        in_specs=[hbm()] * 14 + [vmem()] * 2,
+        in_specs=[hbm()] * 12 + [vmem()] * 3,
         out_specs=[vmem()] * 4,
         scratch_shapes=[pltpu.SMEM((2, 2), jnp.int32)]
-        + buffers(held + SAVED + [((3 * C, C), BF16)] + WORK)
-        + [pltpu.SemaphoreType.DMA((17,))],
+        + buffers(held + SAVED + WORK)
+        + [pltpu.SemaphoreType.DMA((12,))],
         compiler_params=compiler_params(),
         name="backward1",
-    )(shifts, final, *others, target, gain, noise, w_out_t, *saved, w_qkv_t, east, west)
+    )(shifts, final, *others, target, gain, noise, *saved, w_out_t, w_qkv_t, east)
 
 
 def backward0(shifts, d_in, d_east, saved, gain, gain_in, scale_in, w_qkv_t, w_out_t):
     return pl.pallas_call(
         backward0_kernel,
-        out_shape=shapes([((LAT, 16, C), F32), ((TOK, C), BF16), ((2, C), F32)]),
-        in_specs=[hbm()] * 8 + [vmem()] * 4,
+        out_shape=shapes([((LAT, 16, C), F32), ((ROWS, C), BF16), ((2, C), F32)]),
+        in_specs=[hbm()] * 6 + [vmem()] * 6,
         out_specs=[vmem()] * 3,
         scratch_shapes=[pltpu.SMEM((2, 2), jnp.int32), pltpu.VMEM((1, C), F32)]
-        + buffers([((C, C), BF16)] + SAVED + [((3 * C, C), BF16)] + WORK)
-        + [pltpu.SemaphoreType.DMA((11,))],
+        + buffers(SAVED + [((LAT, 48, C), F32)] + WORK[1:])
+        + [pltpu.SemaphoreType.DMA((6,))],
         compiler_params=compiler_params(),
         name="backward0",
-    )(shifts, gain, w_out_t, *saved, w_qkv_t, d_in, d_east, gain_in, scale_in)
-
-
-def along(value, axis, steps):
-    count = lax.axis_size(axis)
-    return lax.ppermute(value, axis, [(at, (at + steps) % count) for at in range(count)])
-
-
-def swapped(value, axis, bit):
-    count = lax.axis_size(axis)
-    return lax.ppermute(value, axis, [(at, at ^ bit) for at in range(count)])
-
-
-def total_over_devices(value, axis):
-    bit = 1
-    while bit < lax.axis_size(axis):
-        value = value + swapped(value, axis, bit)
-        bit *= 2
-    return value
+    )(shifts, gain, *saved, w_out_t, w_qkv_t, d_in, d_east, gain_in, scale_in)
+
+
+MEMBER = ("pair", "core")
+TILE = ("far", "row", "half")
+
+
+def along(value, steps):
+    count = lax.axis_size(TILE)
+    return lax.ppermute(value, TILE, [(at, (at + steps) % count) for at in range(count)])
+
+
+def other(value, axis):
+    return lax.ppermute(value, axis, [(0, 1), (1, 0)])
+
+
+def total_over(value, axes):
+    count = lax.axis_size(axes)
+    copies = jnp.broadcast_to(value[None], (count,) + value.shape)
+    return jnp.sum(lax.all_to_all(copies, axes, 0, 0), axis=0)
 
 
 def local(initial, target, noise, w_qkv, w_out, gain, noise_scale, shifts):
     initial, noise = initial[0], noise[:, 0]
-
-    def both_ways(part):
-        shape = part.shape[:-3] + (TOK, C)
-        first = part[..., :WIN, :].reshape(shape).astype(BF16)
-        last = part[..., WIN:, :].reshape(shape).astype(BF16)
-        return along(first, "tile", -1), along(last, "tile", 1)
-
-    initial_sides = both_ways(initial)
-    noise_sides = both_ways(noise)
-    w_qkv_t, w_out_t = transposed(w_qkv), transposed(w_out)
-    initial_sides, w_qkv_t, w_out_t = lax.optimization_barrier((initial_sides, w_qkv_t, w_out_t))
     gain_row, scale_row = gain[None], noise_scale[None]
-    before, *saved0 = forward0(shifts, initial, *initial_sides, gain_row, w_qkv, w_out)
-    noise_sides, target_now = lax.optimization_barrier((noise_sides, target))
-    target_sides = both_ways(target_now)
+    east, west = borders(initial, noise, target)
+    east, west = along(east, -1), along(west, 1)
+    prepared = prepare(w_qkv, w_out)
+    east, west, prepared = lax.optimization_barrier((east, west, prepared))
+    here, here_t = prepared[:2], prepared[2:]
+    before, *saved0 = forward0(shifts, initial, east, west, gain_row, *here)
     sent, final, noise_here, *saved1 = forward1(
-        shifts, before, noise, *noise_sides, gain_row, scale_row, w_qkv, w_out
-    )
-    far = swapped(sent, "member", 2)
-    near = swapped(sent, "member", 1)
-    far_near = swapped(far, "member", 1)
+        shifts, before, noise, east, gain_row, scale_row, *here
+    )
+    far = other(sent, "pair")
+    near = other(sent, "core")
+    far_near = other(far, "core")
     d_one, head, gain_part, scale_part = backward1(
         shifts,
         final,
         (near, far, far_near),
         target,
-        *target_sides,
+        east,
         noise_here,
         saved1,
         gain_row,
-        w_qkv_t,
-        w_out_t,
+        *here_t,
     )
     own, tail, sums = backward0(
-        shifts,
-        d_one,
-        along(head, "tile", -1),
-        saved0,
-        gain_row,
-        gain_part,
-        scale_part,
-        w_qkv_t,
-        w_out_t,
-    )
-    arrived = along(tail, "tile", 1)
-    sums = total_over_devices(sums, "member")
+        shifts, d_one, along(head, -1), saved0, gain_row, gain_part, scale_part, *here_t
+    )
+    arrived = along(tail, 1)
+    sums = total_over(sums, MEMBER + TILE[1:])
     sums, arrived = lax.optimization_barrier((sums, arrived))
-    column = jnp.arange(WIN)[None, :, None]
-    first = jnp.where(
-        column < shifts[0, 1], arrived.reshape(LAT, WIN, C).astype(F32), own[:, :WIN]
-    )
-    state_grad = jnp.concatenate([first, own[:, WIN:]], axis=1)[None]
-    sums = total_over_devices(sums, "tile")
-    members = lax.axis_size("member")
-    factor = (members * LAT * initial.shape[1] * lax.axis_size("tile")) ** (-0.5)
+    sums = total_over(sums, TILE[0])
+    column = jnp.arange(16)[None, :, None]
+    state_grad = jnp.where(
+        column < origin0(shifts) + WIN, arrived.reshape(LAT, 16, C).astype(F32), own
+    )[None]
+    members = lax.axis_size(MEMBER)
+    factor = (members * LAT * initial.shape[1] * lax.axis_size(TILE)) ** (-0.5)
     return (state_grad, sums[0] * factor, sums[1] * factor)
 
 
 def solution(mesh):
+    members, tiles = mesh.devices.shape
+    fine = Mesh(mesh.devices.reshape(members // 2, 2, tiles // 8, 4, 2), MEMBER + TILE)
     in_specs = (
-        P("member", None, "tile", None),
-        P(None, "tile", None),
-        P(None, "member", None, "tile", None),
+        P(MEMBER, None, TILE, None),
+        P(None, TILE, None),
+        P(None, MEMBER, None, TILE, None),
         P(),
         P(),
         P(),
         P(),
         P(),
     )
-    out_specs = (P("member", None, "tile", None), P(), P())
-    return jax.shard_map(local, mesh=mesh, in_specs=in_specs, out_specs=out_specs, check_vma=False)
+    out_specs = (P(MEMBER, None, TILE, None), P(), P())
+    return jax.shard_map(local, mesh=fine, in_specs=in_specs, out_specs=out_specs, check_vma=False)

time: 130 us -> 101 us (0.78)
  waiting for transfers between devices: 55 us -> 31.8 us
  Pallas kernels: 32.2 us -> 27 us
  starting transfers between devices: 32.9 us -> 29.2 us
  between operations: 0.85 us -> 3.37 us
  local copies, waits for them, and re-layouts: 4.51 us -> 6.4 us
  other arithmetic: 3.32 us -> 1.66 us
    ppermute x19 -> x7, waiting for transfers between devices: 55 us -> 20.1 us  [the longest x4 11.7 us: along(): lax.ppermute(value, TILE, [(at, (at + steps) % count) for at in range(cou...]
    ppermute x19 -> x7, starting transfers between devices: 32.9 us -> 14.6 us  [the longest x4 13.2 us: along(): lax.ppermute(value, TILE, [(at, (at + steps) % count) for at in range(cou...]
    all_to_all x0 -> x2, starting transfers between devices: none -> 14.5 us  [total_over(): return jnp.sum(lax.all_to_all(copies, axes, 0, 0), axis=0)]
    all_to_all x0 -> x2, waiting for transfers between devices: none -> 11.7 us  [total_over(): return jnp.sum(lax.all_to_all(copies, axes, 0, 0), axis=0)]
    pallas_call x1, Pallas kernels: 8.3 us -> 5.83 us  [backward1(): pl.pallas_call(backward1_kernel, out_shape=shapes([((ROWS, C), F32), ((TO...]
    pallas_call x2, Pallas kernels: 4.42 us -> 6.3 us  [the longest x1 3.96 us: prepare(): pl.pallas_call(prepare_kernel, out_shape=shapes(WEIGHTS + [((3 * C, C), B...]
    pallas_call x1, Pallas kernels: 7.74 us -> 5.97 us  [backward0(): pl.pallas_call(backward0_kernel, out_shape=shapes([((LAT, 16, C), F32), (...]
    unnamed x18 -> x16, local copies, waits for them, and re-layouts: 2.82 us -> 4.41 us
  transfers between devices with their start and end apart: 19 -> 9, of which waited for: 14 -> 6; matrix products, arithmetic and copies ran while one was open for 3% -> 2% of each run, Pallas kernels for 8% -> 4%
where the time goes in v3:
time: 101 us; the launch traced here: 99.4 us
  waiting for transfers between devices  31.8 us (31%)
  starting transfers between devices  29.2 us (29%)
  Pallas kernels  27 us (27%)
  local copies, waits for them, and re-layouts  6.4 us (6%)
  between operations  3.37 us (3%)
  other arithmetic  1.66 us (2%)
    all_to_all x2, starting transfers between devices, total_over(): return jnp.sum(lax.all_to_all(copies, axes, 0, 0), axis=0)  14.5 us
    ppermute x4, starting transfers between devices, along(): lax.ppermute(value, TILE, [(at, (at + steps) % count) for at in range(cou...  13.2 us
    ppermute x4, waiting for transfers between devices, along(): lax.ppermute(value, TILE, [(at, (at + steps) % count) for at in range(cou...  11.7 us
    all_to_all x2, waiting for transfers between devices, total_over(): return jnp.sum(lax.all_to_all(copies, axes, 0, 0), axis=0)  11.7 us
    ppermute x3, waiting for transfers between devices, other(): return lax.ppermute(value, axis, [(0, 1), (1, 0)])  8.4 us
    pallas_call x1, Pallas kernels, backward0(): pl.pallas_call(backward0_kernel, out_shape=shapes([((LAT, 16, C), F32), (...  5.97 us
    pallas_call x1, Pallas kernels, backward1(): pl.pallas_call(backward1_kernel, out_shape=shapes([((ROWS, C), F32), ((TO...  5.83 us
    pallas_call x1, Pallas kernels, forward0(): pl.pallas_call(forward0_kernel, out_shape=shapes([((LAT, 24, C), F32)] +...  4.7 us
  transfers between devices with their start and end apart: 9, of which 6 were waited for; matrix products, arithmetic and copies ran while one was open for 2% of the time, Pallas kernels for 4%

profile of v3, /device:TPU:32, one launch (start us, length us, event | category | flops | bytes accessed | tf_op | source)
XLA Modules:
  0.0 99.4 jit_solution(5240522752903978229)
XLA Ops:
  0.6 0.0 copy-start.1
  0.6 0.0 copy-start.6
  0.7 0.0 copy-start.5
  0.7 2.3 %borders.1 = (bf16[320,1024]{1,0:T(8,128)(2,1)}, bf16[64,1024]{1,0:T(8,128)(2,1)}) custom-call(f32[8,16,1024]{2,1,0:T(8,128)} %bitcast.12, bf16[2,8,16,1024]{3,2,1,0:T(8,128)(2,1)} %bitcast.14, f32[8,16,1024]{2,1,0:T(8,128)} %target_hbm.3), custom_call_target="tpu_custom_call" | custom-call | tf_op jit(solution)/shard_map/borders/pallas_call | solution.py:418
  3.0 5.0 %collective-permute-start = (bf16[320,1024]{1,0:T(8,128)(2,1)}, bf16[320,1024]{1,0:T(8,128)(2,1)S(1)}, u32[]{:S(2)}, u32[]{:S(2)}) collective-permute-start(bf16[320,1024]{1,0:T(8,128)(2,1)} %get-tuple-element.36), channel_id=1, source_target_pairs={{0,63},{1,0},{2,1},{3,2},{4,3},{5,4},{6,5},{7,6},{8,7},{9,8},{10,9... | collective-permute-start | bytes 1966088 | tf_op jit(solution)/shard_map/ppermute | solution.py:712
  8.0 0.0 collective-permute-start.1
  8.0 0.0 copy-start
  8.0 2.8 %copy-done = bf16[1024,3072]{1,0:T(8,128)(2,1)S(1)} copy-done((bf16[1024,3072]{1,0:T(8,128)(2,1)S(1)}, bf16[1024,3072]{1,0:T(8,128)(2,1)}, u32[]{:S(2)}) %copy-start) | copy-done | bytes 6291480
  10.8 0.0 copy-start.4
  10.8 1.6 %copy-done.4 = bf16[1024,1024]{1,0:T(8,128)(2,1)S(1)} copy-done((bf16[1024,1024]{1,0:T(8,128)(2,1)S(1)}, bf16[1024,1024]{1,0:T(8,128)(2,1)}, u32[]{:S(2)}) %copy-start.4) | copy-done | bytes 2097176
  12.4 4.0 %prepare.1 = (bf16[1024,3072]{1,0:T(8,128)(2,1)S(1)}, bf16[1024,1024]{1,0:T(8,128)(2,1)S(1)}, bf16[3072,1024]{1,0:T(8,128)(2,1)S(1)}, bf16[1024,1024]{1,0:T(8,128)(2,1)S(1)}) custom-call(bf16[1024,3072]{1,0:T(8,128)(2,1)S(1)} %copy-done, bf16[1024,1024]{1,0:T(8,128)(2,1)S(1)} %copy-done.4), custom_call_target="tpu_custom_call" | custom-call | tf_op jit(solution)/shard_map/prepare/pallas_call | solution.py:387
  16.4 0.0 copy-start.2
  16.4 0.0 copy-start.7
  16.4 7.9 %collective-permute-done.1.west = bf16[64,1024]{1,0:T(8,128)(2,1)S(1)} collective-permute-done((bf16[64,1024]{1,0:T(8,128)(2,1)}, bf16[64,1024]{1,0:T(8,128)(2,1)S(1)}, u32[]{:S(2)}, u32[]{:S(2)}) %collective-permute-start.1) | collective-permute-done | bytes 131104 | tf_op jit(solution)/shard_map/ppermute | solution.py:712
  24.3 0.0 collective-permute-done.east
  24.3 0.0 copy-done.1
  24.3 0.0 copy-done.6
  24.3 0.0 copy-done.5
  24.3 4.7 %forward0.1 = (f32[8,24,1024]{2,1,0:T(8,128)S(1)}, bf16[128,3072]{1,0:T(8,128)(2,1)S(1)}, bf16[16,64,256]{2,1,0:T(8,128)(2,1)S(1)}, bf16[128,1024]{1,0:T(8,128)(2,1)S(1)}, f32[128,128]{1,0:T(8,128)S(1)}) custom-call(f32[8,16,1024]{2,1,0:T(8,128)S(1)} %bitcast.13, s32[2,2]{1,0:T(2,128)S(1)} %copy-done.6, f32[1,1024]{1,0:T(1,128)S(1)} %bitcast.16, ...), custom_call_target="tpu_custom_call" | custom-call | tf_op jit(solution)/shard_map/forward0/pallas_call | solution.py:320
  29.0 0.0 copy-start.3
  29.0 0.0 copy-done.2
  29.0 0.0 copy-done.7
  29.0 4.1 %forward1.1 = (bf16[128,1024]{1,0:T(8,128)(2,1)S(1)}, f32[128,1024]{1,0:T(8,128)S(1)}, f32[2,128,1024]{2,1,0:T(8,128)S(1)}, bf16[128,3072]{1,0:T(8,128)(2,1)S(1)...) custom-call(bf16[2,8,16,1024]{3,2,1,0:T(8,128)(2,1)S(1)} %bitcast.15, ...), custom_call_target="tpu_custom_call" | custom-call | tf_op jit(solution)/shard_map/forward1/pallas_call | solution.py:347
  33.2 1.4 %collective-permute-start.3 = (bf16[128,1024]{1,0:T(8,128)(2,1)S(1)}, bf16[128,1024]{1,0:T(8,128)(2,1)S(1)}, u32[]{:S(2)}, u32[]{:S(2)}) collective-permute-start(bf16[128,1024]{1,0:T(8,128)(2,1)S(1)} %get-tuple-element.54), channel_id=1, source_target_pairs={{0,128},{128,0},{1,129},{129,1},{2,130},{130,2},{3,131},{131,3},{4... | collective-permute-start | bytes 786440 | tf_op jit(solution)/shard_map/ppermute | solution.py:716
  34.6 0.0 collective-permute-start.2
  34.6 6.9 %collective-permute-done.3.far_hbm = bf16[128,1024]{1,0:T(8,128)(2,1)S(1)} collective-permute-done((bf16[128,1024]{1,0:T(8,128)(2,1)S(1)}, bf16[128,1024]{1,0:T(8,128)(2,1)S(1)}, u32[]{:S(2)}, u32[]{:S(2)}) %collective-permute-start.3) | collective-permute-done | bytes 262176 | tf_op jit(solution)/shard_map/ppermute | solution.py:716
  41.5 0.0 collective-permute-start.4
  41.5 0.0 collective-permute-done.2.near_hbm
  41.5 1.5 %collective-permute-done.4.far_near_hbm = bf16[128,1024]{1,0:T(8,128)(2,1)S(1)} collective-permute-done((bf16[128,1024]{1,0:T(8,128)(2,1)S(1)}, bf16[128,1024]{1,0:T(8,128)(2,1)S(1)}, u32[]{:S(2)}, u32[]{:S(2)}) %collective-permute-start.4) | collective-permute-done | bytes 262176 | tf_op jit(solution)/shard_map/ppermute | solution.py:716
  43.1 0.0 copy-done.3
  43.1 5.8 %backward1.1 = (f32[128,1024]{1,0:T(8,128)S(1)}, bf16[64,1024]{1,0:T(8,128)(2,1)S(1)}, f32[8,1024]{1,0:T(8,128)S(1)}, f32[8,1024]{1,0:T(8,128)S(1)}) custom-call(s32[2,2]{1,0:T(2,128)S(1)} %copy-done.6, f32[128,1024]{1,0:T(8,128)S(1)} %get-tuple-element.53.final_hbm, bf16[128,1024]{1,0:T(8,128)(2,1)S(1)} %collective-permute-done.2.near_hbm, ...), custom_call_target="tpu_custom_call" | custom-call | tf_op jit(solution)/shard_map/backward1/pallas_call | solution.py:679
  48.9 3.9 %collective-permute-start.5 = (bf16[64,1024]{1,0:T(8,128)(2,1)S(1)}, bf16[64,1024]{1,0:T(8,128)(2,1)S(1)}, u32[]{:S(2)}, u32[]{:S(2)}) collective-permute-start(bf16[64,1024]{1,0:T(8,128)(2,1)S(1)} %get-tuple-element.61), channel_id=1, source_target_pairs={{0,63},{1,0},{2,1},{3,2},{4,3},{5,4},{6,5},{7,6},{8,7},{9,8},{10,9... | collective-permute-start | bytes 393224 | tf_op jit(solution)/shard_map/ppermute | solution.py:712
  52.8 3.8 %collective-permute-done.5.d_east = bf16[64,1024]{1,0:T(8,128)(2,1)S(1)} collective-permute-done((bf16[64,1024]{1,0:T(8,128)(2,1)S(1)}, bf16[64,1024]{1,0:T(8,128)(2,1)S(1)}, u32[]{:S(2)}, u32[]{:S(2)}) %collective-permute-start.5) | collective-permute-done | bytes 131104 | tf_op jit(solution)/shard_map/ppermute | solution.py:712
  56.7 6.0 %backward0.1 = (f32[8,16,1024]{2,1,0:T(8,128)S(1)}, bf16[128,1024]{1,0:T(8,128)(2,1)S(1)}, f32[2,1024]{1,0:T(2,128)S(1)}) custom-call(s32[2,2]{1,0:T(2,128)S(1)} %copy-done.6, f32[1,1024]{1,0:T(1,128)S(1)} %bitcast.19, bf16[128,3072]{1,0:T(8,128)(2,1)S(1)} %get-tuple-element.46.packed_hbm, bf16[16,64,256]{2,1,0:T(8,128)(2,1)S(1)} %get-tuple-element.47.weights_hbm, ...), custom_call_target="tpu_custom_call" | custom-call | tf_op jit(solution)/shard_map/backward0/pallas_call | solution.py:693
  62.6 4.2 %collective-permute-start.6 = (bf16[128,1024]{1,0:T(8,128)(2,1)S(1)}, bf16[128,1024]{1,0:T(8,128)(2,1)S(1)}, u32[]{:S(2)}, u32[]{:S(2)}) collective-permute-start(bf16[128,1024]{1,0:T(8,128)(2,1)S(1)} %get-tuple-element.65), channel_id=1, source_target_pairs={{0,1},{1,2},{2,3},{3,4},{4,5},{5,6},{6,7},{7,8},{8,9},{9,10},{10,1... | collective-permute-start | bytes 786440 | tf_op jit(solution)/shard_map/ppermute | solution.py:712
  66.9 0.8 broadcast_in_dim.33
  67.6 4.9 %all-to-all-start = ((f32[32,2,1024]{2,1,0:T(2,128)}), f32[32,2,1024]{2,1,0:T(2,128)S(1)}, u32[]{:S(2)}, u32[]{:S(2)}) async-start(f32[32,2,1024]{2,1,0:T(2,128)} %broadcast_in_dim.33), calls=%async_computation | async-start | bytes 524288 | tf_op jit(solution)/shard_map/all_to_all | solution.py:722
  72.5 0.6 fusion.1
  75.7 5.7 %all-to-all-done = f32[32,2,1024]{2,1,0:T(2,128)S(1)} async-done(((f32[32,2,1024]{2,1,0:T(2,128)}), f32[32,2,1024]{2,1,0:T(2,128)S(1)}, u32[]{:S(2)}, u32[]{:S(2)}) %all-to-all-start) | async-done | bytes 262176 | tf_op jit(solution)/shard_map/all_to_all | solution.py:722
  81.4 0.1 reduce_sum.18
  81.5 0.0 collective-permute-done.6
  81.5 0.6 broadcast_in_dim.35
  82.2 9.7 %all-to-all-start.1 = ((f32[8,2,1024]{2,1,0:T(2,128)}), f32[8,2,1024]{2,1,0:T(2,128)S(1)}, u32[]{:S(2)}, u32[]{:S(2)}) async-start(f32[8,2,1024]{2,1,0:T(2,128)} %broadcast_in_dim.35), calls=%async_computation.1 | async-start | bytes 131072 | tf_op jit(solution)/shard_map/all_to_all | solution.py:722
  91.8 0.9 fusion
  92.7 6.0 %all-to-all-done.1 = f32[8,2,1024]{2,1,0:T(2,128)S(1)} async-done(((f32[8,2,1024]{2,1,0:T(2,128)}), f32[8,2,1024]{2,1,0:T(2,128)S(1)}, u32[]{:S(2)}, u32[]{:S(2)}) %all-to-all-start.1) | async-done | bytes 65568 | tf_op jit(solution)/shard_map/all_to_all | solution.py:722
  98.8 0.6 slice_multiply_fusion
  (2 shorter events, 0.0 us)
Async XLA Ops:
  0.6 23.7 %copy-start.1 = (f32[1,8,16,1024]{3,2,1,0:T(8,128)S(1)}, f32[1,8,16,1024]{3,2,1,0:T(8,128)}, u32[]{:S(2)}) copy-start(f32[1,8,16,1024]{3,2,1,0:T(8,128)} %param.8) | copy-start | bytes 1572868
  0.6 23.7 %copy-start.6 = (s32[2,2]{1,0:T(2,128)S(1)}, s32[2,2]{1,0:T(2,128)}, u32[]{:S(2)}) copy-start(s32[2,2]{1,0:T(2,128)} %shifts_hbm.7) | copy-start | bytes 52
  0.7 23.7 %copy-start.5 = (f32[1024]{0:T(1024)S(1)}, f32[1024]{0:T(1024)}, u32[]{:S(2)}) copy-start(f32[1024]{0:T(1024)} %param.13) | copy-start | bytes 12292
  3.0 21.3 %collective-permute-start = (bf16[320,1024]{1,0:T(8,128)(2,1)}, bf16[320,1024]{1,0:T(8,128)(2,1)S(1)}, u32[]{:S(2)}, u32[]{:S(2)}) collective-permute-start(bf16[320,1024]{1,0:T(8,128)(2,1)} %get-tuple-element.36), channel_id=1, source_target_pairs={{0,63},{1,0},{2,1},{3,2},{4,3},{5,4},{6,5},{7,6},{8,7},{9,8},{10,9... | collective-permute-start | bytes 1966088 | tf_op jit(solution)/shard_map/ppermute | solution.py:712
  8.0 16.3 %collective-permute-start.1 = (bf16[64,1024]{1,0:T(8,128)(2,1)}, bf16[64,1024]{1,0:T(8,128)(2,1)S(1)}, u32[]{:S(2)}, u32[]{:S(2)}) collective-permute-start(bf16[64,1024]{1,0:T(8,128)(2,1)} %get-tuple-element.37), channel_id=1, source_target_pairs={{0,1},{1,2},{2,3},{3,4},{4,5},{5,6},{6,7},{7,8},{8,9},{9,10},{10,1... | collective-permute-start | bytes 393224 | tf_op jit(solution)/shard_map/ppermute | solution.py:712
  8.0 2.8 %copy-start = (bf16[1024,3072]{1,0:T(8,128)(2,1)S(1)}, bf16[1024,3072]{1,0:T(8,128)(2,1)}, u32[]{:S(2)}) copy-start(bf16[1024,3072]{1,0:T(8,128)(2,1)} %w_qkv_hbm.1) | copy-start | bytes 18874372
  10.8 1.6 %copy-start.4 = (bf16[1024,1024]{1,0:T(8,128)(2,1)S(1)}, bf16[1024,1024]{1,0:T(8,128)(2,1)}, u32[]{:S(2)}) copy-start(bf16[1024,1024]{1,0:T(8,128)(2,1)} %w_out_hbm.1) | copy-start | bytes 6291460
  16.4 12.7 %copy-start.2 = (bf16[2,1,8,16,1024]{4,3,2,1,0:T(8,128)(2,1)S(1)}, bf16[2,1,8,16,1024]{4,3,2,1,0:T(8,128)(2,1)}, u32[]{:S(2)}) copy-start(bf16[2,1,8,16,1024]{4,3,2,1,0:T(8,128)(2,1)} %param.10) | copy-start | bytes 1572868
  16.4 12.7 %copy-start.7 = (f32[1024]{0:T(1024)S(1)}, f32[1024]{0:T(1024)}, u32[]{:S(2)}) copy-start(f32[1024]{0:T(1024)} %param.14) | copy-start | bytes 12292
  29.0 14.0 %copy-start.3 = (f32[8,16,1024]{2,1,0:T(8,128)S(1)}, f32[8,16,1024]{2,1,0:T(8,128)}, u32[]{:S(2)}) copy-start(f32[8,16,1024]{2,1,0:T(8,128)} %target_hbm.3) | copy-start | bytes 1572868
  33.2 8.3 %collective-permute-start.3 = (bf16[128,1024]{1,0:T(8,128)(2,1)S(1)}, bf16[128,1024]{1,0:T(8,128)(2,1)S(1)}, u32[]{:S(2)}, u32[]{:S(2)}) collective-permute-start(bf16[128,1024]{1,0:T(8,128)(2,1)S(1)} %get-tuple-element.54), channel_id=1, source_target_pairs={{0,128},{128,0},{1,129},{129,1},{2,130},{130,2},{3,131},{131,3},{4... | collective-permute-start | bytes 786440 | tf_op jit(solution)/shard_map/ppermute | solution.py:716
  34.6 6.9 %collective-permute-start.2 = (bf16[128,1024]{1,0:T(8,128)(2,1)S(1)}, bf16[128,1024]{1,0:T(8,128)(2,1)S(1)}, u32[]{:S(2)}, u32[]{:S(2)}) collective-permute-start(bf16[128,1024]{1,0:T(8,128)(2,1)S(1)} %get-tuple-element.54), channel_id=1, source_target_pairs={{0,64},{64,0},{1,65},{65,1},{2,66},{66,2},{3,67},{67,3},{4,68},{68... | collective-permute-start | bytes 786440 | tf_op jit(solution)/shard_map/ppermute | solution.py:716
  41.5 1.5 %collective-permute-start.4 = (bf16[128,1024]{1,0:T(8,128)(2,1)S(1)}, bf16[128,1024]{1,0:T(8,128)(2,1)S(1)}, u32[]{:S(2)}, u32[]{:S(2)}) collective-permute-start(bf16[128,1024]{1,0:T(8,128)(2,1)S(1)} %collective-permute-done.3.far_hbm), channel_id=1, source_target_pairs={{0,64},{64,0},{1,65},{65,1},{2,66},{66,2},{3,67},{67,3},{4,68},{68... | collective-permute-start | bytes 786440 | tf_op jit(solution)/shard_map/ppermute | solution.py:716
  48.9 7.8 %collective-permute-start.5 = (bf16[64,1024]{1,0:T(8,128)(2,1)S(1)}, bf16[64,1024]{1,0:T(8,128)(2,1)S(1)}, u32[]{:S(2)}, u32[]{:S(2)}) collective-permute-start(bf16[64,1024]{1,0:T(8,128)(2,1)S(1)} %get-tuple-element.61), channel_id=1, source_target_pairs={{0,63},{1,0},{2,1},{3,2},{4,3},{5,4},{6,5},{7,6},{8,7},{9,8},{10,9... | collective-permute-start | bytes 393224 | tf_op jit(solution)/shard_map/ppermute | solution.py:712
  62.6 18.9 %collective-permute-start.6 = (bf16[128,1024]{1,0:T(8,128)(2,1)S(1)}, bf16[128,1024]{1,0:T(8,128)(2,1)S(1)}, u32[]{:S(2)}, u32[]{:S(2)}) collective-permute-start(bf16[128,1024]{1,0:T(8,128)(2,1)S(1)} %get-tuple-element.65), channel_id=1, source_target_pairs={{0,1},{1,2},{2,3},{3,4},{4,5},{5,6},{6,7},{7,8},{8,9},{9,10},{10,1... | collective-permute-start | bytes 786440 | tf_op jit(solution)/shard_map/ppermute | solution.py:712
  67.6 13.8 %all-to-all-start = ((f32[32,2,1024]{2,1,0:T(2,128)}), f32[32,2,1024]{2,1,0:T(2,128)S(1)}, u32[]{:S(2)}, u32[]{:S(2)}) async-start(f32[32,2,1024]{2,1,0:T(2,128)} %broadcast_in_dim.33), calls=%async_computation | async-start | bytes 524288 | tf_op jit(solution)/shard_map/all_to_all | solution.py:722
  82.2 16.6 %all-to-all-start.1 = ((f32[8,2,1024]{2,1,0:T(2,128)}), f32[8,2,1024]{2,1,0:T(2,128)S(1)}, u32[]{:S(2)}, u32[]{:S(2)}) async-start(f32[8,2,1024]{2,1,0:T(2,128)} %broadcast_in_dim.35), calls=%async_computation.1 | async-start | bytes 131072 | tf_op jit(solution)/shard_map/all_to_all | solution.py:722

commit v4 on v3

v4 whole, which is shorter than its diff:
```python
import functools

import jax
import jax.numpy as jnp
from jax import lax
from jax.experimental import pallas as pl
from jax.experimental.pallas import tpu as pltpu
from jax.sharding import Mesh
from jax.sharding import PartitionSpec as P

C = 1024
HEAD = 32
WIN = 8
LAT = 8
TOK = LAT * WIN
GROUP = 4
LANES = GROUP * HEAD
GROUPS = C // LANES
SPAN = GROUP * TOK
SCALE = HEAD ** (-0.5)
SMOOTH = 0.25
F32 = jnp.float32
BF16 = jnp.bfloat16
VMEM_LIMIT = 14 * 1024 * 1024


def dot(left, right):
    return lax.dot_general(left, right, (((1,), (0,)), ((), ())), preferred_element_type=F32)


def dot_nt(left, right):
    return lax.dot_general(left, right, (((1,), (1,)), ((), ())), preferred_element_type=F32)


def dot_tn(left, right):
    return lax.dot_general(left, right, (((0,), (0,)), ((), ())), preferred_element_type=F32)


def head_masks():
    lane = lax.broadcasted_iota(jnp.int32, (TOK, LANES), 1) // HEAD
    return [lane == head for head in range(GROUP)]


def by_head(value, masks):
    zero = jnp.zeros_like(value)
    return jnp.concatenate([jnp.where(mask, value, zero) for mask in masks], axis=0)


def fold_heads(stacked, masks):
    out = stacked[:TOK]
    for head in range(1, GROUP):
        out = jnp.where(masks[head], stacked[head * TOK : (head + 1) * TOK], out)
    return out


def lat_mask(lat_shift):
    key_lat = lax.broadcasted_iota(jnp.int32, (TOK, SPAN), 0) // WIN
    query_lat = (lax.broadcasted_iota(jnp.int32, (TOK, SPAN), 1) % TOK) // WIN
    return (key_lat < lat_shift) == (query_lat < lat_shift)


def lanes(start, size):
    return pl.ds(pl.multiple_of(start, 128), size)


def fill(ext, own_ref, side, start):
    columns = side.shape[0] // LAT
    for row in range(LAT):
        ext[row, start : start + 16, :] = own_ref[row].astype(F32)
        ext[row, start + 16 : start + 16 + columns, :] = side[
            row * columns : (row + 1) * columns
        ]


NOISE_ROWS = LAT * 7
PART_ROWS = TOK // 4
EAST_INITIAL = 2 * NOISE_ROWS + PART_ROWS
INITIAL_ROWS = LAT * 15
EAST_ROWS = 256
SENT_ROWS = 2 * TOK + PART_ROWS
QUARTER = C // 4


def member_index():
    return lax.axis_index("pair") * 2 + lax.axis_index("core")


def quarter(member):
    return pl.ds(pl.multiple_of(member * QUARTER, QUARTER), QUARTER)


def frame(ext, row, start, columns):
    held = ext.shape[1]
    return pltpu.roll(ext[row], lax.rem(held - start, held), 0)[:columns]


def norm_rows(x_ref, rows, gain, normed_ref, scaled_ref, spread_ref, saved):
    for at in range(0, rows, 32):
        x = x_ref[at : at + 32, :]
        centre = jnp.mean(x, axis=-1, keepdims=True)
        offset = x - centre
        spread = lax.rsqrt(jnp.mean(offset * offset, axis=-1, keepdims=True) + 1e-05)
        scaled = offset * spread
        normed_ref[at : at + 32, :] = (scaled * gain).astype(BF16)
        if at < saved:
            scaled_ref[at : at + 32, :] = scaled.astype(BF16)
            spread_ref[at : at + 32, :] = jnp.broadcast_to(spread, (32, 128))


def attend(windows, packed_ref, weights_ref, mixed_ref, lat_shift, saved):
    masks = head_masks()
    allowed = lat_mask(lat_shift)

    def group(at, _):
        for window in range(windows):
            rows = slice(window * TOK, (window + 1) * TOK)
            queries = packed_ref[rows, lanes(at * LANES, LANES)]
            keys = packed_ref[rows, lanes(C + at * LANES, LANES)]
            values = packed_ref[rows, lanes(2 * C + at * LANES, LANES)]
            scores = dot_nt(keys, by_head(queries, masks))
            scores = jnp.where(allowed, scores, -1e9 / SCALE)
            highest = jnp.max(scores, axis=0, keepdims=True)
            raised = jnp.exp((scores - highest) * SCALE)
            total = jnp.sum(raised, axis=0, keepdims=True)
            weights = (raised * (1.0 / total)).astype(BF16)
            if window < saved:
                weights_ref[window * GROUPS + at] = weights
            mixed = fold_heads(dot_tn(weights, values), masks)
            mixed_ref[rows, lanes(at * LANES, LANES)] = mixed.astype(BF16)
        return 0

    lax.fori_loop(0, GROUPS, group, 0, unroll=GROUPS)


def window_rows(window, row):
    start = window * TOK + row * WIN
    return slice(start, start + WIN)


def start_copies(sems, first, pairs):
    copies = []
    for at, (source, destination) in enumerate(pairs):
        copy = pltpu.make_async_copy(source, destination, sems.at[first + at])
        copy.start()
        copies.append(copy)
    return copies


def wait_all(copies):
    for copy in copies:
        copy.wait()


def column_parts(source, destination, parts):
    width = source.shape[1] // parts
    return [
        (source.at[:, pl.ds(at * width, width)], destination.at[:, pl.ds(at * width, width)])
        for at in range(parts)
    ]


def forward0_kernel(
    shifts_hbm,
    initial,
    gain,
    w_qkv,
    w_out,
    east,
    west,
    following_out,
    packed_out,
    weights_out,
    scaled_out,
    spread_out,
    shifts,
    ext,
    state,
    normed,
    packed,
    mixed,
    sems,
):
    small = start_copies(sems, 0, [(shifts_hbm, shifts)])
    fill(ext, initial, east[EAST_INITIAL:, :].astype(F32)[:INITIAL_ROWS], WIN)
    before = west[...].astype(F32)
    for row in range(LAT):
        ext[row, 0:WIN, :] = before[row * WIN : (row + 1) * WIN]
    wait_all(small)
    lat_shift = shifts[0, 0]
    for row in range(LAT):
        part = frame(ext, row, shifts[0, 1], 32)
        for window in range(4):
            state[window_rows(window, row), :] = part[window * WIN : (window + 1) * WIN]
    norm_rows(state, 4 * TOK, gain[...], normed, scaled_out, spread_out, 3 * TOK)
    for part in range(6):
        at = slice(part * 512, (part + 1) * 512)
        packed[:, at] = dot(normed[...], w_qkv[:, at]).astype(BF16)
    packed_out[...] = packed[: 3 * TOK, :]
    attend(4, packed, weights_out, mixed, lat_shift, 3)
    for part in range(4):
        at = slice(part * 256, (part + 1) * 256)
        following = state[:, at] + dot(mixed[...], w_out[:, at])
        for row in range(LAT):
            for window in range(4):
                following_out[row, window * WIN : (window + 1) * WIN, at] = following[
                    window_rows(window, row)
                ]


def forward1_kernel(
    shifts_hbm,
    noise,
    gain,
    noise_scale,
    w_qkv,
    w_out,
    before,
    east,
    sent_out,
    final,
    noise_here,
    packed,
    weights,
    scaled,
    spread,
    shifts,
    ext,
    state,
    normed,
    mixed,
    sems,
):
    small = start_copies(sems, 0, [(shifts_hbm, shifts)])
    side = east[: 2 * NOISE_ROWS, :].astype(F32)
    fill(ext, noise.at[0], side[:NOISE_ROWS], 0)
    wait_all(small)
    lat_shift, lon1 = shifts[1, 0], shifts[1, 1]
    scale = noise_scale[...]
    for row in range(LAT):
        part = frame(ext, row, lon1, 16)
        fields = frame(before, row, lon1 - shifts[0, 1] + WIN, 16)
        for window in range(2):
            rows = window_rows(window, row)
            here = part[window * WIN : (window + 1) * WIN]
            state[rows, :] = fields[window * WIN : (window + 1) * WIN] + scale * here
            noise_here[0, rows, :] = here
    fill(ext, noise.at[1], side[NOISE_ROWS:], 0)
    for row in range(LAT):
        part = frame(ext, row, lon1, 16)
        for window in range(2):
            rows = window_rows(window, row)
            here = part[window * WIN : (window + 1) * WIN]
            final[rows, :] = state[rows, :] + scale * here
            noise_here[1, rows, :] = here
    norm_rows(state, 2 * TOK, gain[...], normed, scaled, spread, 2 * TOK)
    for part in range(6):
        at = slice(part * 512, (part + 1) * 512)
        packed[:, at] = dot(normed[...], w_qkv[:, at]).astype(BF16)
    attend(2, packed, weights, mixed, lat_shift, 2)
    for part in range(4):
        at = slice(part * 256, (part + 1) * 256)
        last = final[:, at] + dot(mixed[...], w_out[:, at])
        final[:, at] = last
        sent_out[0:ROWS, at] = last.astype(BF16)
    sent_out[ROWS:SENT_ROWS, :] = east[2 * NOISE_ROWS : EAST_INITIAL, :]


def vmem():
    return pl.BlockSpec(memory_space=pltpu.VMEM)


def hbm():
    return pl.BlockSpec(memory_space=pltpu.HBM)


def cost(microseconds):
    return pl.CostEstimate(
        flops=0, bytes_accessed=int(microseconds * 3_500_000), transcendentals=0
    )


def compiler_params():
    return pltpu.CompilerParams(vmem_limit_bytes=VMEM_LIMIT)


ROWS = 2 * TOK


def saved(windows):
    return [
        ((windows * TOK, 3 * C), BF16),
        ((windows * GROUPS, TOK, SPAN), BF16),
        ((windows * TOK, C), BF16),
        ((windows * TOK, 128), F32),
    ]


def shapes(entries):
    return [jax.ShapeDtypeStruct(shape, dtype) for shape, dtype in entries]


def buffers(entries):
    return [pltpu.VMEM(shape, dtype) for shape, dtype in entries]


WEIGHTS = [((C, 3 * C), BF16), ((C, C), BF16)]


def shifts_buffers():
    return [pltpu.SMEM((2, 2), jnp.int32)]


def forward0(shifts, initial, east, west, gain, w_qkv, w_out):
    rows = 4 * TOK
    return pl.pallas_call(
        forward0_kernel,
        out_shape=shapes([((LAT, 32, C), F32)] + saved(3)),
        in_specs=[hbm()] + [vmem()] * 6,
        out_specs=[vmem()] * 5,
        scratch_shapes=shifts_buffers()
        + buffers(
            [
                ((LAT, 40, C), F32),
                ((rows, C), F32),
                ((rows, C), BF16),
                ((rows, 3 * C), BF16),
                ((rows, C), BF16),
            ]
        )
        + [pltpu.SemaphoreType.DMA((1,))],
        compiler_params=compiler_params(),
        cost_estimate=cost(5),
        name="forward0",
    )(shifts, initial, gain, w_qkv, w_out, east, west)


def forward1(shifts, before, noise, east, gain, noise_scale, w_qkv, w_out):
    return pl.pallas_call(
        forward1_kernel,
        out_shape=shapes([((SENT_ROWS, C), BF16), ((ROWS, C), F32), ((2, ROWS, C), F32)] + saved(2)),
        in_specs=[hbm()] + [vmem()] * 7,
        out_specs=[vmem()] * 7,
        scratch_shapes=shifts_buffers()
        + buffers(
            [
                ((LAT, 24, C), F32),
                ((ROWS, C), F32),
                ((ROWS, C), BF16),
                ((ROWS, C), BF16),
            ]
        )
        + [pltpu.SemaphoreType.DMA((1,))],
        compiler_params=compiler_params(),
        cost_estimate=cost(4),
        name="forward1",
    )(shifts, noise, gain, noise_scale, w_qkv, w_out, before, east)


def prepare_kernel(w_qkv_hbm, w_out_hbm, w_qkv, w_out, w_qkv_t, w_out_t, sems):
    copies = start_copies(sems, 0, column_parts(w_qkv_hbm, w_qkv, 6))
    copies += start_copies(sems, 6, column_parts(w_out_hbm, w_out, 2))
    for part in range(8):
        copies[part].wait()
        held, turned = (w_qkv, w_qkv_t) if part < 6 else (w_out, w_out_t)
        at = part % 6 * 512
        turned[at : at + 512, :] = held[:, at : at + 512].T


def prepare(w_qkv, w_out):
    return pl.pallas_call(
        prepare_kernel,
        out_shape=shapes(WEIGHTS + [((3 * C, C), BF16), ((C, C), BF16)]),
        in_specs=[hbm()] * 2,
        out_specs=[vmem()] * 4,
        scratch_shapes=[pltpu.SemaphoreType.DMA((8,))],
        compiler_params=compiler_params(),
        cost_estimate=cost(8),
        name="prepare",
    )(w_qkv, w_out)


def borders_kernel(
    initial_hbm,
    noise_hbm,
    target_hbm,
    east,
    west,
    initial,
    noise,
    target,
    sems,
):
    copies = start_copies(
        sems,
        0,
        [
            (initial_hbm.at[pl.ds(0, 4)], initial.at[pl.ds(0, 4)]),
            (initial_hbm.at[pl.ds(4, 4)], initial.at[pl.ds(4, 4)]),
            (noise_hbm.at[0], noise.at[0]),
            (noise_hbm.at[1], noise.at[1]),
            (target_hbm.at[pl.ds(0, 4)], target.at[pl.ds(0, 4)]),
            (target_hbm.at[pl.ds(4, 4)], target.at[pl.ds(4, 4)]),
        ],
    )

    def rows(held, first, columns):
        return [held[row].astype(F32)[first : first + columns] for row in range(LAT)]

    wait_all(copies[:2])
    spare = jnp.zeros((EAST_ROWS - EAST_INITIAL - INITIAL_ROWS, C), F32)
    east[EAST_INITIAL:, :] = jnp.concatenate(rows(initial, 0, 15) + [spare]).astype(BF16)
    west[...] = jnp.concatenate(rows(initial, WIN, WIN)).astype(BF16)
    wait_all(copies[2:4])
    east[: 2 * NOISE_ROWS, :] = jnp.concatenate(
        rows(noise.at[0], 0, 7) + rows(noise.at[1], 0, 7)
    ).astype(BF16)
    wait_all(copies[4:])
    mine = quarter(member_index())
    part = jnp.concatenate([target[row, 0:WIN, mine] for row in range(LAT)])
    for at in range(4):
        east[2 * NOISE_ROWS : EAST_INITIAL, at * QUARTER : (at + 1) * QUARTER] = part[
            at * PART_ROWS : (at + 1) * PART_ROWS
        ].astype(BF16)


def borders(initial, noise, target):
    return pl.pallas_call(
        borders_kernel,
        out_shape=shapes(
            [
                ((EAST_ROWS, C), BF16),
                ((TOK, C), BF16),
                ((LAT, 16, C), F32),
                ((2, LAT, 16, C), BF16),
                ((LAT, 16, C), F32),
            ]
        ),
        in_specs=[hbm()] * 3,
        out_specs=[vmem()] * 5,
        scratch_shapes=[pltpu.SemaphoreType.DMA((6,))],
        compiler_params=pltpu.CompilerParams(vmem_limit_bytes=52 * 1024 * 1024),
        cost_estimate=cost(2),
        name="borders",
    )(initial, noise, target)


def attend_back(windows, d_mixed, d_packed):
    masks = head_masks()

    def group(at, _):
        for window, (packed, weights_ref) in enumerate(windows):
            rows = slice(window * TOK, (window + 1) * TOK)
            here = lanes(at * LANES, LANES)
            queries = packed[:, here]
            keys = packed[:, lanes(C + at * LANES, LANES)]
            values = packed[:, lanes(2 * C + at * LANES, LANES)]
            d_mixed_blocks = by_head(d_mixed[rows, here], masks)
            weights = weights_ref[at]
            d_weights = dot_nt(values, d_mixed_blocks)
            d_values = dot(weights, d_mixed_blocks)
            probs = weights.astype(F32)
            centred = d_weights - jnp.sum(d_weights * probs, axis=0, keepdims=True)
            d_scores = (probs * centred * SCALE).astype(BF16)
            d_keys = dot(d_scores, by_head(queries, masks))
            d_queries = fold_heads(dot_tn(d_scores, keys), masks)
            d_packed[rows, here] = d_queries.astype(BF16)
            d_packed[rows, lanes(C + at * LANES, LANES)] = d_keys.astype(BF16)
            d_packed[rows, lanes(2 * C + at * LANES, LANES)] = d_values.astype(BF16)
        return 0

    lax.fori_loop(0, GROUPS, group, 0, unroll=GROUPS)


def saved_window(window, packed, weights, scaled, spread):
    rows = pl.ds(pl.multiple_of(window * TOK, TOK), TOK)
    groups = pl.ds(window * GROUPS, GROUPS)
    return packed.at[rows], weights.at[groups], scaled.at[rows], spread.at[rows]


def slope(difference):
    return difference * lax.rsqrt(difference * difference + SMOOTH * SMOOTH)


def step_back(d_next, windows, w_qkv_t, w_out_t, d_mixed, d_packed, d_normed):
    d_branch = d_next[...].astype(BF16)
    for part in range(4):
        at = slice(part * 256, (part + 1) * 256)
        d_mixed[:, at] = dot(d_branch, w_out_t[:, at]).astype(BF16)
    attend_back([window[:2] for window in windows], d_mixed, d_packed)
    for part in range(4):
        at = slice(part * 256, (part + 1) * 256)
        d_normed[:, at] = dot(d_packed[...], w_qkv_t[:, at])


def norm_back(at, d_next, windows, d_normed, gain):
    rows = slice(at, at + 32)
    _, _, scaled_ref, spread_ref = windows[at // TOK]
    inside = slice(at % TOK, at % TOK + 32)
    scaled = scaled_ref[inside, :].astype(F32)
    d_here = d_normed[rows, :]
    d_hat = d_here * gain
    spread = spread_ref[inside, 0:1]
    d_fields = spread * (
        d_hat
        - jnp.mean(d_hat, axis=-1, keepdims=True)
        - scaled * jnp.mean(d_hat * scaled, axis=-1, keepdims=True)
    )
    return d_next[rows, :] + d_fields, eight_rows(d_here * scaled)


def eight_rows(value):
    out = value[0:8]
    for at in range(8, value.shape[0], 8):
        out = out + value[at : at + 8]
    return out


def backward1_kernel(
    shifts_hbm,
    final,
    near,
    far,
    far_near,
    target,
    gain,
    noise,
    packed,
    weights,
    scaled,
    spread,
    w_out_t,
    w_qkv_t,
    sent,
    d_out,
    sent_out,
    head_out,
    gain_out,
    scale_out,
    shifts,
    ext,
    d_next,
    d_mixed,
    d_packed,
    d_normed,
    sems,
):
    small = start_copies(sems, 0, [(shifts_hbm, shifts)])
    me = member_index()
    for other_bits, held in enumerate((sent, near, far, far_near)):
        theirs = quarter(me ^ other_bits)
        part = held[ROWS:SENT_ROWS, :].astype(F32)
        for at in range(4):
            d_next[at * PART_ROWS : (at + 1) * PART_ROWS, theirs] = part[
                :, at * QUARTER : (at + 1) * QUARTER
            ]
    fill(ext, target, d_next[0:TOK, :], 0)
    wait_all(small)
    for row in range(LAT):
        part = frame(ext, row, shifts[1, 1], 16)
        for window in range(2):
            d_normed[window_rows(window, row), :] = part[window * WIN : (window + 1) * WIN]
    scale_total = jnp.zeros((8, C), F32)
    for at in range(0, ROWS, 32):
        rows = slice(at, at + 32)
        here = final[rows, :]
        pairs = (
            slope(here - near[rows, :].astype(F32))
            + slope(here - far[rows, :].astype(F32))
            + slope(here - far_near[rows, :].astype(F32))
        )
        seed = slope(here - d_normed[rows, :]) - pairs * (1.0 / 3.0)
        d_next[rows, :] = seed
        scale_total = scale_total + eight_rows(seed * noise[1, rows, :])
    windows = [saved_window(at, packed, weights, scaled, spread) for at in range(2)]
    step_back(d_next, windows, w_qkv_t, w_out_t, d_mixed, d_packed, d_normed)
    gain_total = jnp.zeros((8, C), F32)
    for at in range(0, ROWS, 32):
        rows = slice(at, at + 32)
        d_here, gain_part = norm_back(at, d_next, windows, d_normed, gain[...])
        d_out[rows, :] = d_here
        sent_out[rows, :] = d_here.astype(BF16)
        if at < TOK:
            head_out[rows, :] = d_here.astype(BF16)
        gain_total = gain_total + gain_part
        scale_total = scale_total + eight_rows(d_here * noise[0, rows, :])
    gain_out[...] = gain_total
    scale_out[...] = scale_total


def inner_window(shifts):
    return jnp.where(shifts[0, 1] >= shifts[1, 1], 1, 2)


def backward0_inner_kernel(
    shifts_hbm,
    gain,
    packed,
    weights,
    scaled,
    spread,
    w_out_t,
    w_qkv_t,
    d_in,
    gain_in,
    d_out,
    gain_out,
    shifts,
    ext,
    d_next,
    d_mixed,
    d_packed,
    d_normed,
    sems,
):
    small = start_copies(sems, 0, [(shifts_hbm, shifts)])
    for row in range(LAT):
        ext[row, 0:8, :] = d_in[row * WIN : (row + 1) * WIN, :]
        ext[row, 8:16, :] = d_in[TOK + row * WIN : TOK + (row + 1) * WIN, :]
    wait_all(small)
    window = inner_window(shifts)
    start = shifts[0, 1] - shifts[1, 1] + (window - 1) * WIN
    for row in range(LAT):
        d_next[row * WIN : (row + 1) * WIN, :] = frame(ext, row, start, WIN)
    windows = [saved_window(window, packed, weights, scaled, spread)]
    step_back(d_next, windows, w_qkv_t, w_out_t, d_mixed, d_packed, d_normed)
    gain_total = gain_in[...]
    for at in range(0, TOK, 32):
        d_here, gain_part = norm_back(at, d_next, windows, d_normed, gain[...])
        d_out[at : at + 32, :] = d_here
        gain_total = gain_total + gain_part
    gain_out[...] = gain_total


def backward0_outer_kernel(
    shifts_hbm,
    gain,
    packed,
    weights,
    scaled,
    spread,
    w_out_t,
    w_qkv_t,
    d_in,
    d_west,
    d_east,
    d_inner,
    gain_in,
    scale_in,
    own_out,
    sums_out,
    shifts,
    ext,
    d_next,
    d_mixed,
    d_packed,
    d_normed,
    sems,
):
    small = start_copies(sems, 0, [(shifts_hbm, shifts)])
    west, east = d_west[...].astype(F32), d_east[...].astype(F32)
    for row in range(LAT):
        here = slice(row * WIN, (row + 1) * WIN)
        there = slice(TOK + row * WIN, TOK + (row + 1) * WIN)
        ext[row, 0:8, :] = west[here]
        ext[row, 8:16, :] = west[there]
        ext[row, 16:24, :] = d_in[here, :]
        ext[row, 24:32, :] = d_in[there, :]
        ext[row, 32:40, :] = east[here]
    wait_all(small)
    lon0 = shifts[0, 1]
    inner = inner_window(shifts)
    picked = [0, 3 - inner]
    start = lon0 - shifts[1, 1] + WIN
    for row in range(LAT):
        for place, window in enumerate(picked):
            d_next[window_rows(place, row), :] = frame(ext, row, start + window * WIN, WIN)
    windows = [saved_window(window, packed, weights, scaled, spread) for window in picked]
    step_back(d_next, windows, w_qkv_t, w_out_t, d_mixed, d_packed, d_normed)
    gain_total = gain_in[...]
    for at in range(0, ROWS, 32):
        d_here, gain_part = norm_back(at, d_next, windows, d_normed, gain[...])
        d_normed[at : at + 32, :] = d_here
        if at >= TOK:
            gain_total = gain_total + gain_part
    sums = [jnp.sum(total, axis=0, keepdims=True) for total in (gain_total, scale_in[...])]
    sums = jnp.concatenate(
        [part[:, at : at + 128] for part in sums for at in range(0, C, 128)]
    ).astype(BF16)
    for copy in range(sums_out.shape[0]):
        sums_out[copy] = sums
    first = inner == 1
    for row in range(LAT):
        done = d_inner[row * WIN : (row + 1) * WIN, :]
        rest = d_normed[window_rows(1, row), :]
        ext[row, 0:8, :] = d_normed[window_rows(0, row), :]
        ext[row, 8:16, :] = jnp.where(first, done, rest)
        ext[row, 16:24, :] = jnp.where(first, rest, done)
        own_out[row] = frame(ext, row, WIN - lon0, 16)


WORK = [
    ((LAT, 24, C), F32),
    ((ROWS, C), F32),
    ((ROWS, C), BF16),
    ((ROWS, 3 * C), BF16),
    ((ROWS, C), F32),
]
SUMS = [((8, C), F32)] * 2


def backward1(shifts, final, sent, others, target, noise, held, gain, w_qkv_t, w_out_t):
    return pl.pallas_call(
        backward1_kernel,
        out_shape=shapes([((ROWS, C), F32), ((ROWS, C), BF16), ((TOK, C), BF16)] + SUMS),
        in_specs=[hbm()] + [vmem()] * 14,
        out_specs=[vmem()] * 5,
        scratch_shapes=shifts_buffers() + buffers(WORK) + [pltpu.SemaphoreType.DMA((1,))],
        compiler_params=compiler_params(),
        cost_estimate=cost(6),
        name="backward1",
    )(shifts, final, *others, target, gain, noise, *held, w_out_t, w_qkv_t, sent)


def backward0_buffers(windows, columns):
    rows = windows * TOK
    return (
        shifts_buffers()
        + buffers(
            [
                ((LAT, columns, C), F32),
                ((rows, C), F32),
                ((rows, C), BF16),
                ((rows, 3 * C), BF16),
                ((rows, C), F32),
            ]
        )
        + [pltpu.SemaphoreType.DMA((1,))]
    )


def backward0_inner(shifts, d_in, held, gain, gain_in, w_qkv_t, w_out_t):
    return pl.pallas_call(
        backward0_inner_kernel,
        out_shape=shapes([((TOK, C), F32), ((8, C), F32)]),
        in_specs=[hbm()] + [vmem()] * 9,
        out_specs=[vmem()] * 2,
        scratch_shapes=backward0_buffers(1, 16),
        compiler_params=compiler_params(),
        cost_estimate=cost(4),
        name="backward0_inner",
    )(shifts, gain, *held, w_out_t, w_qkv_t, d_in, gain_in)


def backward0_outer(copies, shifts, d_parts, held, gain, sums_in, w_qkv_t, w_out_t):
    return pl.pallas_call(
        backward0_outer_kernel,
        out_shape=shapes([((LAT, 16, C), F32), ((copies, 16, 128), BF16)]),
        in_specs=[hbm()] + [vmem()] * 13,
        out_specs=[vmem()] * 2,
        scratch_shapes=backward0_buffers(2, 40),
        compiler_params=compiler_params(),
        cost_estimate=cost(5),
        name="backward0_outer",
    )(shifts, gain, *held, w_out_t, w_qkv_t, *d_parts, *sums_in)


MEMBER = ("pair", "core")
TILE = ("far", "row", "half")


def along(value, steps):
    count = lax.axis_size(TILE)
    return lax.ppermute(value, TILE, [(at, (at + steps) % count) for at in range(count)])


def other(value, axis):
    return lax.ppermute(value, axis, [(0, 1), (1, 0)])


def total_over(copies, axes):
    return jnp.sum(lax.all_to_all(copies, axes, 0, 0).astype(F32), axis=0)


def local(initial, target, noise, w_qkv, w_out, gain, noise_scale, shifts):
    initial, noise = initial[0], noise[:, 0]
    gain_row, scale_row = gain[None], noise_scale[None]
    east, west, initial, noise, target = borders(initial, noise, target)
    east, west = along(east, -1), along(west, 1)
    prepared = prepare(w_qkv, w_out)
    east, west, prepared = lax.optimization_barrier((east, west, prepared))
    here, here_t = prepared[:2], prepared[2:]
    before, *saved0 = forward0(shifts, initial, east, west, gain_row, *here)
    sent, final, noise_here, *saved1 = forward1(
        shifts, before, noise, east, gain_row, scale_row, *here
    )
    far = other(sent, "pair")
    near = other(sent, "core")
    far_near = other(far, "core")
    d_one, d_sent, head, gain_part, scale_part = backward1(
        shifts,
        final,
        sent,
        (near, far, far_near),
        target,
        noise_here,
        saved1,
        gain_row,
        *here_t,
    )
    d_east, d_west = along(head, -1), along(d_sent, 1)
    d_inner, gain_part = backward0_inner(shifts, d_one, saved0, gain_row, gain_part, *here_t)
    near_axes = MEMBER + TILE[1:]
    state_grad, sums = backward0_outer(
        lax.axis_size(near_axes),
        shifts,
        (d_one, d_west, d_east, d_inner),
        saved0,
        gain_row,
        (gain_part, scale_part),
        *here_t,
    )
    sums = total_over(sums, near_axes).astype(BF16)
    sums = jnp.broadcast_to(sums[None], (lax.axis_size(TILE[0]),) + sums.shape)
    sums = total_over(sums, TILE[0]).reshape(2, C)
    members = lax.axis_size(MEMBER)
    factor = (members * LAT * initial.shape[1] * lax.axis_size(TILE)) ** (-0.5)
    return (state_grad[None], sums[0] * factor, sums[1] * factor)


def solution(mesh):
    members, tiles = mesh.devices.shape
    fine = Mesh(mesh.devices.reshape(members // 2, 2, tiles // 8, 4, 2), MEMBER + TILE)
    in_specs = (
        P(MEMBER, None, TILE, None),
        P(None, TILE, None),
        P(None, MEMBER, None, TILE, None),
        P(),
        P(),
        P(),
        P(),
        P(),
    )
    out_specs = (P(MEMBER, None, TILE, None), P(), P())
    return jax.shard_map(local, mesh=fine, in_specs=in_specs, out_specs=out_specs, check_vma=False)
```

time: 101 us -> 96.9 us (0.959)
  blocking collectives: 0 us -> 27.3 us
  starting transfers between devices: 29.2 us -> 13.2 us
  waiting for transfers between devices: 31.8 us -> 19.2 us
  Pallas kernels: 27 us -> 29.8 us
  between operations: 3.37 us -> 0.73 us
  local copies, waits for them, and re-layouts: 6.4 us -> 4.4 us
    all_to_all x0 -> x2, blocking collectives: none -> 27.3 us  [total_over(): return jnp.sum(lax.all_to_all(copies, axes, 0, 0).astype(F32), axis=0)]
    all_to_all x2 -> x0, starting transfers between devices: 14.5 us -> none  [total_over(): return jnp.sum(lax.all_to_all(copies, axes, 0, 0), axis=0)]
    all_to_all x2 -> x0, waiting for transfers between devices: 11.7 us -> none  [total_over(): return jnp.sum(lax.all_to_all(copies, axes, 0, 0), axis=0)]
    pallas_call x5 -> x6, Pallas kernels: 23 us -> 25.9 us  [the longest x1 6.15 us: backward0_outer(): pl.pallas_call(backward0_outer_kernel, out_shape=shapes([((LAT, 16, C), F...]
    ppermute x4, waiting for transfers between devices: 11.7 us -> 10.2 us  [along(): lax.ppermute(value, TILE, [(at, (at + steps) % count) for at in range(cou...]
    ppermute x4, starting transfers between devices: 13.2 us -> 11.6 us  [along(): lax.ppermute(value, TILE, [(at, (at + steps) % count) for at in range(cou...]
    broadcast_in_dim x2 -> x1, local copies, waits for them, and re-layouts: 1.41 us -> 0.01 us  [local(): sums = jnp.broadcast_to(sums[None], (lax.axis_size(TILE[0]),) + sums.shape)]
    unnamed x16 -> x12, local copies, waits for them, and re-layouts: 4.41 us -> 4.39 us
  transfers between devices with their start and end apart: 9 -> 7, of which waited for: 6 -> 4; matrix products, arithmetic and copies ran while one was open for 2% -> 0% of each run, Pallas kernels for 4% -> 8%
where the time goes in v4:
time: 96.9 us; the launch traced here: 95.3 us
  Pallas kernels  29.8 us (31%)
  blocking collectives  27.3 us (28%)
  waiting for transfers between devices  19.2 us (20%)
  starting transfers between devices  13.2 us (14%)
  local copies, waits for them, and re-layouts  4.4 us (5%)
    all_to_all x2, blocking collectives, total_over(): return jnp.sum(lax.all_to_all(copies, axes, 0, 0).astype(F32), axis=0)  27.3 us
    ppermute x4, starting transfers between devices, along(): lax.ppermute(value, TILE, [(at, (at + steps) % count) for at in range(cou...  11.6 us
    ppermute x4, waiting for transfers between devices, along(): lax.ppermute(value, TILE, [(at, (at + steps) % count) for at in range(cou...  10.2 us
    ppermute x3, waiting for transfers between devices, other(): return lax.ppermute(value, axis, [(0, 1), (1, 0)])  9.04 us
    pallas_call x1, Pallas kernels, backward0_outer(): pl.pallas_call(backward0_outer_kernel, out_shape=shapes([((LAT, 16, C), F...  6.15 us
    pallas_call x1, Pallas kernels, backward1(): pl.pallas_call(backward1_kernel, out_shape=shapes([((ROWS, C), F32), ((RO...  5.46 us
    pallas_call x1, Pallas kernels, forward0(): pl.pallas_call(forward0_kernel, out_shape=shapes([((LAT, 32, C), F32)] +...  5.03 us
    unnamed x12, local copies, waits for them, and re-layouts  4.39 us
  transfers between devices with their start and end apart: 7, of which 4 were waited for; matrix products, arithmetic and copies ran while one was open for 0% of the time, Pallas kernels for 8%

profile of v4, /device:TPU:32, one launch (start us, length us, event | category | flops | bytes accessed | tf_op | source)
XLA Modules:
  0.0 95.3 jit_solution(5327104269799288469)
XLA Ops:
  0.6 2.2 %borders.1 = (bf16[256,1024]{1,0:T(8,128)(2,1)S(1)}, bf16[64,1024]{1,0:T(8,128)(2,1)S(1)}, f32[8,16,1024]{2,1,0:T(8,128)S(1)}, bf16[2,8,16,1024]{3,2,1,0:T(8,128)(2,1)S(1)}, f32[8,16,1024]{2,1,0:T(8,128)}) custom-call(f32[8,16,1024]{2,1,0:T(8,128)} %bitcast.15, bf16[2,8,16,1024]{3,2,1,0:T(8,128)(2,1)} %bitcast.16, f32[8,16,1024]{2,1,0:T(8,128)} %target_hbm.1), custom_call_target="tpu_custom_call" | custom-call | bytes 7000000 | tf_op jit(solution)/shard_map/borders/pallas_call | solution.py:427
  2.8 5.0 %collective-permute-start = (bf16[256,1024]{1,0:T(8,128)(2,1)S(1)}, bf16[256,1024]{1,0:T(8,128)(2,1)S(1)}, u32[]{:S(2)}, u32[]{:S(2)}) collective-permute-start(bf16[256,1024]{1,0:T(8,128)(2,1)S(1)} %get-tuple-element.40), channel_id=1, source_target_pairs={{0,63},{1,0},{2,1},{3,2},{4,3},{5,4},{6,5},{7,6},{8,7},{9,8},{10,9... | collective-permute-start | bytes 1572872 | tf_op jit(solution)/shard_map/ppermute | solution.py:773
  7.8 0.0 collective-permute-start.1
  7.8 0.0 copy-start
  7.8 2.8 %copy-done = bf16[1024,3072]{1,0:T(8,128)(2,1)S(1)} copy-done((bf16[1024,3072]{1,0:T(8,128)(2,1)S(1)}, bf16[1024,3072]{1,0:T(8,128)(2,1)}, u32[]{:S(2)}) %copy-start) | copy-done | bytes 6291480
  10.6 0.0 copy-start.1
  10.6 1.6 %copy-done.1 = bf16[1024,1024]{1,0:T(8,128)(2,1)S(1)} copy-done((bf16[1024,1024]{1,0:T(8,128)(2,1)S(1)}, bf16[1024,1024]{1,0:T(8,128)(2,1)}, u32[]{:S(2)}) %copy-start.1) | copy-done | bytes 2097176
  12.2 0.0 copy-start.3
  12.2 0.0 copy-start.4
  12.2 4.0 %prepare.1 = (bf16[1024,3072]{1,0:T(8,128)(2,1)S(1)}, bf16[1024,1024]{1,0:T(8,128)(2,1)S(1)}, bf16[3072,1024]{1,0:T(8,128)(2,1)S(1)}, bf16[1024,1024]{1,0:T(8,128)(2,1)S(1)}) custom-call(bf16[1024,3072]{1,0:T(8,128)(2,1)S(1)} %copy-done, bf16[1024,1024]{1,0:T(8,128)(2,1)S(1)} %copy-done.1), custom_call_target="tpu_custom_call" | custom-call | bytes 28000000 | tf_op jit(solution)/shard_map/prepare/pallas_call | solution.py:370
  16.2 4.8 %collective-permute-done.1.west = bf16[64,1024]{1,0:T(8,128)(2,1)S(1)} collective-permute-done((bf16[64,1024]{1,0:T(8,128)(2,1)S(1)}, bf16[64,1024]{1,0:T(8,128)(2,1)S(1)}, u32[]{:S(2)}, u32[]{:S(2)}) %collective-permute-start.1) | collective-permute-done | bytes 131104 | tf_op jit(solution)/shard_map/ppermute | solution.py:773
  21.0 0.0 collective-permute-done.east
  21.0 0.0 copy-done.3
  21.0 0.0 copy-done.4
  21.0 0.0 copy-start.5
  21.0 5.0 %forward0.1 = (f32[8,32,1024]{2,1,0:T(8,128)S(1)}, bf16[192,3072]{1,0:T(8,128)(2,1)S(1)}, bf16[24,64,256]{2,1,0:T(8,128)(2,1)S(1)}, bf16[192,1024]{1,0:T(8,128)(2,1)S(1)}, f32[192,128]{1,0:T(8,128)S(1)}) custom-call(s32[2,2]{1,0:T(2,128)S(1)} %copy-done.4, f32[8,16,1024]{2,1,0:T(8,128)S(1)} %get-tuple-element.39.initial, f32[1,1024]{1,0:T(1,128)S(1)} %bitcast.9, ...), custom_call_target="tpu_custom_call" | custom-call | bytes 17500000 | tf_op jit(solution)/shard_map/forward0/pallas_call | solution.py:315
  26.0 0.0 copy-done.5
  26.0 0.0 copy-start.2
  26.1 3.3 %forward1.1 = (bf16[144,1024]{1,0:T(8,128)(2,1)S(1)}, f32[128,1024]{1,0:T(8,128)S(1)}, f32[2,128,1024]{2,1,0:T(8,128)S(1)}, bf16[128,3072]{1,0:T(8,128)(2,1)S(1)...) custom-call(s32[2,2]{1,0:T(2,128)S(1)} %copy-done.4, ...), custom_call_target="tpu_custom_call" | custom-call | bytes 14000000 | tf_op jit(solution)/shard_map/forward1/pallas_call | solution.py:338
  29.4 1.5 %collective-permute-start.3 = (bf16[144,1024]{1,0:T(8,128)(2,1)S(1)}, bf16[144,1024]{1,0:T(8,128)(2,1)S(1)}, u32[]{:S(2)}, u32[]{:S(2)}) collective-permute-start(bf16[144,1024]{1,0:T(8,128)(2,1)S(1)} %get-tuple-element.59.sent), channel_id=1, source_target_pairs={{0,128},{128,0},{1,129},{129,1},{2,130},{130,2},{3,131},{131,3},{4... | collective-permute-start | bytes 884744 | tf_op jit(solution)/shard_map/ppermute | solution.py:777
  30.9 0.0 collective-permute-start.2
  30.9 7.5 %collective-permute-done.3.far = bf16[144,1024]{1,0:T(8,128)(2,1)S(1)} collective-permute-done((bf16[144,1024]{1,0:T(8,128)(2,1)S(1)}, bf16[144,1024]{1,0:T(8,128)(2,1)S(1)}, u32[]{:S(2)}, u32[]{:S(2)}) %collective-permute-start.3) | collective-permute-done | bytes 294944 | tf_op jit(solution)/shard_map/ppermute | solution.py:777
  38.4 0.0 collective-permute-start.4
  38.4 0.0 collective-permute-done.2.near
  38.4 1.6 %collective-permute-done.4.far_near = bf16[144,1024]{1,0:T(8,128)(2,1)S(1)} collective-permute-done((bf16[144,1024]{1,0:T(8,128)(2,1)S(1)}, bf16[144,1024]{1,0:T(8,128)(2,1)S(1)}, u32[]{:S(2)}, u32[]{:S(2)}) %collective-permute-start.4) | collective-permute-done | bytes 294944 | tf_op jit(solution)/shard_map/ppermute | solution.py:777
  40.0 0.0 copy-done.2
  40.0 5.5 %backward1.1 = (f32[128,1024]{1,0:T(8,128)S(1)}, bf16[128,1024]{1,0:T(8,128)(2,1)S(1)}, bf16[64,1024]{1,0:T(8,128)(2,1)S(1)}, f32[8,1024]{1,0:T(8,128)S(1)}, f32[8,1024]{1,0:T(8,128)S(1)}) custom-call(s32[2,2]{1,0:T(2,128)S(1)} %copy-done.4, f32[128,1024]{1,0:T(8,128)S(1)} %get-tuple-element.58.final, bf16[144,1024]{1,0:T(8,128)(2,1)S(1)} %collective-permute-done.2.near, ...), custom_call_target="tpu_custom_call" | custom-call | bytes 21000000 | tf_op jit(solution)/shard_map/backward1/pallas_call | solution.py:712
  45.4 4.1 %collective-permute-start.5 = (bf16[128,1024]{1,0:T(8,128)(2,1)S(1)}, bf16[128,1024]{1,0:T(8,128)(2,1)S(1)}, u32[]{:S(2)}, u32[]{:S(2)}) collective-permute-start(bf16[128,1024]{1,0:T(8,128)(2,1)S(1)} %get-tuple-element.67), channel_id=1, source_target_pairs={{0,1},{1,2},{2,3},{3,4},{4,5},{5,6},{6,7},{7,8},{8,9},{9,10},{10,1... | collective-permute-start | bytes 786440 | tf_op jit(solution)/shard_map/ppermute | solution.py:773
  49.5 2.5 %collective-permute-start.6 = (bf16[64,1024]{1,0:T(8,128)(2,1)S(1)}, bf16[64,1024]{1,0:T(8,128)(2,1)S(1)}, u32[]{:S(2)}, u32[]{:S(2)}) collective-permute-start(bf16[64,1024]{1,0:T(8,128)(2,1)S(1)} %get-tuple-element.68), channel_id=1, source_target_pairs={{0,63},{1,0},{2,1},{3,2},{4,3},{5,4},{6,5},{7,6},{8,7},{9,8},{10,9... | collective-permute-start | bytes 393224 | tf_op jit(solution)/shard_map/ppermute | solution.py:773
  52.0 3.7 %backward0_inner.1 = (f32[64,1024]{1,0:T(8,128)S(1)}, f32[8,1024]{1,0:T(8,128)S(1)}) custom-call(s32[2,2]{1,0:T(2,128)S(1)} %copy-done.4, f32[1,1024]{1,0:T(1,128)S(1)} %bitcast.12, bf16[192,3072]{1,0:T(8,128)(2,1)S(1)} %get-tuple-element.50.packed, bf16[24,64,256]{2,1,0:T(8,128)(2,1)S(1)} %get-tuple-element.51.weights, ...), custom_call_target="tpu_custom_call" | custom-call | bytes 14000000 | tf_op jit(solution)/shard_map/backward0_inner/pallas_call | solution.py:742
  55.8 5.4 %collective-permute-done.6.d_east = bf16[64,1024]{1,0:T(8,128)(2,1)S(1)} collective-permute-done((bf16[64,1024]{1,0:T(8,128)(2,1)S(1)}, bf16[64,1024]{1,0:T(8,128)(2,1)S(1)}, u32[]{:S(2)}, u32[]{:S(2)}) %collective-permute-start.6) | collective-permute-done | bytes 131104 | tf_op jit(solution)/shard_map/ppermute | solution.py:773
  61.2 0.0 collective-permute-done.5.d_west
  61.2 6.2 %backward0_outer.1 = (f32[8,16,1024]{2,1,0:T(8,128)}, bf16[32,16,128]{2,1,0:T(8,128)(2,1)S(1)}) custom-call(s32[2,2]{1,0:T(2,128)S(1)} %copy-done.4, f32[1,1024]{1,0:T(1,128)S(1)} %bitcast.13, bf16[192,3072]{1,0:T(8,128)(2,1)S(1)} %get-tuple-element.50.packed, bf16[24,64,256]{2,1,0:T(8,128)(2,1)S(1)} %get-tuple-element.51.weights, ...), custom_call_target="tpu_custom_call" | custom-call | bytes 17500000 | tf_op jit(solution)/shard_map/backward0_outer/pallas_call | solution.py:755
  67.3 12.3 %all_to_all.10 = bf16[32,16,128]{2,1,0:T(8,128)(2,1)S(1)} all-to-all(bf16[32,16,128]{2,1,0:T(8,128)(2,1)S(1)} %get-tuple-element.74), channel_id=1, replica_groups=mesh['pair'=2,'core'=2,'far'=8,'row'=4,'half'=2] {'pair','core','row','h..., dimensions={0} | all-to-all | bytes 262144 | tf_op jit(solution)/shard_map/all_to_all | solution.py:781
  79.7 14.9 %all_to_all.11 = bf16[8,16,128]{2,1,0:T(8,128)(2,1)S(1)} all-to-all(bf16[8,16,128]{2,1,0:T(8,128)(2,1)S(1)} %broadcast_in_dim.18), channel_id=1, replica_groups=mesh['pair'=2,'core'=2,'far'=8,'row'=4,'half'=2] {'far'}, dimensions={0} | all-to-all | bytes 65536 | tf_op jit(solution)/shard_map/all_to_all | solution.py:781
  94.7 0.6 fusion
  (3 shorter events, 0.1 us)
Async XLA Ops:
  2.8 18.2 %collective-permute-start = (bf16[256,1024]{1,0:T(8,128)(2,1)S(1)}, bf16[256,1024]{1,0:T(8,128)(2,1)S(1)}, u32[]{:S(2)}, u32[]{:S(2)}) collective-permute-start(bf16[256,1024]{1,0:T(8,128)(2,1)S(1)} %get-tuple-element.40), channel_id=1, source_target_pairs={{0,63},{1,0},{2,1},{3,2},{4,3},{5,4},{6,5},{7,6},{8,7},{9,8},{10,9... | collective-permute-start | bytes 1572872 | tf_op jit(solution)/shard_map/ppermute | solution.py:773
  7.8 13.2 %collective-permute-start.1 = (bf16[64,1024]{1,0:T(8,128)(2,1)S(1)}, bf16[64,1024]{1,0:T(8,128)(2,1)S(1)}, u32[]{:S(2)}, u32[]{:S(2)}) collective-permute-start(bf16[64,1024]{1,0:T(8,128)(2,1)S(1)} %get-tuple-element.41), channel_id=1, source_target_pairs={{0,1},{1,2},{2,3},{3,4},{4,5},{5,6},{6,7},{7,8},{8,9},{9,10},{10,1... | collective-permute-start | bytes 393224 | tf_op jit(solution)/shard_map/ppermute | solution.py:773
  7.8 2.8 %copy-start = (bf16[1024,3072]{1,0:T(8,128)(2,1)S(1)}, bf16[1024,3072]{1,0:T(8,128)(2,1)}, u32[]{:S(2)}) copy-start(bf16[1024,3072]{1,0:T(8,128)(2,1)} %w_qkv_hbm.1) | copy-start | bytes 18874372
  10.6 1.6 %copy-start.1 = (bf16[1024,1024]{1,0:T(8,128)(2,1)S(1)}, bf16[1024,1024]{1,0:T(8,128)(2,1)}, u32[]{:S(2)}) copy-start(bf16[1024,1024]{1,0:T(8,128)(2,1)} %w_out_hbm.1) | copy-start | bytes 6291460
  12.2 8.8 %copy-start.3 = (f32[1024]{0:T(1024)S(1)}, f32[1024]{0:T(1024)}, u32[]{:S(2)}) copy-start(f32[1024]{0:T(1024)} %param.13) | copy-start | bytes 12292
  12.2 8.8 %copy-start.4 = (s32[2,2]{1,0:T(2,128)S(1)}, s32[2,2]{1,0:T(2,128)}, u32[]{:S(2)}) copy-start(s32[2,2]{1,0:T(2,128)} %shifts_hbm.9) | copy-start | bytes 52
  21.0 5.0 %copy-start.5 = (f32[1024]{0:T(1024)S(1)}, f32[1024]{0:T(1024)}, u32[]{:S(2)}) copy-start(f32[1024]{0:T(1024)} %param.14) | copy-start | bytes 12292
  26.0 13.9 %copy-start.2 = (f32[8,16,1024]{2,1,0:T(8,128)S(1)}, f32[8,16,1024]{2,1,0:T(8,128)}, u32[]{:S(2)}) copy-start(f32[8,16,1024]{2,1,0:T(8,128)} %get-tuple-element.60.target) | copy-start | bytes 1572868
  29.4 9.0 %collective-permute-start.3 = (bf16[144,1024]{1,0:T(8,128)(2,1)S(1)}, bf16[144,1024]{1,0:T(8,128)(2,1)S(1)}, u32[]{:S(2)}, u32[]{:S(2)}) collective-permute-start(bf16[144,1024]{1,0:T(8,128)(2,1)S(1)} %get-tuple-element.59.sent), channel_id=1, source_target_pairs={{0,128},{128,0},{1,129},{129,1},{2,130},{130,2},{3,131},{131,3},{4... | collective-permute-start | bytes 884744 | tf_op jit(solution)/shard_map/ppermute | solution.py:777
  30.9 7.5 %collective-permute-start.2 = (bf16[144,1024]{1,0:T(8,128)(2,1)S(1)}, bf16[144,1024]{1,0:T(8,128)(2,1)S(1)}, u32[]{:S(2)}, u32[]{:S(2)}) collective-permute-start(bf16[144,1024]{1,0:T(8,128)(2,1)S(1)} %get-tuple-element.59.sent), channel_id=1, source_target_pairs={{0,64},{64,0},{1,65},{65,1},{2,66},{66,2},{3,67},{67,3},{4,68},{68... | collective-permute-start | bytes 884744 | tf_op jit(solution)/shard_map/ppermute | solution.py:777
  38.4 1.6 %collective-permute-start.4 = (bf16[144,1024]{1,0:T(8,128)(2,1)S(1)}, bf16[144,1024]{1,0:T(8,128)(2,1)S(1)}, u32[]{:S(2)}, u32[]{:S(2)}) collective-permute-start(bf16[144,1024]{1,0:T(8,128)(2,1)S(1)} %collective-permute-done.3.far), channel_id=1, source_target_pairs={{0,64},{64,0},{1,65},{65,1},{2,66},{66,2},{3,67},{67,3},{4,68},{68... | collective-permute-start | bytes 884744 | tf_op jit(solution)/shard_map/ppermute | solution.py:777
  45.4 15.7 %collective-permute-start.5 = (bf16[128,1024]{1,0:T(8,128)(2,1)S(1)}, bf16[128,1024]{1,0:T(8,128)(2,1)S(1)}, u32[]{:S(2)}, u32[]{:S(2)}) collective-permute-start(bf16[128,1024]{1,0:T(8,128)(2,1)S(1)} %get-tuple-element.67), channel_id=1, source_target_pairs={{0,1},{1,2},{2,3},{3,4},{4,5},{5,6},{6,7},{7,8},{8,9},{9,10},{10,1... | collective-permute-start | bytes 786440 | tf_op jit(solution)/shard_map/ppermute | solution.py:773
  49.5 11.7 %collective-permute-start.6 = (bf16[64,1024]{1,0:T(8,128)(2,1)S(1)}, bf16[64,1024]{1,0:T(8,128)(2,1)S(1)}, u32[]{:S(2)}, u32[]{:S(2)}) collective-permute-start(bf16[64,1024]{1,0:T(8,128)(2,1)S(1)} %get-tuple-element.68), channel_id=1, source_target_pairs={{0,63},{1,0},{2,1},{3,2},{4,3},{5,4},{6,5},{7,6},{8,7},{9,8},{10,9... | collective-permute-start | bytes 393224 | tf_op jit(solution)/shard_map/ppermute | solution.py:773

commit v5 on v4

--- a/solution.py
+++ b/solution.py
@@ -41,9 +41,14 @@
     return [lane == head for head in range(GROUP)]
 
 
-def by_head(value, masks):
-    zero = jnp.zeros_like(value)
-    return jnp.concatenate([jnp.where(mask, value, zero) for mask in masks], axis=0)
+def head_blocks():
+    block = lax.broadcasted_iota(jnp.int32, (SPAN, LANES), 0) // TOK
+    lane = lax.broadcasted_iota(jnp.int32, (SPAN, LANES), 1) // HEAD
+    return jnp.where(block == lane, 1.0, 0.0).astype(BF16)
+
+
+def by_head(value, blocks):
+    return jnp.concatenate([value] * GROUP, axis=0) * blocks
 
 
 def fold_heads(stacked, masks):
@@ -75,10 +80,10 @@
 NOISE_ROWS = LAT * 7
 PART_ROWS = TOK // 4
 EAST_INITIAL = 2 * NOISE_ROWS + PART_ROWS
-INITIAL_ROWS = LAT * 15
-EAST_ROWS = 256
+EAST_ROWS = EAST_INITIAL + LAT * 14
 SENT_ROWS = 2 * TOK + PART_ROWS
 QUARTER = C // 4
+TO_EAST, TO_WEST = 14, 6
 
 
 def member_index():
@@ -92,6 +97,11 @@
 def frame(ext, row, start, columns):
     held = ext.shape[1]
     return pltpu.roll(ext[row], lax.rem(held - start, held), 0)[:columns]
+
+
+def frame_of_eight(ext, row, start):
+    base = pl.multiple_of(lax.div(start, 8) * 8, 8)
+    return pltpu.roll(ext[row, pl.ds(base, 16), :], lax.rem(16 - lax.rem(start, 8), 16), 0)[:8]
 
 
 def norm_rows(x_ref, rows, gain, normed_ref, scaled_ref, spread_ref, saved):
@@ -108,7 +118,7 @@
 
 
 def attend(windows, packed_ref, weights_ref, mixed_ref, lat_shift, saved):
-    masks = head_masks()
+    masks, blocks = head_masks(), head_blocks()
     allowed = lat_mask(lat_shift)
 
     def group(at, _):
@@ -117,7 +127,7 @@
             queries = packed_ref[rows, lanes(at * LANES, LANES)]
             keys = packed_ref[rows, lanes(C + at * LANES, LANES)]
             values = packed_ref[rows, lanes(2 * C + at * LANES, LANES)]
-            scores = dot_nt(keys, by_head(queries, masks))
+            scores = dot_nt(keys, by_head(queries, blocks))
             scores = jnp.where(allowed, scores, -1e9 / SCALE)
             highest = jnp.max(scores, axis=0, keepdims=True)
             raised = jnp.exp((scores - highest) * SCALE)
@@ -181,7 +191,8 @@
     sems,
 ):
     small = start_copies(sems, 0, [(shifts_hbm, shifts)])
-    fill(ext, initial, east[EAST_INITIAL:, :].astype(F32)[:INITIAL_ROWS], WIN)
+    fill(ext, initial, east[EAST_INITIAL:, :].astype(F32), WIN)
+    ext[:, 38:40, :] = jnp.zeros((LAT, 2, C), F32)
     before = west[...].astype(F32)
     for row in range(LAT):
         ext[row, 0:WIN, :] = before[row * WIN : (row + 1) * WIN]
@@ -407,8 +418,7 @@
         return [held[row].astype(F32)[first : first + columns] for row in range(LAT)]
 
     wait_all(copies[:2])
-    spare = jnp.zeros((EAST_ROWS - EAST_INITIAL - INITIAL_ROWS, C), F32)
-    east[EAST_INITIAL:, :] = jnp.concatenate(rows(initial, 0, 15) + [spare]).astype(BF16)
+    east[EAST_INITIAL:, :] = jnp.concatenate(rows(initial, 0, 14)).astype(BF16)
     west[...] = jnp.concatenate(rows(initial, WIN, WIN)).astype(BF16)
     wait_all(copies[2:4])
     east[: 2 * NOISE_ROWS, :] = jnp.concatenate(
@@ -445,7 +455,7 @@
 
 
 def attend_back(windows, d_mixed, d_packed):
-    masks = head_masks()
+    masks, blocks = head_masks(), head_blocks()
 
     def group(at, _):
         for window, (packed, weights_ref) in enumerate(windows):
@@ -454,14 +464,14 @@
             queries = packed[:, here]
             keys = packed[:, lanes(C + at * LANES, LANES)]
             values = packed[:, lanes(2 * C + at * LANES, LANES)]
-            d_mixed_blocks = by_head(d_mixed[rows, here], masks)
+            d_mixed_blocks = by_head(d_mixed[rows, here], blocks)
             weights = weights_ref[at]
             d_weights = dot_nt(values, d_mixed_blocks)
             d_values = dot(weights, d_mixed_blocks)
             probs = weights.astype(F32)
             centred = d_weights - jnp.sum(d_weights * probs, axis=0, keepdims=True)
             d_scores = (probs * centred * SCALE).astype(BF16)
-            d_keys = dot(d_scores, by_head(queries, masks))
+            d_keys = dot(d_scores, by_head(queries, blocks))
             d_queries = fold_heads(dot_tn(d_scores, keys), masks)
             d_packed[rows, here] = d_queries.astype(BF16)
             d_packed[rows, lanes(C + at * LANES, LANES)] = d_keys.astype(BF16)
@@ -578,13 +588,17 @@
         rows = slice(at, at + 32)
         d_here, gain_part = norm_back(at, d_next, windows, d_normed, gain[...])
         d_out[rows, :] = d_here
-        sent_out[rows, :] = d_here.astype(BF16)
-        if at < TOK:
-            head_out[rows, :] = d_here.astype(BF16)
         gain_total = gain_total + gain_part
         scale_total = scale_total + eight_rows(d_here * noise[0, rows, :])
     gain_out[...] = gain_total
     scale_out[...] = scale_total
+    first = [d_out[window_rows(0, row), :] for row in range(LAT)]
+    second = [d_out[window_rows(1, row), :] for row in range(LAT)]
+    head_out[...] = jnp.concatenate([part[:TO_WEST] for part in first]).astype(BF16)
+    skipped = 16 - TO_EAST
+    sent_out[...] = jnp.concatenate(
+        [part for row in range(LAT) for part in (first[row][skipped:], second[row])]
+    ).astype(BF16)
 
 
 def inner_window(shifts):
@@ -661,11 +675,10 @@
     for row in range(LAT):
         here = slice(row * WIN, (row + 1) * WIN)
         there = slice(TOK + row * WIN, TOK + (row + 1) * WIN)
-        ext[row, 0:8, :] = west[here]
-        ext[row, 8:16, :] = west[there]
+        ext[row, 16 - TO_EAST : 16, :] = west[row * TO_EAST : (row + 1) * TO_EAST]
         ext[row, 16:24, :] = d_in[here, :]
         ext[row, 24:32, :] = d_in[there, :]
-        ext[row, 32:40, :] = east[here]
+        ext[row, 32 : 32 + TO_WEST, :] = east[row * TO_WEST : (row + 1) * TO_WEST]
     wait_all(small)
     lon0 = shifts[0, 1]
     inner = inner_window(shifts)
@@ -673,7 +686,7 @@
     start = lon0 - shifts[1, 1] + WIN
     for row in range(LAT):
         for place, window in enumerate(picked):
-            d_next[window_rows(place, row), :] = frame(ext, row, start + window * WIN, WIN)
+            d_next[window_rows(place, row), :] = frame_of_eight(ext, row, start + window * WIN)
     windows = [saved_window(window, packed, weights, scaled, spread) for window in picked]
     step_back(d_next, windows, w_qkv_t, w_out_t, d_mixed, d_packed, d_normed)
     gain_total = gain_in[...]
@@ -711,7 +724,9 @@
 def backward1(shifts, final, sent, others, target, noise, held, gain, w_qkv_t, w_out_t):
     return pl.pallas_call(
         backward1_kernel,
-        out_shape=shapes([((ROWS, C), F32), ((ROWS, C), BF16), ((TOK, C), BF16)] + SUMS),
+        out_shape=shapes(
+            [((ROWS, C), F32), ((LAT * TO_EAST, C), BF16), ((LAT * TO_WEST, C), BF16)] + SUMS
+        ),
         in_specs=[hbm()] + [vmem()] * 14,
         out_specs=[vmem()] * 5,
         scratch_shapes=shifts_buffers() + buffers(WORK) + [pltpu.SemaphoreType.DMA((1,))],
@@ -777,8 +792,9 @@
     return lax.ppermute(value, axis, [(0, 1), (1, 0)])
 
 
-def total_over(copies, axes):
-    return jnp.sum(lax.all_to_all(copies, axes, 0, 0).astype(F32), axis=0)
+def total_over(copies, axes, groups=None):
+    parts = lax.all_to_all(copies, axes, 0, 0, axis_index_groups=groups)
+    return jnp.sum(parts.astype(F32), axis=0)
 
 
 def local(initial, target, noise, w_qkv, w_out, gain, noise_scale, shifts):
@@ -820,8 +836,9 @@
         *here_t,
     )
     sums = total_over(sums, near_axes).astype(BF16)
-    sums = jnp.broadcast_to(sums[None], (lax.axis_size(TILE[0]),) + sums.shape)
-    sums = total_over(sums, TILE[0]).reshape(2, C)
+    count = lax.axis_size(TILE[0])
+    sums = jnp.broadcast_to(sums[None], (count,) + sums.shape)
+    sums = total_over(sums, TILE[0], [list(range(count))[::-1]]).reshape(2, C)
     members = lax.axis_size(MEMBER)
     factor = (members * LAT * initial.shape[1] * lax.axis_size(TILE)) ** (-0.5)
     return (state_grad[None], sums[0] * factor, sums[1] * factor)

time: 96.9 us -> 93 us (0.960)
  waiting for transfers between devices: 19.2 us -> 17.1 us
  blocking collectives: 27.3 us -> 25.7 us
    ppermute x4, waiting for transfers between devices: 10.2 us -> 8.08 us  [along(): lax.ppermute(value, TILE, [(at, (at + steps) % count) for at in range(cou...]
    all_to_all x2, blocking collectives: 27.3 us -> 25.7 us  [total_over(): parts = lax.all_to_all(copies, axes, 0, 0, axis_index_groups=groups)]
where the time goes in v5:
time: 93 us; the launch traced here: 91.4 us
  Pallas kernels  29.6 us (32%)
  blocking collectives  25.7 us (28%)
  waiting for transfers between devices  17.1 us (18%)
  starting transfers between devices  13.2 us (14%)
  local copies, waits for them, and re-layouts  4.4 us (5%)
    all_to_all x2, blocking collectives, total_over(): parts = lax.all_to_all(copies, axes, 0, 0, axis_index_groups=groups)  25.7 us
    ppermute x4, starting transfers between devices, along(): lax.ppermute(value, TILE, [(at, (at + steps) % count) for at in range(cou...  11.6 us
    ppermute x3, waiting for transfers between devices, other(): return lax.ppermute(value, axis, [(0, 1), (1, 0)])  9.04 us
    ppermute x4, waiting for transfers between devices, along(): lax.ppermute(value, TILE, [(at, (at + steps) % count) for at in range(cou...  8.08 us
    pallas_call x1, Pallas kernels, backward0_outer(): pl.pallas_call(backward0_outer_kernel, out_shape=shapes([((LAT, 16, C), F...  5.9 us
    pallas_call x1, Pallas kernels, backward1(): pl.pallas_call(backward1_kernel, out_shape=shapes([((ROWS, C), F32), ((LA...  5.55 us
    pallas_call x1, Pallas kernels, forward0(): pl.pallas_call(forward0_kernel, out_shape=shapes([((LAT, 32, C), F32)] +...  4.98 us
    unnamed x12, local copies, waits for them, and re-layouts  4.39 us
  transfers between devices with their start and end apart: 7, of which 4 were waited for; matrix products, arithmetic and copies ran while one was open for 0% of the time, Pallas kernels for 8%

profile of v5, /device:TPU:32, one launch (start us, length us, event | category | flops | bytes accessed | tf_op | source)
XLA Modules:
  0.0 91.4 jit_solution(1055027910286248946)
XLA Ops:
  0.6 2.2 %borders.1 = (bf16[240,1024]{1,0:T(8,128)(2,1)S(1)}, bf16[64,1024]{1,0:T(8,128)(2,1)S(1)}, f32[8,16,1024]{2,1,0:T(8,128)S(1)}, bf16[2,8,16,1024]{3,2,1,0:T(8,128)(2,1)S(1)}, f32[8,16,1024]{2,1,0:T(8,128)}) custom-call(f32[8,16,1024]{2,1,0:T(8,128)} %bitcast.15, bf16[2,8,16,1024]{3,2,1,0:T(8,128)(2,1)} %bitcast.16, f32[8,16,1024]{2,1,0:T(8,128)} %target_hbm.1), custom_call_target="tpu_custom_call" | custom-call | bytes 7000000 | tf_op jit(solution)/shard_map/borders/pallas_call | solution.py:437
  2.8 5.0 %collective-permute-start = (bf16[240,1024]{1,0:T(8,128)(2,1)S(1)}, bf16[240,1024]{1,0:T(8,128)(2,1)S(1)}, u32[]{:S(2)}, u32[]{:S(2)}) collective-permute-start(bf16[240,1024]{1,0:T(8,128)(2,1)S(1)} %get-tuple-element.40), channel_id=1, source_target_pairs={{0,63},{1,0},{2,1},{3,2},{4,3},{5,4},{6,5},{7,6},{8,7},{9,8},{10,9... | collective-permute-start | bytes 1474568 | tf_op jit(solution)/shard_map/ppermute | solution.py:788
  7.8 0.0 collective-permute-start.1
  7.8 0.0 copy-start
  7.8 2.8 %copy-done = bf16[1024,3072]{1,0:T(8,128)(2,1)S(1)} copy-done((bf16[1024,3072]{1,0:T(8,128)(2,1)S(1)}, bf16[1024,3072]{1,0:T(8,128)(2,1)}, u32[]{:S(2)}) %copy-start) | copy-done | bytes 6291480
  10.6 0.0 copy-start.1
  10.6 1.6 %copy-done.1 = bf16[1024,1024]{1,0:T(8,128)(2,1)S(1)} copy-done((bf16[1024,1024]{1,0:T(8,128)(2,1)S(1)}, bf16[1024,1024]{1,0:T(8,128)(2,1)}, u32[]{:S(2)}) %copy-start.1) | copy-done | bytes 2097176
  12.2 0.0 copy-start.3
  12.2 0.0 copy-start.4
  12.2 4.0 %prepare.1 = (bf16[1024,3072]{1,0:T(8,128)(2,1)S(1)}, bf16[1024,1024]{1,0:T(8,128)(2,1)S(1)}, bf16[3072,1024]{1,0:T(8,128)(2,1)S(1)}, bf16[1024,1024]{1,0:T(8,128)(2,1)S(1)}) custom-call(bf16[1024,3072]{1,0:T(8,128)(2,1)S(1)} %copy-done, bf16[1024,1024]{1,0:T(8,128)(2,1)S(1)} %copy-done.1), custom_call_target="tpu_custom_call" | custom-call | bytes 28000000 | tf_op jit(solution)/shard_map/prepare/pallas_call | solution.py:381
  16.2 4.1 %collective-permute-done.1.west = bf16[64,1024]{1,0:T(8,128)(2,1)S(1)} collective-permute-done((bf16[64,1024]{1,0:T(8,128)(2,1)S(1)}, bf16[64,1024]{1,0:T(8,128)(2,1)S(1)}, u32[]{:S(2)}, u32[]{:S(2)}) %collective-permute-start.1) | collective-permute-done | bytes 131104 | tf_op jit(solution)/shard_map/ppermute | solution.py:788
  20.3 0.0 collective-permute-done.east
  20.3 0.0 copy-done.3
  20.3 0.0 copy-done.4
  20.3 0.0 copy-start.5
  20.3 5.0 %forward0.1 = (f32[8,32,1024]{2,1,0:T(8,128)S(1)}, bf16[192,3072]{1,0:T(8,128)(2,1)S(1)}, bf16[24,64,256]{2,1,0:T(8,128)(2,1)S(1)}, bf16[192,1024]{1,0:T(8,128)(2,1)S(1)}, f32[192,128]{1,0:T(8,128)S(1)}) custom-call(s32[2,2]{1,0:T(2,128)S(1)} %copy-done.4, f32[8,16,1024]{2,1,0:T(8,128)S(1)} %get-tuple-element.39.initial, f32[1,1024]{1,0:T(1,128)S(1)} %bitcast.9, ...), custom_call_target="tpu_custom_call" | custom-call | bytes 17500000 | tf_op jit(solution)/shard_map/forward0/pallas_call | solution.py:326
  25.3 0.0 copy-done.5
  25.3 0.0 copy-start.2
  25.3 3.3 %forward1.1 = (bf16[144,1024]{1,0:T(8,128)(2,1)S(1)}, f32[128,1024]{1,0:T(8,128)S(1)}, f32[2,128,1024]{2,1,0:T(8,128)S(1)}, bf16[128,3072]{1,0:T(8,128)(2,1)S(1)...) custom-call(s32[2,2]{1,0:T(2,128)S(1)} %copy-done.4, ...), custom_call_target="tpu_custom_call" | custom-call | bytes 14000000 | tf_op jit(solution)/shard_map/forward1/pallas_call | solution.py:349
  28.6 1.5 %collective-permute-start.3 = (bf16[144,1024]{1,0:T(8,128)(2,1)S(1)}, bf16[144,1024]{1,0:T(8,128)(2,1)S(1)}, u32[]{:S(2)}, u32[]{:S(2)}) collective-permute-start(bf16[144,1024]{1,0:T(8,128)(2,1)S(1)} %get-tuple-element.59.sent), channel_id=1, source_target_pairs={{0,128},{128,0},{1,129},{129,1},{2,130},{130,2},{3,131},{131,3},{4... | collective-permute-start | bytes 884744 | tf_op jit(solution)/shard_map/ppermute | solution.py:792
  30.2 0.0 collective-permute-start.2
  30.2 7.5 %collective-permute-done.3.far = bf16[144,1024]{1,0:T(8,128)(2,1)S(1)} collective-permute-done((bf16[144,1024]{1,0:T(8,128)(2,1)S(1)}, bf16[144,1024]{1,0:T(8,128)(2,1)S(1)}, u32[]{:S(2)}, u32[]{:S(2)}) %collective-permute-start.3) | collective-permute-done | bytes 294944 | tf_op jit(solution)/shard_map/ppermute | solution.py:792
  37.6 0.0 collective-permute-start.4
  37.6 0.0 collective-permute-done.2.near
  37.6 1.6 %collective-permute-done.4.far_near = bf16[144,1024]{1,0:T(8,128)(2,1)S(1)} collective-permute-done((bf16[144,1024]{1,0:T(8,128)(2,1)S(1)}, bf16[144,1024]{1,0:T(8,128)(2,1)S(1)}, u32[]{:S(2)}, u32[]{:S(2)}) %collective-permute-start.4) | collective-permute-done | bytes 294944 | tf_op jit(solution)/shard_map/ppermute | solution.py:792
  39.2 0.0 copy-done.2
  39.2 5.6 %backward1.1 = (f32[128,1024]{1,0:T(8,128)S(1)}, bf16[112,1024]{1,0:T(8,128)(2,1)S(1)}, bf16[48,1024]{1,0:T(8,128)(2,1)S(1)}, f32[8,1024]{1,0:T(8,128)S(1)}, f32[8,1024]{1,0:T(8,128)S(1)}) custom-call(s32[2,2]{1,0:T(2,128)S(1)} %copy-done.4, f32[128,1024]{1,0:T(8,128)S(1)} %get-tuple-element.58.final, bf16[144,1024]{1,0:T(8,128)(2,1)S(1)} %collective-permute-done.2.near, ...), custom_call_target="tpu_custom_call" | custom-call | bytes 21000000 | tf_op jit(solution)/shard_map/backward1/pallas_call | solution.py:725
  44.8 4.1 %collective-permute-start.5 = (bf16[112,1024]{1,0:T(8,128)(2,1)S(1)}, bf16[112,1024]{1,0:T(8,128)(2,1)S(1)}, u32[]{:S(2)}, u32[]{:S(2)}) collective-permute-start(bf16[112,1024]{1,0:T(8,128)(2,1)S(1)} %get-tuple-element.67), channel_id=1, source_target_pairs={{0,1},{1,2},{2,3},{3,4},{4,5},{5,6},{6,7},{7,8},{8,9},{9,10},{10,1... | collective-permute-start | bytes 688136 | tf_op jit(solution)/shard_map/ppermute | solution.py:788
  48.8 2.5 %collective-permute-start.6 = (bf16[48,1024]{1,0:T(8,128)(2,1)S(1)}, bf16[48,1024]{1,0:T(8,128)(2,1)S(1)}, u32[]{:S(2)}, u32[]{:S(2)}) collective-permute-start(bf16[48,1024]{1,0:T(8,128)(2,1)S(1)} %get-tuple-element.68), channel_id=1, source_target_pairs={{0,63},{1,0},{2,1},{3,2},{4,3},{5,4},{6,5},{7,6},{8,7},{9,8},{10,9... | collective-permute-start | bytes 294920 | tf_op jit(solution)/shard_map/ppermute | solution.py:788
  51.4 3.7 %backward0_inner.1 = (f32[64,1024]{1,0:T(8,128)S(1)}, f32[8,1024]{1,0:T(8,128)S(1)}) custom-call(s32[2,2]{1,0:T(2,128)S(1)} %copy-done.4, f32[1,1024]{1,0:T(1,128)S(1)} %bitcast.12, bf16[192,3072]{1,0:T(8,128)(2,1)S(1)} %get-tuple-element.50.packed, bf16[24,64,256]{2,1,0:T(8,128)(2,1)S(1)} %get-tuple-element.51.weights, ...), custom_call_target="tpu_custom_call" | custom-call | bytes 14000000 | tf_op jit(solution)/shard_map/backward0_inner/pallas_call | solution.py:757
  55.1 4.0 %collective-permute-done.6.d_east = bf16[48,1024]{1,0:T(8,128)(2,1)S(1)} collective-permute-done((bf16[48,1024]{1,0:T(8,128)(2,1)S(1)}, bf16[48,1024]{1,0:T(8,128)(2,1)S(1)}, u32[]{:S(2)}, u32[]{:S(2)}) %collective-permute-start.6) | collective-permute-done | bytes 98336 | tf_op jit(solution)/shard_map/ppermute | solution.py:788
  59.1 0.0 collective-permute-done.5.d_west
  59.1 5.9 %backward0_outer.1 = (f32[8,16,1024]{2,1,0:T(8,128)}, bf16[32,16,128]{2,1,0:T(8,128)(2,1)S(1)}) custom-call(s32[2,2]{1,0:T(2,128)S(1)} %copy-done.4, f32[1,1024]{1,0:T(1,128)S(1)} %bitcast.13, bf16[192,3072]{1,0:T(8,128)(2,1)S(1)} %get-tuple-element.50.packed, bf16[24,64,256]{2,1,0:T(8,128)(2,1)S(1)} %get-tuple-element.51.weights, ...), custom_call_target="tpu_custom_call" | custom-call | bytes 17500000 | tf_op jit(solution)/shard_map/backward0_outer/pallas_call | solution.py:770
  65.0 12.3 %all_to_all.10 = bf16[32,16,128]{2,1,0:T(8,128)(2,1)S(1)} all-to-all(bf16[32,16,128]{2,1,0:T(8,128)(2,1)S(1)} %get-tuple-element.74), channel_id=1, replica_groups=mesh['pair'=2,'core'=2,'far'=8,'row'=4,'half'=2] {'pair','core','row','h..., dimensions={0} | all-to-all | bytes 262144 | tf_op jit(solution)/shard_map/all_to_all | solution.py:796
  77.4 13.4 %all_to_all.11 = bf16[8,16,128]{2,1,0:T(8,128)(2,1)S(1)} all-to-all(bf16[8,16,128]{2,1,0:T(8,128)(2,1)S(1)} %broadcast_in_dim.18), channel_id=1, replica_groups={{56,48,40,32,24,16,8,0},{57,49,41,33,25,17,9,1},{58,50,42,34,26,18,10,2..., dimensions={0} | all-to-all | bytes 65536 | tf_op jit(solution)/shard_map/all_to_all | solution.py:796
  90.8 0.6 fusion
  (3 shorter events, 0.1 us)
Async XLA Ops:
  2.8 17.5 %collective-permute-start = (bf16[240,1024]{1,0:T(8,128)(2,1)S(1)}, bf16[240,1024]{1,0:T(8,128)(2,1)S(1)}, u32[]{:S(2)}, u32[]{:S(2)}) collective-permute-start(bf16[240,1024]{1,0:T(8,128)(2,1)S(1)} %get-tuple-element.40), channel_id=1, source_target_pairs={{0,63},{1,0},{2,1},{3,2},{4,3},{5,4},{6,5},{7,6},{8,7},{9,8},{10,9... | collective-permute-start | bytes 1474568 | tf_op jit(solution)/shard_map/ppermute | solution.py:788
  7.8 12.4 %collective-permute-start.1 = (bf16[64,1024]{1,0:T(8,128)(2,1)S(1)}, bf16[64,1024]{1,0:T(8,128)(2,1)S(1)}, u32[]{:S(2)}, u32[]{:S(2)}) collective-permute-start(bf16[64,1024]{1,0:T(8,128)(2,1)S(1)} %get-tuple-element.41), channel_id=1, source_target_pairs={{0,1},{1,2},{2,3},{3,4},{4,5},{5,6},{6,7},{7,8},{8,9},{9,10},{10,1... | collective-permute-start | bytes 393224 | tf_op jit(solution)/shard_map/ppermute | solution.py:788
  7.8 2.8 %copy-start = (bf16[1024,3072]{1,0:T(8,128)(2,1)S(1)}, bf16[1024,3072]{1,0:T(8,128)(2,1)}, u32[]{:S(2)}) copy-start(bf16[1024,3072]{1,0:T(8,128)(2,1)} %w_qkv_hbm.1) | copy-start | bytes 18874372
  10.6 1.6 %copy-start.1 = (bf16[1024,1024]{1,0:T(8,128)(2,1)S(1)}, bf16[1024,1024]{1,0:T(8,128)(2,1)}, u32[]{:S(2)}) copy-start(bf16[1024,1024]{1,0:T(8,128)(2,1)} %w_out_hbm.1) | copy-start | bytes 6291460
  12.2 8.1 %copy-start.3 = (f32[1024]{0:T(1024)S(1)}, f32[1024]{0:T(1024)}, u32[]{:S(2)}) copy-start(f32[1024]{0:T(1024)} %param.13) | copy-start | bytes 12292
  12.2 8.1 %copy-start.4 = (s32[2,2]{1,0:T(2,128)S(1)}, s32[2,2]{1,0:T(2,128)}, u32[]{:S(2)}) copy-start(s32[2,2]{1,0:T(2,128)} %shifts_hbm.9) | copy-start | bytes 52
  20.3 5.0 %copy-start.5 = (f32[1024]{0:T(1024)S(1)}, f32[1024]{0:T(1024)}, u32[]{:S(2)}) copy-start(f32[1024]{0:T(1024)} %param.14) | copy-start | bytes 12292
  25.3 13.9 %copy-start.2 = (f32[8,16,1024]{2,1,0:T(8,128)S(1)}, f32[8,16,1024]{2,1,0:T(8,128)}, u32[]{:S(2)}) copy-start(f32[8,16,1024]{2,1,0:T(8,128)} %get-tuple-element.60.target) | copy-start | bytes 1572868
  28.6 9.0 %collective-permute-start.3 = (bf16[144,1024]{1,0:T(8,128)(2,1)S(1)}, bf16[144,1024]{1,0:T(8,128)(2,1)S(1)}, u32[]{:S(2)}, u32[]{:S(2)}) collective-permute-start(bf16[144,1024]{1,0:T(8,128)(2,1)S(1)} %get-tuple-element.59.sent), channel_id=1, source_target_pairs={{0,128},{128,0},{1,129},{129,1},{2,130},{130,2},{3,131},{131,3},{4... | collective-permute-start | bytes 884744 | tf_op jit(solution)/shard_map/ppermute | solution.py:792
  30.2 7.5 %collective-permute-start.2 = (bf16[144,1024]{1,0:T(8,128)(2,1)S(1)}, bf16[144,1024]{1,0:T(8,128)(2,1)S(1)}, u32[]{:S(2)}, u32[]{:S(2)}) collective-permute-start(bf16[144,1024]{1,0:T(8,128)(2,1)S(1)} %get-tuple-element.59.sent), channel_id=1, source_target_pairs={{0,64},{64,0},{1,65},{65,1},{2,66},{66,2},{3,67},{67,3},{4,68},{68... | collective-permute-start | bytes 884744 | tf_op jit(solution)/shard_map/ppermute | solution.py:792
  37.6 1.6 %collective-permute-start.4 = (bf16[144,1024]{1,0:T(8,128)(2,1)S(1)}, bf16[144,1024]{1,0:T(8,128)(2,1)S(1)}, u32[]{:S(2)}, u32[]{:S(2)}) collective-permute-start(bf16[144,1024]{1,0:T(8,128)(2,1)S(1)} %collective-permute-done.3.far), channel_id=1, source_target_pairs={{0,64},{64,0},{1,65},{65,1},{2,66},{66,2},{3,67},{67,3},{4,68},{68... | collective-permute-start | bytes 884744 | tf_op jit(solution)/shard_map/ppermute | solution.py:792
  44.8 14.4 %collective-permute-start.5 = (bf16[112,1024]{1,0:T(8,128)(2,1)S(1)}, bf16[112,1024]{1,0:T(8,128)(2,1)S(1)}, u32[]{:S(2)}, u32[]{:S(2)}) collective-permute-start(bf16[112,1024]{1,0:T(8,128)(2,1)S(1)} %get-tuple-element.67), channel_id=1, source_target_pairs={{0,1},{1,2},{2,3},{3,4},{4,5},{5,6},{6,7},{7,8},{8,9},{9,10},{10,1... | collective-permute-start | bytes 688136 | tf_op jit(solution)/shard_map/ppermute | solution.py:788
  48.8 10.3 %collective-permute-start.6 = (bf16[48,1024]{1,0:T(8,128)(2,1)S(1)}, bf16[48,1024]{1,0:T(8,128)(2,1)S(1)}, u32[]{:S(2)}, u32[]{:S(2)}) collective-permute-start(bf16[48,1024]{1,0:T(8,128)(2,1)S(1)} %get-tuple-element.68), channel_id=1, source_target_pairs={{0,63},{1,0},{2,1},{3,2},{4,3},{5,4},{6,5},{7,6},{8,7},{9,8},{10,9... | collective-permute-start | bytes 294920 | tf_op jit(solution)/shard_map/ppermute | solution.py:788

commit v6 on v5

--- a/solution.py
+++ b/solution.py
@@ -835,10 +835,11 @@
         (gain_part, scale_part),
         *here_t,
     )
-    sums = total_over(sums, near_axes).astype(BF16)
+    near = lax.axis_size(near_axes)
+    sums = total_over(sums, near_axes, [list(range(near))[::-1]]).astype(BF16)
     count = lax.axis_size(TILE[0])
     sums = jnp.broadcast_to(sums[None], (count,) + sums.shape)
-    sums = total_over(sums, TILE[0], [list(range(count))[::-1]]).reshape(2, C)
+    sums = total_over(sums, TILE[0], [[4, 5, 3, 6, 2, 7, 1, 0]]).reshape(2, C)
     members = lax.axis_size(MEMBER)
     factor = (members * LAT * initial.shape[1] * lax.axis_size(TILE)) ** (-0.5)
     return (state_grad[None], sums[0] * factor, sums[1] * factor)

time: 93 us -> 89.6 us (0.963); the launches traced: 91.4 us -> 89.2 us
  blocking collectives: 25.7 us -> 23.5 us
    all_to_all x2, blocking collectives: 25.7 us -> 23.5 us  [total_over(): parts = lax.all_to_all(copies, axes, 0, 0, axis_index_groups=groups)]
  transfers between devices with their start and end apart: 7 -> 7, of which waited for: 4 -> 4; matrix products, arithmetic and copies ran while one was open for 0% -> 0% of each run, Pallas kernels for 8% -> 9%
where the time goes in v6:
time: 89.6 us; the launch traced here: 89.2 us
  Pallas kernels  29.6 us (33%)
  blocking collectives  23.5 us (26%)
  waiting for transfers between devices  17.1 us (19%)
  starting transfers between devices  13.2 us (15%)
  local copies, waits for them, and re-layouts  4.4 us (5%)
    all_to_all x2, blocking collectives, total_over(): parts = lax.all_to_all(copies, axes, 0, 0, axis_index_groups=groups)  23.5 us
    ppermute x4, starting transfers between devices, along(): lax.ppermute(value, TILE, [(at, (at + steps) % count) for at in range(cou...  11.6 us
    ppermute x3, waiting for transfers between devices, other(): return lax.ppermute(value, axis, [(0, 1), (1, 0)])  9.04 us
    ppermute x4, waiting for transfers between devices, along(): lax.ppermute(value, TILE, [(at, (at + steps) % count) for at in range(cou...  8.08 us
    pallas_call x1, Pallas kernels, backward0_outer(): pl.pallas_call(backward0_outer_kernel, out_shape=shapes([((LAT, 16, C), F...  5.9 us
    pallas_call x1, Pallas kernels, backward1(): pl.pallas_call(backward1_kernel, out_shape=shapes([((ROWS, C), F32), ((LA...  5.55 us
    pallas_call x1, Pallas kernels, forward0(): pl.pallas_call(forward0_kernel, out_shape=shapes([((LAT, 32, C), F32)] +...  4.98 us
    unnamed x12, local copies, waits for them, and re-layouts  4.39 us
  transfers between devices with their start and end apart: 7, of which 4 were waited for; matrix products, arithmetic and copies ran while one was open for 0% of the time, Pallas kernels for 9%

profile of v6, /device:TPU:32, one launch (start us, length us, event | category | flops | bytes accessed | tf_op | source)
XLA Modules:
  0.0 89.2 jit_solution(6231286593376190889)
XLA Ops:
  0.6 2.2 %borders.1 = (bf16[240,1024]{1,0:T(8,128)(2,1)S(1)}, bf16[64,1024]{1,0:T(8,128)(2,1)S(1)}, f32[8,16,1024]{2,1,0:T(8,128)S(1)}, bf16[2,8,16,1024]{3,2,1,0:T(8,128)(2,1)S(1)}, f32[8,16,1024]{2,1,0:T(8,128)}) custom-call(f32[8,16,1024]{2,1,0:T(8,128)} %bitcast.15, bf16[2,8,16,1024]{3,2,1,0:T(8,128)(2,1)} %bitcast.16, f32[8,16,1024]{2,1,0:T(8,128)} %target_hbm.1), custom_call_target="tpu_custom_call" | custom-call | bytes 7000000 | tf_op jit(solution)/shard_map/borders/pallas_call | solution.py:437
  2.8 5.0 %collective-permute-start = (bf16[240,1024]{1,0:T(8,128)(2,1)S(1)}, bf16[240,1024]{1,0:T(8,128)(2,1)S(1)}, u32[]{:S(2)}, u32[]{:S(2)}) collective-permute-start(bf16[240,1024]{1,0:T(8,128)(2,1)S(1)} %get-tuple-element.40), channel_id=1, source_target_pairs={{0,63},{1,0},{2,1},{3,2},{4,3},{5,4},{6,5},{7,6},{8,7},{9,8},{10,9... | collective-permute-start | bytes 1474568 | tf_op jit(solution)/shard_map/ppermute | solution.py:788
  7.8 0.0 collective-permute-start.1
  7.8 0.0 copy-start
  7.8 2.8 %copy-done = bf16[1024,3072]{1,0:T(8,128)(2,1)S(1)} copy-done((bf16[1024,3072]{1,0:T(8,128)(2,1)S(1)}, bf16[1024,3072]{1,0:T(8,128)(2,1)}, u32[]{:S(2)}) %copy-start) | copy-done | bytes 6291480
  10.6 0.0 copy-start.1
  10.6 1.6 %copy-done.1 = bf16[1024,1024]{1,0:T(8,128)(2,1)S(1)} copy-done((bf16[1024,1024]{1,0:T(8,128)(2,1)S(1)}, bf16[1024,1024]{1,0:T(8,128)(2,1)}, u32[]{:S(2)}) %copy-start.1) | copy-done | bytes 2097176
  12.2 0.0 copy-start.3
  12.2 0.0 copy-start.4
  12.2 4.0 %prepare.1 = (bf16[1024,3072]{1,0:T(8,128)(2,1)S(1)}, bf16[1024,1024]{1,0:T(8,128)(2,1)S(1)}, bf16[3072,1024]{1,0:T(8,128)(2,1)S(1)}, bf16[1024,1024]{1,0:T(8,128)(2,1)S(1)}) custom-call(bf16[1024,3072]{1,0:T(8,128)(2,1)S(1)} %copy-done, bf16[1024,1024]{1,0:T(8,128)(2,1)S(1)} %copy-done.1), custom_call_target="tpu_custom_call" | custom-call | bytes 28000000 | tf_op jit(solution)/shard_map/prepare/pallas_call | solution.py:381
  16.2 4.1 %collective-permute-done.1.west = bf16[64,1024]{1,0:T(8,128)(2,1)S(1)} collective-permute-done((bf16[64,1024]{1,0:T(8,128)(2,1)S(1)}, bf16[64,1024]{1,0:T(8,128)(2,1)S(1)}, u32[]{:S(2)}, u32[]{:S(2)}) %collective-permute-start.1) | collective-permute-done | bytes 131104 | tf_op jit(solution)/shard_map/ppermute | solution.py:788
  20.3 0.0 collective-permute-done.east
  20.3 0.0 copy-done.3
  20.3 0.0 copy-done.4
  20.3 0.0 copy-start.5
  20.3 5.0 %forward0.1 = (f32[8,32,1024]{2,1,0:T(8,128)S(1)}, bf16[192,3072]{1,0:T(8,128)(2,1)S(1)}, bf16[24,64,256]{2,1,0:T(8,128)(2,1)S(1)}, bf16[192,1024]{1,0:T(8,128)(2,1)S(1)}, f32[192,128]{1,0:T(8,128)S(1)}) custom-call(s32[2,2]{1,0:T(2,128)S(1)} %copy-done.4, f32[8,16,1024]{2,1,0:T(8,128)S(1)} %get-tuple-element.39.initial, f32[1,1024]{1,0:T(1,128)S(1)} %bitcast.9, ...), custom_call_target="tpu_custom_call" | custom-call | bytes 17500000 | tf_op jit(solution)/shard_map/forward0/pallas_call | solution.py:326
  25.3 0.0 copy-done.5
  25.3 0.0 copy-start.2
  25.3 3.3 %forward1.1 = (bf16[144,1024]{1,0:T(8,128)(2,1)S(1)}, f32[128,1024]{1,0:T(8,128)S(1)}, f32[2,128,1024]{2,1,0:T(8,128)S(1)}, bf16[128,3072]{1,0:T(8,128)(2,1)S(1)...) custom-call(s32[2,2]{1,0:T(2,128)S(1)} %copy-done.4, ...), custom_call_target="tpu_custom_call" | custom-call | bytes 14000000 | tf_op jit(solution)/shard_map/forward1/pallas_call | solution.py:349
  28.6 1.5 %collective-permute-start.3 = (bf16[144,1024]{1,0:T(8,128)(2,1)S(1)}, bf16[144,1024]{1,0:T(8,128)(2,1)S(1)}, u32[]{:S(2)}, u32[]{:S(2)}) collective-permute-start(bf16[144,1024]{1,0:T(8,128)(2,1)S(1)} %get-tuple-element.59.sent), channel_id=1, source_target_pairs={{0,128},{128,0},{1,129},{129,1},{2,130},{130,2},{3,131},{131,3},{4... | collective-permute-start | bytes 884744 | tf_op jit(solution)/shard_map/ppermute | solution.py:792
  30.2 0.0 collective-permute-start.2
  30.2 7.5 %collective-permute-done.3.far = bf16[144,1024]{1,0:T(8,128)(2,1)S(1)} collective-permute-done((bf16[144,1024]{1,0:T(8,128)(2,1)S(1)}, bf16[144,1024]{1,0:T(8,128)(2,1)S(1)}, u32[]{:S(2)}, u32[]{:S(2)}) %collective-permute-start.3) | collective-permute-done | bytes 294944 | tf_op jit(solution)/shard_map/ppermute | solution.py:792
  37.6 0.0 collective-permute-start.4
  37.6 0.0 collective-permute-done.2.near
  37.6 1.6 %collective-permute-done.4.far_near = bf16[144,1024]{1,0:T(8,128)(2,1)S(1)} collective-permute-done((bf16[144,1024]{1,0:T(8,128)(2,1)S(1)}, bf16[144,1024]{1,0:T(8,128)(2,1)S(1)}, u32[]{:S(2)}, u32[]{:S(2)}) %collective-permute-start.4) | collective-permute-done | bytes 294944 | tf_op jit(solution)/shard_map/ppermute | solution.py:792
  39.2 0.0 copy-done.2
  39.2 5.6 %backward1.1 = (f32[128,1024]{1,0:T(8,128)S(1)}, bf16[112,1024]{1,0:T(8,128)(2,1)S(1)}, bf16[48,1024]{1,0:T(8,128)(2,1)S(1)}, f32[8,1024]{1,0:T(8,128)S(1)}, f32[8,1024]{1,0:T(8,128)S(1)}) custom-call(s32[2,2]{1,0:T(2,128)S(1)} %copy-done.4, f32[128,1024]{1,0:T(8,128)S(1)} %get-tuple-element.58.final, bf16[144,1024]{1,0:T(8,128)(2,1)S(1)} %collective-permute-done.2.near, ...), custom_call_target="tpu_custom_call" | custom-call | bytes 21000000 | tf_op jit(solution)/shard_map/backward1/pallas_call | solution.py:725
  44.8 4.1 %collective-permute-start.5 = (bf16[112,1024]{1,0:T(8,128)(2,1)S(1)}, bf16[112,1024]{1,0:T(8,128)(2,1)S(1)}, u32[]{:S(2)}, u32[]{:S(2)}) collective-permute-start(bf16[112,1024]{1,0:T(8,128)(2,1)S(1)} %get-tuple-element.67), channel_id=1, source_target_pairs={{0,1},{1,2},{2,3},{3,4},{4,5},{5,6},{6,7},{7,8},{8,9},{9,10},{10,1... | collective-permute-start | bytes 688136 | tf_op jit(solution)/shard_map/ppermute | solution.py:788
  48.8 2.5 %collective-permute-start.6 = (bf16[48,1024]{1,0:T(8,128)(2,1)S(1)}, bf16[48,1024]{1,0:T(8,128)(2,1)S(1)}, u32[]{:S(2)}, u32[]{:S(2)}) collective-permute-start(bf16[48,1024]{1,0:T(8,128)(2,1)S(1)} %get-tuple-element.68), channel_id=1, source_target_pairs={{0,63},{1,0},{2,1},{3,2},{4,3},{5,4},{6,5},{7,6},{8,7},{9,8},{10,9... | collective-permute-start | bytes 294920 | tf_op jit(solution)/shard_map/ppermute | solution.py:788
  51.4 3.7 %backward0_inner.1 = (f32[64,1024]{1,0:T(8,128)S(1)}, f32[8,1024]{1,0:T(8,128)S(1)}) custom-call(s32[2,2]{1,0:T(2,128)S(1)} %copy-done.4, f32[1,1024]{1,0:T(1,128)S(1)} %bitcast.12, bf16[192,3072]{1,0:T(8,128)(2,1)S(1)} %get-tuple-element.50.packed, bf16[24,64,256]{2,1,0:T(8,128)(2,1)S(1)} %get-tuple-element.51.weights, ...), custom_call_target="tpu_custom_call" | custom-call | bytes 14000000 | tf_op jit(solution)/shard_map/backward0_inner/pallas_call | solution.py:757
  55.1 4.0 %collective-permute-done.6.d_east = bf16[48,1024]{1,0:T(8,128)(2,1)S(1)} collective-permute-done((bf16[48,1024]{1,0:T(8,128)(2,1)S(1)}, bf16[48,1024]{1,0:T(8,128)(2,1)S(1)}, u32[]{:S(2)}, u32[]{:S(2)}) %collective-permute-start.6) | collective-permute-done | bytes 98336 | tf_op jit(solution)/shard_map/ppermute | solution.py:788
  59.1 0.0 collective-permute-done.5.d_west
  59.1 5.9 %backward0_outer.1 = (f32[8,16,1024]{2,1,0:T(8,128)}, bf16[32,16,128]{2,1,0:T(8,128)(2,1)S(1)}) custom-call(s32[2,2]{1,0:T(2,128)S(1)} %copy-done.4, f32[1,1024]{1,0:T(1,128)S(1)} %bitcast.13, bf16[192,3072]{1,0:T(8,128)(2,1)S(1)} %get-tuple-element.50.packed, bf16[24,64,256]{2,1,0:T(8,128)(2,1)S(1)} %get-tuple-element.51.weights, ...), custom_call_target="tpu_custom_call" | custom-call | bytes 17500000 | tf_op jit(solution)/shard_map/backward0_outer/pallas_call | solution.py:770
  65.0 11.1 %all_to_all.10 = bf16[32,16,128]{2,1,0:T(8,128)(2,1)S(1)} all-to-all(bf16[32,16,128]{2,1,0:T(8,128)(2,1)S(1)} %get-tuple-element.74), channel_id=1, replica_groups={{199,198,197,196,195,194,193,192,135,134,133,132,131,130,129,128,71,70,..., dimensions={0} | all-to-all | bytes 262144 | tf_op jit(solution)/shard_map/all_to_all | solution.py:796
  76.2 12.4 %all_to_all.11 = bf16[8,16,128]{2,1,0:T(8,128)(2,1)S(1)} all-to-all(bf16[8,16,128]{2,1,0:T(8,128)(2,1)S(1)} %broadcast_in_dim.18), channel_id=1, replica_groups={{32,40,24,48,16,56,8,0},{33,41,25,49,17,57,9,1},{34,42,26,50,18,58,10,2..., dimensions={0} | all-to-all | bytes 65536 | tf_op jit(solution)/shard_map/all_to_all | solution.py:796
  88.6 0.6 fusion
  (3 shorter events, 0.1 us)
Async XLA Ops:
  2.8 17.5 %collective-permute-start = (bf16[240,1024]{1,0:T(8,128)(2,1)S(1)}, bf16[240,1024]{1,0:T(8,128)(2,1)S(1)}, u32[]{:S(2)}, u32[]{:S(2)}) collective-permute-start(bf16[240,1024]{1,0:T(8,128)(2,1)S(1)} %get-tuple-element.40), channel_id=1, source_target_pairs={{0,63},{1,0},{2,1},{3,2},{4,3},{5,4},{6,5},{7,6},{8,7},{9,8},{10,9... | collective-permute-start | bytes 1474568 | tf_op jit(solution)/shard_map/ppermute | solution.py:788
  7.8 12.4 %collective-permute-start.1 = (bf16[64,1024]{1,0:T(8,128)(2,1)S(1)}, bf16[64,1024]{1,0:T(8,128)(2,1)S(1)}, u32[]{:S(2)}, u32[]{:S(2)}) collective-permute-start(bf16[64,1024]{1,0:T(8,128)(2,1)S(1)} %get-tuple-element.41), channel_id=1, source_target_pairs={{0,1},{1,2},{2,3},{3,4},{4,5},{5,6},{6,7},{7,8},{8,9},{9,10},{10,1... | collective-permute-start | bytes 393224 | tf_op jit(solution)/shard_map/ppermute | solution.py:788
  7.8 2.8 %copy-start = (bf16[1024,3072]{1,0:T(8,128)(2,1)S(1)}, bf16[1024,3072]{1,0:T(8,128)(2,1)}, u32[]{:S(2)}) copy-start(bf16[1024,3072]{1,0:T(8,128)(2,1)} %w_qkv_hbm.1) | copy-start | bytes 18874372
  10.6 1.6 %copy-start.1 = (bf16[1024,1024]{1,0:T(8,128)(2,1)S(1)}, bf16[1024,1024]{1,0:T(8,128)(2,1)}, u32[]{:S(2)}) copy-start(bf16[1024,1024]{1,0:T(8,128)(2,1)} %w_out_hbm.1) | copy-start | bytes 6291460
  12.2 8.1 %copy-start.3 = (f32[1024]{0:T(1024)S(1)}, f32[1024]{0:T(1024)}, u32[]{:S(2)}) copy-start(f32[1024]{0:T(1024)} %param.13) | copy-start | bytes 12292
  12.2 8.1 %copy-start.4 = (s32[2,2]{1,0:T(2,128)S(1)}, s32[2,2]{1,0:T(2,128)}, u32[]{:S(2)}) copy-start(s32[2,2]{1,0:T(2,128)} %shifts_hbm.9) | copy-start | bytes 52
  20.3 5.0 %copy-start.5 = (f32[1024]{0:T(1024)S(1)}, f32[1024]{0:T(1024)}, u32[]{:S(2)}) copy-start(f32[1024]{0:T(1024)} %param.14) | copy-start | bytes 12292
  25.3 13.9 %copy-start.2 = (f32[8,16,1024]{2,1,0:T(8,128)S(1)}, f32[8,16,1024]{2,1,0:T(8,128)}, u32[]{:S(2)}) copy-start(f32[8,16,1024]{2,1,0:T(8,128)} %get-tuple-element.60.target) | copy-start | bytes 1572868
  28.6 9.0 %collective-permute-start.3 = (bf16[144,1024]{1,0:T(8,128)(2,1)S(1)}, bf16[144,1024]{1,0:T(8,128)(2,1)S(1)}, u32[]{:S(2)}, u32[]{:S(2)}) collective-permute-start(bf16[144,1024]{1,0:T(8,128)(2,1)S(1)} %get-tuple-element.59.sent), channel_id=1, source_target_pairs={{0,128},{128,0},{1,129},{129,1},{2,130},{130,2},{3,131},{131,3},{4... | collective-permute-start | bytes 884744 | tf_op jit(solution)/shard_map/ppermute | solution.py:792
  30.2 7.5 %collective-permute-start.2 = (bf16[144,1024]{1,0:T(8,128)(2,1)S(1)}, bf16[144,1024]{1,0:T(8,128)(2,1)S(1)}, u32[]{:S(2)}, u32[]{:S(2)}) collective-permute-start(bf16[144,1024]{1,0:T(8,128)(2,1)S(1)} %get-tuple-element.59.sent), channel_id=1, source_target_pairs={{0,64},{64,0},{1,65},{65,1},{2,66},{66,2},{3,67},{67,3},{4,68},{68... | collective-permute-start | bytes 884744 | tf_op jit(solution)/shard_map/ppermute | solution.py:792
  37.6 1.6 %collective-permute-start.4 = (bf16[144,1024]{1,0:T(8,128)(2,1)S(1)}, bf16[144,1024]{1,0:T(8,128)(2,1)S(1)}, u32[]{:S(2)}, u32[]{:S(2)}) collective-permute-start(bf16[144,1024]{1,0:T(8,128)(2,1)S(1)} %collective-permute-done.3.far), channel_id=1, source_target_pairs={{0,64},{64,0},{1,65},{65,1},{2,66},{66,2},{3,67},{67,3},{4,68},{68... | collective-permute-start | bytes 884744 | tf_op jit(solution)/shard_map/ppermute | solution.py:792
  44.8 14.4 %collective-permute-start.5 = (bf16[112,1024]{1,0:T(8,128)(2,1)S(1)}, bf16[112,1024]{1,0:T(8,128)(2,1)S(1)}, u32[]{:S(2)}, u32[]{:S(2)}) collective-permute-start(bf16[112,1024]{1,0:T(8,128)(2,1)S(1)} %get-tuple-element.67), channel_id=1, source_target_pairs={{0,1},{1,2},{2,3},{3,4},{4,5},{5,6},{6,7},{7,8},{8,9},{9,10},{10,1... | collective-permute-start | bytes 688136 | tf_op jit(solution)/shard_map/ppermute | solution.py:788
  48.8 10.3 %collective-permute-start.6 = (bf16[48,1024]{1,0:T(8,128)(2,1)S(1)}, bf16[48,1024]{1,0:T(8,128)(2,1)S(1)}, u32[]{:S(2)}, u32[]{:S(2)}) collective-permute-start(bf16[48,1024]{1,0:T(8,128)(2,1)S(1)} %get-tuple-element.68), channel_id=1, source_target_pairs={{0,63},{1,0},{2,1},{3,2},{4,3},{5,4},{6,5},{7,6},{8,7},{9,8},{10,9... | collective-permute-start | bytes 294920 | tf_op jit(solution)/shard_map/ppermute | solution.py:788
